TPU v7x, 256 devices: a whole 4x4x8 slice. The times are simulated.
256 devices in a mesh: seg: 8 (over x, core), dom: 32 (over z, y).
Axes of the slice: x: 4, y: 4, z: 8, core: 2. Of those that a mesh axis runs over, the one named last changes fastest.
Arguments:
- element_state: float32 [180, 393216], P(None, ('seg', 'dom')), may hold values from -6 to 6
- face_source: int32 [4, 393216], P(None, ('seg', 'dom')), may hold values from 0 to 10239, as said below
- send_faces: int32 [32, 32768], P(None, ('seg', 'dom')), may hold values from 0 to 6143
- plus_faces: int32 [32768], P(('seg', 'dom')), may hold values from 0 to 6143, as said below
- minus_faces: int32 [32768], P(('seg', 'dom')), may hold values from 0 to 6143
- fault_count: int32 [256], P(('seg', 'dom')), may hold values from 1 to 128, as said below
- normal_stress: float32 [16, 32768], P(None, ('seg', 'dom')), may hold values from 1 to 10
- state_variable: float32 [16, 32768], P(None, ('seg', 'dom')), may hold values from 0.5 to 3
- geometry: float32 [3, 393216], P(None, ('seg', 'dom')), may hold values from 0.3 to 3
- face_area: float32 [4, 393216], P(None, ('seg', 'dom')), may hold values from 0.5 to 4
- restriction: bfloat16 [120, 180], replicated, may hold values from -0.4375 to 0.4375
- volume_ops: bfloat16 [540, 180], replicated, may hold values from -0.4375 to 0.4375
- lift_operator: bfloat16 [180, 120], replicated, may hold values from -0.5 to 0.5
- to_points: float32 [16, 10], replicated, may hold values from -2 to 2
- to_nodes: float32 [10, 16], replicated, may hold values from -1.5 to 1.5
Outputs:
- element_state_next: float32 [180, 393216], P(None, ('seg', 'dom'))
- fault_slip: float32 [16, 32768], P(None, ('seg', 'dom'))
Inputs may be any that keep to these rules, and one draw needn't show every extreme that they name: `face_source`: on each partition every received slot is named exactly once; fault faces are never named. On each partition plus_faces and minus_faces are all different faces. `fault_count`: some owner has all 128 slots live.
All inputs are finite; a program needn't handle non-finite values.
Results may differ from a plain program's by a relative error of at most 0.0042.
Values may be sent and summed in bfloat16 or wider, within the bound.
No kernel may reach another device: no remote copies, remote signals or barrier semaphores. Data moves between devices by JAX's collectives and lax.ppermute only.
A program may use at most 64 MiB of HBM per device.

v0:
```python
import jax
import jax.numpy as jnp
from jax import lax
from jax.sharding import PartitionSpec as P

STEPS = 2
NEWTON = 4


IMPEDANCE = 1.0
FRICTION_A = 0.2
REGULARIZE = 0.25
TIME_STEP = 0.25


def shifted(value, axis, steps):
    count = lax.axis_size(axis)
    pairs = [(source, (source + steps) % count) for source in range(count)]
    return lax.ppermute(value, axis, pairs)


def inverse_sinh(value):
    return jnp.log(value + jnp.sqrt(value * value + 1.0))


def friction(plus_side, minus_side, normal_stress, state_variable, to_points, to_nodes):
    difference = plus_side.astype(jnp.float32) - minus_side.astype(jnp.float32)
    difference = difference.reshape(3, to_points.shape[1], -1)
    at_points = jnp.einsum("qn,cnf->cqf", to_points, difference, precision=lax.Precision.HIGHEST)
    magnitude = jnp.sqrt(at_points[1] * at_points[1] + at_points[2] * at_points[2] + REGULARIZE)
    rate_scale = 0.5 * jnp.exp(state_variable)
    slip_rate = jnp.zeros_like(magnitude)
    for sweep in range(NEWTON):
        scaled_rate = slip_rate * rate_scale
        residual_value = IMPEDANCE * (
            magnitude - slip_rate
        ) - normal_stress * FRICTION_A * inverse_sinh(scaled_rate)
        derivative = IMPEDANCE + normal_stress * FRICTION_A * rate_scale / jnp.sqrt(
            1.0 + scaled_rate * scaled_rate
        )
        slip_rate = slip_rate + residual_value / derivative
    slip_share = slip_rate / magnitude
    point_jump = jnp.stack([at_points[0], at_points[1] * slip_share, at_points[2] * slip_share])
    nodal_jump = jnp.einsum("nq,cqf->cnf", to_nodes, point_jump, precision=lax.Precision.HIGHEST)
    return (nodal_jump.reshape(-1, nodal_jump.shape[-1]), slip_rate)


def advance_local(element_state, face_jump, geometry, face_area, volume_ops, lift_operator):
    elements = element_state.shape[1]
    packed = element_state.astype(jnp.bfloat16)
    scaled_jump = (
        (face_jump.reshape(-1, 4, elements) * face_area[None])
        .reshape(-1, elements)
        .astype(jnp.bfloat16)
    )
    lifted = jnp.dot(lift_operator, scaled_jump, preferred_element_type=jnp.float32)
    volume = jnp.dot(volume_ops, packed, preferred_element_type=jnp.float32).reshape(
        3, -1, elements
    )
    volume = jnp.sum(volume * geometry[:, None, :], axis=0)
    return element_state + TIME_STEP * (volume - lifted)


def shards(
    element_state,
    face_source,
    send_faces,
    plus_faces,
    minus_faces,
    fault_count,
    normal_stress,
    state_variable,
    geometry,
    face_area,
    restriction,
    volume_ops,
    lift_operator,
    to_points,
    to_nodes,
):
    peers = lax.axis_size("dom")
    elements = element_state.shape[1]
    fault_slots = plus_faces.shape[0]
    rows = restriction.shape[0] // 4
    is_live = jnp.arange(fault_slots, dtype=jnp.int32) < fault_count[0]
    slip_out = jnp.zeros_like(normal_stress)
    for step in range(STEPS):
        packed = element_state.astype(jnp.bfloat16)
        traces = jnp.dot(restriction, packed, preferred_element_type=jnp.float32).astype(
            jnp.bfloat16
        )
        traces = traces.reshape(rows, 4 * elements)
        outgoing = traces[:, send_faces.reshape(-1)].reshape(rows, peers, -1)
        gathered = lax.all_gather(outgoing, "dom", axis=1, tiled=True)
        gathered = gathered.reshape(rows, peers, peers, -1)
        received = lax.dynamic_index_in_dim(gathered, lax.axis_index("dom"), 2, keepdims=False)
        trace_pool = jnp.concatenate([traces, received.reshape(rows, -1)], axis=1)
        exterior = trace_pool[:, face_source.reshape(-1)]
        face_jump = traces.astype(jnp.float32) - exterior.astype(jnp.float32)
        plus_traces = traces[:, plus_faces]
        minus_traces = traces[:, minus_faces]
        partner = shifted(minus_traces, "seg", 1)
        nodal_jump, slip_rate = friction(
            plus_traces, partner, normal_stress, state_variable, to_points, to_nodes
        )
        returned, partner_count = shifted((nodal_jump, fault_count), "seg", -1)
        live_back = jnp.arange(fault_slots, dtype=jnp.int32) < partner_count[0]
        face_jump = face_jump.at[:, plus_faces].set(
            jnp.where(is_live[None, :], nodal_jump, face_jump[:, plus_faces])
        )
        face_jump = face_jump.at[:, minus_faces].set(
            jnp.where(live_back[None, :], -returned, face_jump[:, minus_faces])
        )
        element_state = advance_local(
            element_state, face_jump, geometry, face_area, volume_ops, lift_operator
        )
        slip_out = jnp.where(is_live[None, :], slip_rate, 0.0)
    return (element_state, slip_out)


def solution(mesh):
    placed = (
        P(None, ("seg", "dom")),
        P(None, ("seg", "dom")),
        P(None, ("seg", "dom")),
        P(("seg", "dom")),
        P(("seg", "dom")),
        P(("seg", "dom")),
        P(None, ("seg", "dom")),
        P(None, ("seg", "dom")),
        P(None, ("seg", "dom")),
        P(None, ("seg", "dom")),
        P(),
        P(),
        P(),
        P(),
        P(),
    )
    return jax.shard_map(
        shards,
        mesh=mesh,
        in_specs=placed,
        out_specs=(P(None, ("seg", "dom")), P(None, ("seg", "dom"))),
        check_vma=False,
    )
```

profile of v0, /device:TPU:6, one launch (start us, length us, event | category | flops | bytes accessed | tf_op | source)
XLA Modules:
  0.0 342.3 jit_solution(12429449970131103704)
XLA Ops:
  7.2 1.6 convolution_convert_fusion.1
  9.1 0.9 copy.97
  10.1 15.0 %gather_fusion = bf16[4096,30]{1,0:T(8,128)(2,1)} fusion(bf16[30,6144]{0,1:T(8,128)(2,1)S(1)} %copy.97, s32[4096]{0:T(1024)S(1)} %broadcast_clamp_fusion.1), kind=kCustom, calls=%fused_computation | custom fusion | bytes 507904 | tf_op jit(solution)/shard_map/gather | solution.py:93
  25.1 2.5 copy.99
  27.7 0.5 copy-done.24
  28.2 0.7 gather_fusion.3
  29.0 1.7 collective-permute-start.1
  31.4 0.7 gather_fusion.2
  32.3 1.0 mul.184
  33.3 2.3 mul.185
  35.5 2.4 fusion.10
  38.0 3.7 %reshape.134 = f32[3,180,1536]{2,1,0:T(8,128)} reshape(f32[540,1536]{1,0:T(8,128)} %fusion.10) | data formatting | bytes 6635520 | tf_op jit(solution)/shard_map/reshape | solution.py:57
  41.7 0.6 iota_compare_fusion.1
  42.3 3.6 %multiply_reduce_fusion.1 = f32[180,1536]{1,0:T(8,128)} fusion(f32[3,180,1536]{2,1,0:T(8,128)} %reshape.134, f32[3,1536]{1,0:T(4,128)S(1)} %copy-done.7), kind=kLoop, calls=%fused_computation.17 | loop fusion | flops 1382400 | bytes 4442112 | tf_op jit(solution)/shard_map/reduce_sum | solution.py:60
  45.9 1.2 iota_compare_fusion
  47.1 0.7 bitcast_subtract_fusion.3
  48.5 83.1 %all-gather.3.cloned.1.call-done = bf16[30,1024,128]{2,1,0:T(8,128)(2,1)} async-done(((bf16[30,32,128]{2,1,0:T(8,128)(2,1)}), bf16[30,1024,128]{2,1,0:T(8,128)(2,1)}) %all-gather.3.cloned.1.call-update) | async-done | bytes 7864336 | tf_op jit(solution)/shard_map/all_gather | solution.py:94
  131.5 3.0 dynamic-slice_reduce_fusion.1
  134.7 0.9 pad_maximum_fusion
  135.6 3.4 copy.101
  139.0 22.1 %gather_fusion.1 = bf16[6144,30]{1,0:T(8,128)(2,1)} fusion(bf16[30,10240]{0,1:T(8,128)(2,1)S(1)} %copy.101, s32[6144]{0:T(1024)S(1)} %broadcast_clamp_fusion), kind=kCustom, calls=%fused_computation.1 | custom fusion | bytes 761856 | tf_op jit(solution)/shard_map/gather | solution.py:98
  161.0 2.2 bitcast_subtract_fusion.1
  163.2 2.4 scatter_custom_fusion
  165.7 2.8 scatter_custom_fusion.1
  168.5 1.9 copy.108
  170.4 1.4 reshape.143
  171.8 2.2 fusion.5
  174.6 0.9 copy.109
  175.5 14.9 %gather_fusion.4 = bf16[4096,30]{1,0:T(8,128)(2,1)} fusion(bf16[30,6144]{0,1:T(8,128)(2,1)S(1)} %copy.109, s32[4096]{0:T(1024)S(1)} %broadcast_clamp_fusion.1), kind=kCustom, calls=%fused_computation.6 | custom fusion | bytes 507904 | tf_op jit(solution)/shard_map/gather | solution.py:93
  190.4 2.4 copy.111
  192.8 0.7 gather_fusion.7
  193.7 2.5 convolution_bitcast_fusion
  196.1 3.7 %reshape.144 = f32[3,180,1536]{2,1,0:T(8,128)} reshape(f32[540,1536]{1,0:T(8,128)} %convolution_bitcast_fusion) | data formatting | bytes 6635520 | tf_op jit(solution)/shard_map/reshape | solution.py:57
  199.9 3.5 %multiply_reduce_fusion = f32[180,1536]{1,0:T(8,128)} fusion(f32[3,180,1536]{2,1,0:T(8,128)} %reshape.144, f32[3,1536]{1,0:T(4,128)S(1)} %copy-done.8), kind=kLoop, calls=%fused_computation.16 | loop fusion | flops 1382400 | bytes 4442112 | tf_op jit(solution)/shard_map/reduce_sum | solution.py:60
  203.4 0.7 gather_fusion.6
  204.4 0.7 broadcast_select_fusion
  205.5 1.7 collective-permute-start.4
  207.2 85.0 %all-gather.5.cloned.1.call-done = bf16[30,1024,128]{2,1,0:T(8,128)(2,1)} async-done(((bf16[30,32,128]{2,1,0:T(8,128)(2,1)}), bf16[30,1024,128]{2,1,0:T(8,128)(2,1)}) %all-gather.5.cloned.1.call-update) | async-done | bytes 7864336 | tf_op jit(solution)/shard_map/all_gather | solution.py:94
  292.2 3.0 dynamic-slice_reduce_fusion
  295.3 0.9 pad_maximum_fusion.1
  296.3 3.4 copy.113
  299.7 22.1 %gather_fusion.5 = bf16[6144,30]{1,0:T(8,128)(2,1)} fusion(bf16[30,10240]{0,1:T(8,128)(2,1)S(1)} %copy.113, s32[6144]{0:T(1024)S(1)} %broadcast_clamp_fusion), kind=kCustom, calls=%fused_computation.7 | custom fusion | bytes 761856 | tf_op jit(solution)/shard_map/gather | solution.py:98
  321.7 2.2 bitcast_subtract_fusion
  323.9 2.4 scatter_custom_fusion.2
  326.4 2.6 scatter_custom_fusion.3
  329.0 1.9 copy.120
  331.0 1.4 reshape.151
  332.3 3.2 fusion.2
  (102 shorter events, 2.8 us)
Async XLA Ops:
  7.2 28.3 %copy-start = (bf16[540,180]{0,1:T(8,128)(2,1)S(1)}, bf16[540,180]{0,1:T(8,128)(2,1)}, u32[]{:S(2)}) copy-start(bf16[540,180]{0,1:T(8,128)(2,1)} %param.26) | copy-start | bytes 583204
  7.2 2.8 copy-start.18
  7.2 124.3 %all-gather.3.cloned.1.call-start = ((), (), s32[]{:S(2)}) async-start(), calls=%async_computation | async-start | bytes 8110080 | tf_op jit(solution)/shard_map/all_gather | solution.py:94
  9.1 18.6 %copy-start.26 = (s32[128]{0:T(128)S(1)}, s32[128]{0:T(128)}, u32[]{:S(2)}) copy-start(s32[128]{0:T(128)} %param.19) | copy-start | bytes 1540
  9.1 18.6 %copy-start.27 = (s32[128]{0:T(128)S(1)}, s32[128]{0:T(128)}, u32[]{:S(2)}) copy-start(s32[128]{0:T(128)} %param.18) | copy-start | bytes 1540
  9.1 23.1 %copy-start.17 = (s32[4,1536]{1,0:T(4,128)S(1)}, s32[4,1536]{1,0:T(4,128)}, u32[]{:S(2)}) copy-start(s32[4,1536]{1,0:T(4,128)} %param.16) | copy-start | bytes 73732
  10.0 25.5 %copy-start.1 = (bf16[30,6144]{0,1:T(8,128)(2,1)}, bf16[30,6144]{0,1:T(8,128)(2,1)S(1)}, u32[]{:S(2)}) copy-start(bf16[30,6144]{0,1:T(8,128)(2,1)S(1)} %copy.97) | copy-start | bytes 1105924
  10.0 22.3 %copy-start.16 = (f32[4,1536]{1,0:T(4,128)S(1)}, f32[4,1536]{1,0:T(4,128)}, u32[]{:S(2)}) copy-start(f32[4,1536]{1,0:T(4,128)} %param.24) | copy-start | bytes 73732
  25.1 10.4 %copy-start.4 = (f32[180,1536]{1,0:T(8,128)S(1)}, f32[180,1536]{1,0:T(8,128)}, u32[]{:S(2)}) copy-start(f32[180,1536]{1,0:T(8,128)} %param.15) | copy-start | bytes 3317764
  27.6 264.6 %all-gather.5.cloned.1.call-start = ((), (), s32[]{:S(2)}) async-start(), calls=%async_computation.1 | async-start | bytes 8110080 | tf_op jit(solution)/shard_map/all_gather | solution.py:94
  27.7 0.5 copy-start.24
  27.7 10.2 %copy-start.25 = (s32[128]{0:T(128)}, s32[128]{0:T(128)S(1)}, u32[]{:S(2)}) copy-start(s32[128]{0:T(128)S(1)} %get-tuple-element.9) | copy-start | bytes 1540
  29.0 18.1 %collective-permute-start = (bf16[30,128]{1,0:T(8,128)(2,1)S(1)}, bf16[30,128]{1,0:T(8,128)(2,1)}, u32[]{:S(2)}, u32[]{:S(2)}) collective-permute-start(bf16[30,128]{1,0:T(8,128)(2,1)S(1)} %bitcast.177), channel_id=1, source_target_pairs={{0,32},{32,64},{64,96},{96,128},{128,160},{160,192},{192,224},{224... | collective-permute-start | bytes 23048 | tf_op jit(solution)/shard_map/ppermute | solution.py:19
  29.0 16.9 %collective-permute-start.1 = (s32[1]{0:T(128)}, s32[1]{0:T(128)}, u32[]{:S(2)}, u32[]{:S(2)}) collective-permute-start(s32[1]{0:T(128)} %param.20), channel_id=1, source_target_pairs={{0,224},{32,0},{64,32},{96,64},{128,96},{160,128},{192,160},{224,1... | collective-permute-start | bytes 20 | tf_op jit(solution)/shard_map/ppermute | solution.py:19
  38.0 4.4 %copy-start.7 = (f32[3,1536]{1,0:T(4,128)S(1)}, f32[3,1536]{1,0:T(4,128)}, u32[]{:S(2)}) copy-start(f32[3,1536]{1,0:T(4,128)} %param.23) | copy-start | bytes 55300
  41.7 6.1 %copy-start.9 = (f32[16,10]{1,0:T(8,128)S(1)}, f32[16,10]{1,0:T(8,128)}, u32[]{:S(2)}) copy-start(f32[16,10]{1,0:T(8,128)} %param.28) | copy-start | bytes 1924
  41.7 6.3 %copy-start.12 = (f32[16,128]{1,0:T(8,128)S(1)}, f32[16,128]{1,0:T(8,128)}, u32[]{:S(2)}) copy-start(f32[16,128]{1,0:T(8,128)} %param.22) | copy-start | bytes 24580
  41.7 6.3 %copy-start.14 = (f32[16,128]{1,0:T(8,128)S(1)}, f32[16,128]{1,0:T(8,128)}, u32[]{:S(2)}) copy-start(f32[16,128]{1,0:T(8,128)} %param.21) | copy-start | bytes 24580
  41.7 6.5 %copy-start.10 = (f32[10,16]{1,0:T(8,128)S(1)}, f32[10,16]{1,0:T(8,128)}, u32[]{:S(2)}) copy-start(f32[10,16]{1,0:T(8,128)} %param.29) | copy-start | bytes 1924
  48.4 117.2 %collective-permute-start.2 = (f32[30,128]{0,1:T(8,128)S(1)}, f32[30,128]{0,1:T(8,128)}, u32[]{:S(2)}, u32[]{:S(2)}) collective-permute-start(f32[30,128]{0,1:T(8,128)S(1)} %copy.106), channel_id=1, source_target_pairs={{0,224},{32,0},{64,32},{96,64},{128,96},{160,128},{192,160},{224,1... | collective-permute-start | bytes 46088 | tf_op jit(solution)/shard_map/ppermute | solution.py:19
  161.0 2.2 copy-start.19
  163.2 2.5 copy-start.22
  168.5 3.3 copy-start.5
  171.8 2.2 copy-start.6
  174.0 19.6 %copy-start.3 = (f32[180,1536]{1,0:T(8,128)}, f32[180,1536]{1,0:T(8,128)S(1)}, u32[]{:S(2)}) copy-start(f32[180,1536]{1,0:T(8,128)S(1)} %fusion.5) | copy-start | bytes 3317764
  175.5 27.9 %copy-start.2 = (bf16[30,6144]{0,1:T(8,128)(2,1)}, bf16[30,6144]{0,1:T(8,128)(2,1)S(1)}, u32[]{:S(2)}) copy-start(bf16[30,6144]{0,1:T(8,128)(2,1)S(1)} %copy.109) | copy-start | bytes 1105924
  193.6 10.6 %collective-permute-start.3 = (bf16[30,128]{1,0:T(8,128)(2,1)S(1)}, bf16[30,128]{1,0:T(8,128)(2,1)S(1)}, u32[]{:S(2)}, u32[]{:S(2)}) collective-permute-start(bf16[30,128]{1,0:T(8,128)(2,1)S(1)} %bitcast.178), channel_id=1, source_target_pairs={{0,32},{32,64},{64,96},{96,128},{128,160},{160,192},{192,224},{224... | collective-permute-start | bytes 23048 | tf_op jit(solution)/shard_map/ppermute | solution.py:19
  196.1 3.7 %copy-start.8 = (f32[3,1536]{1,0:T(4,128)S(1)}, f32[3,1536]{1,0:T(4,128)}, u32[]{:S(2)}) copy-start(f32[3,1536]{1,0:T(4,128)} %param.23) | copy-start | bytes 55300
  199.8 4.6 %copy-start.13 = (f32[16,128]{1,0:T(8,128)S(1)}, f32[16,128]{1,0:T(8,128)}, u32[]{:S(2)}) copy-start(f32[16,128]{1,0:T(8,128)} %param.22) | copy-start | bytes 24580
  199.8 4.6 %copy-start.15 = (f32[16,128]{1,0:T(8,128)S(1)}, f32[16,128]{1,0:T(8,128)}, u32[]{:S(2)}) copy-start(f32[16,128]{1,0:T(8,128)} %param.21) | copy-start | bytes 24580
  199.8 4.6 %copy-start.20 = (pred[128]{0:T(512)(128)(4,1)S(1)}, pred[128]{0:T(512)(128)(4,1)}, u32[]{:S(2)}) copy-start(pred[128]{0:T(512)(128)(4,1)} %iota_compare_fusion.1) | copy-start | bytes 388
  199.8 5.3 %copy-start.11 = (f32[10,16]{1,0:T(8,128)S(1)}, f32[10,16]{1,0:T(8,128)}, u32[]{:S(2)}) copy-start(f32[10,16]{1,0:T(8,128)} %param.29) | copy-start | bytes 1924
  205.5 120.9 %collective-permute-start.4 = (f32[30,128]{0,1:T(8,128)S(1)}, f32[30,128]{0,1:T(8,128)}, u32[]{:S(2)}, u32[]{:S(2)}) collective-permute-start(f32[30,128]{0,1:T(8,128)S(1)} %copy.118), channel_id=1, source_target_pairs={{0,224},{32,0},{64,32},{96,64},{128,96},{160,128},{192,160},{224,1... | collective-permute-start | bytes 46088 | tf_op jit(solution)/shard_map/ppermute | solution.py:19
  321.7 2.2 copy-start.21
  323.9 2.5 copy-start.23
Sparse Core Ops, SparseCore 0:
  27.8 103.7 all-gather.2
  193.0 99.1 all-gather.4
where the time goes:
time: 343 us; the launch traced here: 342 us
  waiting for transfers between devices  168 us (49%)
  local copies, waits for them, and re-layouts  115 us (34%)
  other arithmetic  27 us (8%)
  between operations  15.4 us (4%)
  matrix products  12.8 us (4%)
  starting transfers between devices  3.56 us (1%)
    all_gather x2, waiting for transfers between devices, shards(): gathered = lax.all_gather(outgoing, 'dom', axis=1, tiled=True)  168 us
    gather x2, local copies, waits for them, and re-layouts, shards(): exterior = trace_pool[:, face_source.reshape(-1)]  44.1 us
    gather x2, local copies, waits for them, and re-layouts, shards(): outgoing = traces[:, send_faces.reshape(-1)].reshape(rows, peers, -1)  29.9 us
    reshape x2, local copies, waits for them, and re-layouts, advance_local(): jnp.dot(volume_ops, packed, preferred_element_type=jnp.float32)  7.41 us
    reduce_sum x2, other arithmetic, advance_local(): volume = jnp.sum(volume * geometry[:, None, :], axis=0)  7.12 us
  transfers between devices with their start and end apart: 7, of which 2 were waited for; matrix products, arithmetic and copies ran while one was open for 29% of the time, Pallas kernels for 0%

commit v1 on v0

v1 whole, which is shorter than its diff:
```python
import functools

import jax
import jax.numpy as jnp
from jax import lax
from jax.experimental import pallas as pl
from jax.experimental.pallas import tpu as pltpu
from jax.sharding import PartitionSpec as P

STEPS = 2
NEWTON = 4
IMPEDANCE = 1.0
FRICTION_A = 0.2
REGULARIZE = 0.25
TIME_STEP = 0.25

F32 = jnp.float32
BF16 = jnp.bfloat16

VALUES = 180
TRACE = 30
ROWS = 32
ELEMS = 1536
PEERS = 32
SLOTS = 128
POINTS = 16
NODES = 10
BLOCK = 256
TILES = ELEMS // BLOCK
LOCAL = 4 * TILES
REMOTE = PEERS * SLOTS // BLOCK
FAULTS = 2 * SLOTS
VMEM_LIMIT = 32 * 2**20


def inverse_sinh(value):
    return jnp.log(value + jnp.sqrt(value * value + 1.0))


def row_order():
    row = lax.broadcasted_iota(jnp.int32, (4 * ROWS, 4 * TRACE), 0)
    column = lax.broadcasted_iota(jnp.int32, (4 * ROWS, 4 * TRACE), 1)
    face = lax.shift_right_logical(row, 5)
    value = jnp.bitwise_and(row, ROWS - 1)
    return jnp.where(column == 4 * value + face, 1.0, 0.0).astype(BF16)


def make_traces(packed, restriction, table, traces):
    ordered = jnp.dot(row_order(), restriction, preferred_element_type=F32).astype(BF16)
    made = jnp.dot(ordered, packed, preferred_element_type=F32).astype(BF16)
    if traces is not None:
        traces[...] = made
    for block in range(LOCAL):
        face, tile = divmod(block, TILES)
        table[block * ROWS : (block + 1) * ROWS, :] = made[
            face * ROWS : (face + 1) * ROWS, tile * BLOCK : (tile + 1) * BLOCK
        ]


def pick(table, index, blocks):
    low = jnp.bitwise_and(index, BLOCK - 1)
    high = jnp.broadcast_to(lax.shift_right_logical(index, 8), (ROWS, index.shape[1]))
    lanes = lax.broadcasted_iota(jnp.int32, (BLOCK, index.shape[1]), 0)
    selector = jnp.where(lanes == low, 1.0, 0.0).astype(BF16)
    product = jnp.dot(table[0 : blocks * ROWS, :], selector, preferred_element_type=F32)
    picked = jnp.zeros((ROWS, index.shape[1]), F32)
    for block in range(blocks):
        picked = jnp.where(high == block, product[block * ROWS : (block + 1) * ROWS], picked)
    return picked


def send_traces(table, send_faces, plus_faces, minus_faces, sent, plus_out, minus_out):
    def body(turn, carry):
        faces = send_faces[pl.ds(pl.multiple_of(turn * 8, 8), 8), :]
        for pair in range(4):
            index = jnp.concatenate([faces[2 * pair : 2 * pair + 1], faces[2 * pair + 1 : 2 * pair + 2]], axis=1)
            picked = pick(table, index, LOCAL).astype(BF16)
            sent[turn * 8 + 2 * pair] = picked[:, :SLOTS]
            sent[turn * 8 + 2 * pair + 1] = picked[:, SLOTS:]
        return carry

    index = jnp.concatenate([plus_faces[...], minus_faces[...]], axis=1)
    picked = pick(table, index, LOCAL).astype(BF16)
    plus_out[...] = picked[:, :SLOTS].astype(plus_out.dtype)
    minus_out[...] = picked[:, SLOTS:]
    lax.fori_loop(0, PEERS // 8, body, 0)


def friction(difference, stress, state, to_points, to_nodes, jump):
    weights = [jnp.broadcast_to(to_points[:, n : n + 1], stress.shape) for n in range(NODES)]
    at_points = []
    for component in range(3):
        total = weights[0] * difference[component * NODES : component * NODES + 1]
        for n in range(1, NODES):
            row = component * NODES + n
            total = total + weights[n] * difference[row : row + 1]
        at_points.append(total)
    magnitude = jnp.sqrt(at_points[1] * at_points[1] + at_points[2] * at_points[2] + REGULARIZE)
    rate_scale = 0.5 * jnp.exp(state)
    slip_rate = jnp.zeros_like(magnitude)
    for _ in range(NEWTON):
        scaled_rate = slip_rate * rate_scale
        residual_value = IMPEDANCE * (magnitude - slip_rate) - stress * FRICTION_A * inverse_sinh(scaled_rate)
        derivative = IMPEDANCE + stress * FRICTION_A * rate_scale / jnp.sqrt(1.0 + scaled_rate * scaled_rate)
        slip_rate = slip_rate + residual_value / derivative
    share = slip_rate / magnitude
    point_jump = [at_points[0], at_points[1] * share, at_points[2] * share]
    columns = [jnp.broadcast_to(to_nodes[:, q : q + 1], (NODES, stress.shape[1])) for q in range(POINTS)]
    for component in range(3):
        total = columns[0] * point_jump[component][0:1]
        for q in range(1, POINTS):
            total = total + columns[q] * point_jump[component][q : q + 1]
        jump[component * NODES : (component + 1) * NODES, :] = total
    return slip_rate


def first_kernel(
    element_state, send_faces, plus_faces, minus_faces, fault_count, stress, state_variable, restriction,
    sent, plus_out, minus_out, table,
):
    make_traces(element_state[...].astype(BF16), restriction[...], table, None)
    send_traces(table, send_faces, plus_faces, minus_faces, sent, plus_out.at[0:ROWS, :], minus_out)
    plus_out[ROWS : ROWS + POINTS, :] = stress[...]
    plus_out[ROWS + POINTS : ROWS + 2 * POINTS, :] = state_variable[...]
    plus_out[ROWS + 2 * POINTS :, :] = jnp.full((8, SLOTS), fault_count[0], jnp.int32).astype(F32)


def step_kernel(
    last, element_state, received, partner, next_plus, next_constants, face_source, send_faces, plus_faces, minus_faces,
    own_plus, own_minus, fault_count, stress, state_variable, geometry, face_area, restriction, volume_ops,
    lift_operator, to_points, to_nodes, *rest,
):
    if last:
        state_out, slip_out, table, traces, jump, masked, override, scaled = rest
    else:
        state_out, sent, plus_out, minus_out, table, traces, jump, masked, override, scaled = rest
    packed = element_state[...].astype(BF16)
    make_traces(packed, restriction[...], table, traces)
    for block in range(REMOTE):
        table[(LOCAL + block) * ROWS : (LOCAL + block + 1) * ROWS, :] = jnp.concatenate(
            [received[2 * block], received[2 * block + 1]], axis=1
        )

    plus_side = jnp.concatenate([own_plus[0:ROWS, :].astype(F32), next_plus[0:ROWS, :].astype(F32)], axis=1)
    minus_side = jnp.concatenate([partner[...].astype(F32), own_minus[...].astype(F32)], axis=1)
    both_stress = jnp.concatenate([stress[...], next_constants[ROWS : ROWS + POINTS, :]], axis=1)
    both_state = jnp.concatenate([state_variable[...], next_constants[ROWS + POINTS : ROWS + 2 * POINTS, :]], axis=1)
    slip_rate = friction(plus_side - minus_side, both_stress, both_state, to_points[...], to_nodes[...], jump)
    slot = lax.broadcasted_iota(jnp.int32, (1, SLOTS), 1)
    own_live = slot < fault_count[0]
    next_live = slot.astype(F32) < next_constants[ROWS + 2 * POINTS : ROWS + 2 * POINTS + 1, :]
    sign = jnp.concatenate([jnp.where(own_live, 1.0, 0.0), jnp.where(next_live, -1.0, 0.0)], axis=1)
    if last:
        slip_out[...] = jnp.where(own_live, slip_rate[:, :SLOTS], 0.0)

    row = lax.broadcasted_iota(jnp.int32, (ROWS, FAULTS), 0)
    jump[TRACE : TRACE + 2, :] = jnp.zeros((2, FAULTS), F32)
    values = jnp.where(row < TRACE, jump[...] * sign, jnp.where(row == TRACE, jnp.abs(sign), 0.0))
    coarse = values.astype(BF16).astype(F32)
    parts = jnp.concatenate([coarse, values - coarse], axis=0)
    faces = jnp.concatenate([plus_faces[...], minus_faces[...]], axis=1)
    high = jnp.broadcast_to(lax.shift_right_logical(faces, 8), parts.shape)
    for block in range(LOCAL):
        masked[block * 2 * ROWS : (block + 1) * 2 * ROWS, :] = jnp.where(high == block, parts, 0.0).astype(BF16)
    lanes = lax.broadcasted_iota(jnp.int32, (BLOCK, FAULTS), 0)
    selector = jnp.where(lanes == jnp.bitwise_and(faces, BLOCK - 1), 1.0, 0.0).astype(BF16)
    override[...] = lax.dot_general(masked[...], selector, (((1,), (1,)), ((), ())), preferred_element_type=F32)

    def body(face, carry):
        rows = pl.ds(pl.multiple_of(face * ROWS, ROWS), ROWS)
        for tile in range(TILES):
            columns = slice(tile * BLOCK, (tile + 1) * BLOCK)
            exterior = pick(table, face_source[pl.ds(face, 1), columns], LOCAL + REMOTE)
            start = (face * TILES + tile) * 2 * ROWS
            changed = (
                override[pl.ds(pl.multiple_of(start, ROWS), ROWS), :]
                + override[pl.ds(pl.multiple_of(start + ROWS, ROWS), ROWS), :]
            )
            plain = traces[rows, columns].astype(F32) - exterior
            face_jump = jnp.where(changed[TRACE : TRACE + 1] > 0.5, changed, plain)
            scaled[rows, columns] = (face_jump * face_area[pl.ds(face, 1), columns]).astype(BF16)
        return carry

    lax.fori_loop(0, 4, body, 0)

    ordered = lax.dot_general(
        lift_operator[...], row_order(), (((1,), (1,)), ((), ())), preferred_element_type=F32
    ).astype(BF16)
    change = -jnp.dot(ordered, scaled[...], preferred_element_type=F32)
    operators = volume_ops[...].astype(F32)
    for direction in range(3):
        operator = operators[direction * VALUES : (direction + 1) * VALUES].astype(BF16)
        change = change + jnp.dot(operator, packed, preferred_element_type=F32) * geometry[direction : direction + 1, :]
    state = element_state[...] + TIME_STEP * change
    state_out[...] = state
    if not last:
        make_traces(state.astype(BF16), restriction[...], table, None)
        send_traces(table, send_faces, plus_faces, minus_faces, sent, plus_out, minus_out)


def call(kernel, outs, scratch, smem, *args):
    vmem = pl.BlockSpec(memory_space=pltpu.VMEM)
    return pl.pallas_call(
        kernel,
        out_shape=outs,
        in_specs=[pl.BlockSpec(memory_space=pltpu.SMEM) if i == smem else vmem for i in range(len(args))],
        out_specs=[vmem] * len(outs),
        scratch_shapes=scratch,
        compiler_params=pltpu.CompilerParams(vmem_limit_bytes=VMEM_LIMIT),
    )(*args)


def shards(
    element_state,
    face_source,
    send_faces,
    plus_faces,
    minus_faces,
    fault_count,
    normal_stress,
    state_variable,
    geometry,
    face_area,
    restriction,
    volume_ops,
    lift_operator,
    to_points,
    to_nodes,
):
    segments = lax.axis_size("seg")
    up = [(s, (s + 1) % segments) for s in range(segments)]
    down = [(s, (s - 1) % segments) for s in range(segments)]
    plus_faces = plus_faces.reshape(1, SLOTS)
    minus_faces = minus_faces.reshape(1, SLOTS)
    block = jax.ShapeDtypeStruct((ROWS, SLOTS), BF16)
    sent_shape = jax.ShapeDtypeStruct((PEERS, ROWS, SLOTS), BF16)
    table = pltpu.VMEM(((LOCAL + REMOTE) * ROWS, BLOCK), BF16)
    scratch = [
        table,
        pltpu.VMEM((4 * ROWS, ELEMS), BF16),
        pltpu.VMEM((ROWS, FAULTS), F32),
        pltpu.VMEM((LOCAL * 2 * ROWS, FAULTS), BF16),
        pltpu.VMEM((LOCAL * 2 * ROWS, BLOCK), F32),
        pltpu.VMEM((4 * ROWS, ELEMS), BF16),
    ]
    constants_rows = ROWS + 2 * POINTS + 8
    sent, plus, minus = call(
        first_kernel,
        [sent_shape, jax.ShapeDtypeStruct((constants_rows, SLOTS), F32), block],
        [table],
        4,
        element_state, send_faces, plus_faces, minus_faces, fault_count, normal_stress, state_variable, restriction,
    )
    next_constants = None
    for step in range(STEPS):
        last = step == STEPS - 1
        partner = lax.ppermute(minus, "seg", up)
        next_plus = lax.ppermute(plus, "seg", down)
        if next_constants is None:
            next_constants = next_plus
        received = lax.all_to_all(sent, "dom", 0, 0, tiled=True)
        state_shape = jax.ShapeDtypeStruct(element_state.shape, F32)
        if last:
            outs = [state_shape, jax.ShapeDtypeStruct(normal_stress.shape, F32)]
        else:
            outs = [state_shape, sent_shape, block, block]
        result = call(
            functools.partial(step_kernel, last), outs, scratch, 11,
            element_state, received, partner, next_plus, next_constants, face_source, send_faces, plus_faces, minus_faces,
            plus, minus, fault_count, normal_stress, state_variable, geometry, face_area, restriction, volume_ops,
            lift_operator, to_points, to_nodes,
        )
        if last:
            return tuple(result)
        element_state, sent, plus, minus = result


def solution(mesh):
    placed = (
        P(None, ("seg", "dom")),
        P(None, ("seg", "dom")),
        P(None, ("seg", "dom")),
        P(("seg", "dom")),
        P(("seg", "dom")),
        P(("seg", "dom")),
        P(None, ("seg", "dom")),
        P(None, ("seg", "dom")),
        P(None, ("seg", "dom")),
        P(None, ("seg", "dom")),
        P(),
        P(),
        P(),
        P(),
        P(),
    )
    return jax.shard_map(
        shards,
        mesh=mesh,
        in_specs=placed,
        out_specs=(P(None, ("seg", "dom")), P(None, ("seg", "dom"))),
        check_vma=False,
    )
```

time: 343 us -> 69.3 us (0.20)
  waiting for transfers between devices: 168 us -> 22.6 us
  local copies, waits for them, and re-layouts: 115 us -> 5.77 us
  other arithmetic: 27 us -> 0 us
  Pallas kernels: 0 us -> 21 us
  starting transfers between devices: 3.56 us -> 17.8 us
  between operations: 15.4 us -> 1.49 us
  matrix products: 12.8 us -> 0 us
    all_gather x2 -> x0, waiting for transfers between devices: 168 us -> none  [shards(): gathered = lax.all_gather(outgoing, 'dom', axis=1, tiled=True)]
    gather x12 -> x0, local copies, waits for them, and re-layouts: 77.2 us -> none  [the longest x2 44.1 us: shards(): exterior = trace_pool[:, face_source.reshape(-1)]]
    pallas_call x0 -> x3, Pallas kernels: none -> 21 us  [call(): pl.pallas_call(kernel, out_shape=outs, in_specs=[pl.BlockSpec(memory_spac...]
    all_to_all x0 -> x2, waiting for transfers between devices: none -> 18.8 us  [shards(): received = lax.all_to_all(sent, 'dom', 0, 0, tiled=True)]
    reshape x16 -> x0, local copies, waits for them, and re-layouts: 17.5 us -> none  [the longest x2 7.41 us: advance_local(): jnp.dot(volume_ops, packed, preferred_element_type=jnp.float32)]
    all_to_all x0 -> x2, starting transfers between devices: none -> 15.6 us  [shards(): received = lax.all_to_all(sent, 'dom', 0, 0, tiled=True)]
    dot_general x10 -> x0, matrix products: 12.8 us -> none  [the longest x2 5.33 us: advance_local(): jnp.dot(lift_operator, scaled_jump, preferred_element_type=jnp.float32)]
    scatter x4 -> x0, other arithmetic: 10.3 us -> none  [the longest x2 5.4 us: shards(): face_jump.at[:, minus_faces]]
  transfers between devices with their start and end apart: 7 -> 6, of which waited for: 2 -> 4; matrix products, arithmetic and copies ran while one was open for 29% -> 0% of each run, Pallas kernels for 0% -> 0%
where the time goes in v1:
time: 69.3 us; the launch traced here: 68.8 us
  waiting for transfers between devices  22.6 us (33%)
  Pallas kernels  21 us (30%)
  starting transfers between devices  17.8 us (26%)
  local copies, waits for them, and re-layouts  5.77 us (8%)
  between operations  1.49 us (2%)
    pallas_call x3, Pallas kernels, call(): pl.pallas_call(kernel, out_shape=outs, in_specs=[pl.BlockSpec(memory_spac...  21 us
    all_to_all x2, waiting for transfers between devices, shards(): received = lax.all_to_all(sent, 'dom', 0, 0, tiled=True)  18.8 us
    all_to_all x2, starting transfers between devices, shards(): received = lax.all_to_all(sent, 'dom', 0, 0, tiled=True)  15.6 us
    unnamed x40, local copies, waits for them, and re-layouts  5.77 us
    ppermute x2, waiting for transfers between devices, shards(): partner = lax.ppermute(minus, 'seg', up)  3.76 us
    ppermute x2, starting transfers between devices, shards(): next_plus = lax.ppermute(plus, 'seg', down)  1.75 us
  transfers between devices with their start and end apart: 6, of which 4 were waited for; matrix products, arithmetic and copies ran while one was open for 0% of the time, Pallas kernels for 0%

profile of v1, /device:TPU:6, one launch (start us, length us, event | category | flops | bytes accessed | tf_op | source)
XLA Modules:
  0.0 68.8 jit_solution(11741287097287021970)
XLA Ops:
  1.3 0.9 %copy.17.restriction = bf16[120,180]{1,0:T(8,128)(2,1)S(1)} copy(bf16[120,180]{0,1:T(8,128)(2,1)} %param.25) | data formatting | bytes 86400 | tf_op args[10]
  2.2 0.0 copy-start
  2.2 1.2 %copy-done = f32[180,1536]{1,0:T(8,128)S(1)} copy-done((f32[180,1536]{1,0:T(8,128)S(1)}, f32[180,1536]{1,0:T(8,128)}, u32[]{:S(2)}) %copy-start) | copy-done | bytes 1105944
  3.4 0.7 %copy-done.3 = s32[32,128]{1,0:T(8,128)S(1)} copy-done((s32[32,128]{1,0:T(8,128)S(1)}, s32[32,128]{1,0:T(8,128)}, u32[]{:S(2)}) %copy-start.3) | copy-done | bytes 16408
  4.1 0.0 copy-start.8
  4.1 0.7 %copy-done.8 = f32[16,128]{1,0:T(8,128)S(1)} copy-done((f32[16,128]{1,0:T(8,128)S(1)}, f32[16,128]{1,0:T(8,128)}, u32[]{:S(2)}) %copy-start.8) | copy-done | bytes 8216
  4.8 0.0 copy-start.10
  4.8 0.7 %copy-done.10 = f32[16,128]{1,0:T(8,128)S(1)} copy-done((f32[16,128]{1,0:T(8,128)S(1)}, f32[16,128]{1,0:T(8,128)}, u32[]{:S(2)}) %copy-start.10) | copy-done | bytes 8216
  5.5 0.7 copy-done.14
  6.2 0.7 copy-done.16
  6.9 0.0 copy-start.5
  6.9 0.0 copy-start.6
  6.9 0.0 copy-start.7
  6.9 0.0 copy-start.9
  6.9 0.0 copy-start.11
  6.9 0.0 copy-start.12
  6.9 0.0 copy-start.13
  6.9 0.0 copy-start.15
  7.0 0.0 copy-start.17
  7.0 3.6 %shard_map.158 = (bf16[32,32,128]{2,1,0:T(8,128)(2,1)}, f32[72,128]{1,0:T(8,128)S(1)}, bf16[32,128]{1,0:T(8,128)(2,1)S(1)}) custom-call(f32[180,1536]{1,0:T(8,128)S(1)} %copy-done, s32[32,128]{1,0:T(8,128)S(1)} %copy-done.3, s32[1,128]{1,0:T(1,128)S(1)} %bitcast.2, s32[1,128]{1,0:T(1,128)S(1)} %bitcast.5, s32[1]{0:T(128)S(6)} %copy.22.fault_count, ...), custom_call_target="tpu_custom_call" | custom-call | tf_op jit(solution)/shard_map/pallas_call | solution.py:203
  10.6 11.5 %all-to-all-start = ((bf16[32,32,128]{2,1,0:T(8,128)(2,1)}), bf16[32,32,128]{2,1,0:T(8,128)(2,1)S(1)}, u32[]{:S(2)}, u32[]{:S(2)}) async-start(bf16[32,32,128]{2,1,0:T(8,128)(2,1)} %get-tuple-element.9), calls=%async_computation | async-start | bytes 524288 | tf_op jit(solution)/shard_map/all_to_all | solution.py:261
  22.1 0.0 collective-permute-start.1
  22.1 0.5 collective-permute-start
  22.6 0.0 copy-done.18
  22.6 0.1 copy.19.volume_ops
  22.8 2.4 %collective-permute-done.partner = bf16[32,128]{1,0:T(8,128)(2,1)S(1)} collective-permute-done((bf16[32,128]{1,0:T(8,128)(2,1)S(1)}, bf16[32,128]{1,0:T(8,128)(2,1)S(1)}, u32[]{:S(2)}, u32[]{:S(2)}) %collective-permute-start) | collective-permute-done | bytes 8224 | tf_op jit(solution)/shard_map/ppermute | solution.py:257
  25.2 0.0 collective-permute-done.1.next_plus.next_constants
  25.2 9.6 %all-to-all-done.received = bf16[32,32,128]{2,1,0:T(8,128)(2,1)S(1)} async-done(((bf16[32,32,128]{2,1,0:T(8,128)(2,1)}), bf16[32,32,128]{2,1,0:T(8,128)(2,1)S(1)}, u32[]{:S(2)}, u32[]{:S(2)}) %all-to-all-start) | async-done | bytes 262176 | tf_op jit(solution)/shard_map/all_to_all | solution.py:261
  34.8 0.0 copy-done.1
  34.8 0.0 copy-done.2
  34.8 0.0 copy-done.4
  34.8 0.0 copy-done.5
  34.8 0.0 copy-done.6
  34.8 0.0 copy-done.7
  34.8 0.0 copy-done.9
  34.8 0.0 copy-done.11
  34.8 0.0 copy-done.12
  34.8 0.0 copy-done.13
  34.9 0.0 copy-done.15
  34.9 0.0 copy-done.17
  34.9 10.0 %shard_map.159 = (f32[180,1536]{1,0:T(8,128)S(1)}, bf16[32,32,128]{2,1,0:T(8,128)(2,1)}, bf16[32,128]{1,0:T(8,128)(2,1)S(1)}, bf16[32,128]{1,0:T(8,128)(2,1)S(1)}) custom-call(f32[180,1536]{1,0:T(8,128)S(1)} %copy-done.1, bf16[32,32,128]{2,1,0:T(8,128)(2,1)S(1)} %all-to-all-done.received, bf16[32,128]{1,0:T(8,128)(2,1)S(1)} %collective-permute-done.partner, ...), custom_call_target="tpu_custom_call" | custom-call | tf_op jit(solution)/shard_map/pallas_call | solution.py:203
  44.8 4.1 %all-to-all-start.1 = ((bf16[32,32,128]{2,1,0:T(8,128)(2,1)}), bf16[32,32,128]{2,1,0:T(8,128)(2,1)S(1)}, u32[]{:S(2)}, u32[]{:S(2)}) async-start(bf16[32,32,128]{2,1,0:T(8,128)(2,1)} %get-tuple-element.13), calls=%async_computation.1 | async-start | bytes 524288 | tf_op jit(solution)/shard_map/all_to_all | solution.py:261
  48.9 0.0 collective-permute-start.2
  48.9 1.7 %collective-permute-start.3 = (bf16[32,128]{1,0:T(8,128)(2,1)S(1)}, bf16[32,128]{1,0:T(8,128)(2,1)S(1)}, u32[]{:S(2)}, u32[]{:S(2)}) collective-permute-start(bf16[32,128]{1,0:T(8,128)(2,1)S(1)} %get-tuple-element.15.own_plus), channel_id=1, source_target_pairs={{0,224},{32,0},{64,32},{96,64},{128,96},{160,128},{192,160},{224,1... | collective-permute-start | bytes 24584 | tf_op jit(solution)/shard_map/ppermute | solution.py:258
  50.7 1.3 %collective-permute-done.2.partner = bf16[32,128]{1,0:T(8,128)(2,1)S(1)} collective-permute-done((bf16[32,128]{1,0:T(8,128)(2,1)S(1)}, bf16[32,128]{1,0:T(8,128)(2,1)S(1)}, u32[]{:S(2)}, u32[]{:S(2)}) %collective-permute-start.2) | collective-permute-done | bytes 8224 | tf_op jit(solution)/shard_map/ppermute | solution.py:257
  52.0 0.0 collective-permute-done.3.next_plus
  52.0 9.3 %all-to-all-done.1.received = bf16[32,32,128]{2,1,0:T(8,128)(2,1)S(1)} async-done(((bf16[32,32,128]{2,1,0:T(8,128)(2,1)}), bf16[32,32,128]{2,1,0:T(8,128)(2,1)S(1)}, u32[]{:S(2)}, u32[]{:S(2)}) %all-to-all-start.1) | async-done | bytes 262176 | tf_op jit(solution)/shard_map/all_to_all | solution.py:261
  61.3 7.5 %shard_map.160 = (f32[180,1536]{1,0:T(8,128)}, f32[16,128]{1,0:T(8,128)}) custom-call(f32[180,1536]{1,0:T(8,128)S(1)} %get-tuple-element.12.element_state, bf16[32,32,128]{2,1,0:T(8,128)(2,1)S(1)} %all-to-all-done.1.received, bf16[32,128]{1,0:T(8,128)(2,1)S(1)} %collective-permute-done.2.partner, bf16[32,128]{1,0:T(8,128)(2,1)S(1)} %collective-permute-done.3.next_plus, ...), custom_call_target="tpu_custom_call" | custom-call | tf_op jit(solution)/shard_map/pallas_call | solution.py:203
  (7 shorter events, 0.0 us)
Async XLA Ops:
  2.2 1.3 %copy-start = (f32[180,1536]{1,0:T(8,128)S(1)}, f32[180,1536]{1,0:T(8,128)}, u32[]{:S(2)}) copy-start(f32[180,1536]{1,0:T(8,128)} %element_state.3) | copy-start | bytes 3317764
  3.4 0.7 %copy-start.3 = (s32[32,128]{1,0:T(8,128)S(1)}, s32[32,128]{1,0:T(8,128)}, u32[]{:S(2)}) copy-start(s32[32,128]{1,0:T(8,128)} %send_faces.5) | copy-start | bytes 49156
  4.1 0.7 %copy-start.8 = (f32[16,128]{1,0:T(8,128)S(1)}, f32[16,128]{1,0:T(8,128)}, u32[]{:S(2)}) copy-start(f32[16,128]{1,0:T(8,128)} %stress.5) | copy-start | bytes 24580
  4.8 0.7 %copy-start.10 = (f32[16,128]{1,0:T(8,128)S(1)}, f32[16,128]{1,0:T(8,128)}, u32[]{:S(2)}) copy-start(f32[16,128]{1,0:T(8,128)} %state_variable.5) | copy-start | bytes 24580
  5.5 0.7 copy-start.14
  6.2 0.7 copy-start.16
  6.9 15.8 %copy-start.18 = (bf16[540,180]{0,1:T(8,128)(2,1)S(1)}, bf16[540,180]{0,1:T(8,128)(2,1)}, u32[]{:S(2)}) copy-start(bf16[540,180]{0,1:T(8,128)(2,1)} %param.26) | copy-start | bytes 583204
  6.9 27.9 %copy-start.1 = (f32[180,1536]{1,0:T(8,128)S(1)}, f32[180,1536]{1,0:T(8,128)}, u32[]{:S(2)}) copy-start(f32[180,1536]{1,0:T(8,128)} %element_state.3) | copy-start | bytes 3317764
  6.9 27.9 %copy-start.2 = (bf16[180,120]{1,0:T(8,128)(2,1)S(1)}, bf16[180,120]{1,0:T(8,128)(2,1)}, u32[]{:S(2)}) copy-start(bf16[180,120]{1,0:T(8,128)(2,1)} %lift_operator.3) | copy-start | bytes 129604
  6.9 27.9 %copy-start.4 = (s32[32,128]{1,0:T(8,128)S(1)}, s32[32,128]{1,0:T(8,128)}, u32[]{:S(2)}) copy-start(s32[32,128]{1,0:T(8,128)} %send_faces.5) | copy-start | bytes 49156
  6.9 27.9 %copy-start.5 = (s32[4,1536]{1,0:T(4,128)S(1)}, s32[4,1536]{1,0:T(4,128)}, u32[]{:S(2)}) copy-start(s32[4,1536]{1,0:T(4,128)} %face_source.3) | copy-start | bytes 73732
  6.9 27.9 %copy-start.6 = (f32[3,1536]{1,0:T(4,128)S(1)}, f32[3,1536]{1,0:T(4,128)}, u32[]{:S(2)}) copy-start(f32[3,1536]{1,0:T(4,128)} %geometry.3) | copy-start | bytes 55300
  6.9 27.9 %copy-start.7 = (f32[4,1536]{1,0:T(4,128)S(1)}, f32[4,1536]{1,0:T(4,128)}, u32[]{:S(2)}) copy-start(f32[4,1536]{1,0:T(4,128)} %face_area.3) | copy-start | bytes 73732
  6.9 27.9 %copy-start.9 = (f32[16,128]{1,0:T(8,128)S(1)}, f32[16,128]{1,0:T(8,128)}, u32[]{:S(2)}) copy-start(f32[16,128]{1,0:T(8,128)} %stress.5) | copy-start | bytes 24580
  6.9 27.9 %copy-start.11 = (f32[16,128]{1,0:T(8,128)S(1)}, f32[16,128]{1,0:T(8,128)}, u32[]{:S(2)}) copy-start(f32[16,128]{1,0:T(8,128)} %state_variable.5) | copy-start | bytes 24580
  6.9 27.9 %copy-start.12 = (f32[16,10]{1,0:T(8,128)S(1)}, f32[16,10]{1,0:T(8,128)}, u32[]{:S(2)}) copy-start(f32[16,10]{1,0:T(8,128)} %to_points.3) | copy-start | bytes 1924
  6.9 27.9 %copy-start.13 = (f32[10,16]{1,0:T(8,128)S(1)}, f32[10,16]{1,0:T(8,128)}, u32[]{:S(2)}) copy-start(f32[10,16]{1,0:T(8,128)} %to_nodes.3) | copy-start | bytes 1924
  6.9 27.9 %copy-start.15 = (s32[128]{0:T(128)S(1)}, s32[128]{0:T(128)}, u32[]{:S(2)}) copy-start(s32[128]{0:T(128)} %param.18) | copy-start | bytes 1540
  7.0 27.9 %copy-start.17 = (s32[128]{0:T(128)S(1)}, s32[128]{0:T(128)}, u32[]{:S(2)}) copy-start(s32[128]{0:T(128)} %param.19) | copy-start | bytes 1540
  10.6 24.2 %all-to-all-start = ((bf16[32,32,128]{2,1,0:T(8,128)(2,1)}), bf16[32,32,128]{2,1,0:T(8,128)(2,1)S(1)}, u32[]{:S(2)}, u32[]{:S(2)}) async-start(bf16[32,32,128]{2,1,0:T(8,128)(2,1)} %get-tuple-element.9), calls=%async_computation | async-start | bytes 524288 | tf_op jit(solution)/shard_map/all_to_all | solution.py:261
  22.1 3.1 %collective-permute-start.1 = (f32[72,128]{1,0:T(8,128)S(1)}, f32[72,128]{1,0:T(8,128)S(1)}, u32[]{:S(2)}, u32[]{:S(2)}) collective-permute-start(f32[72,128]{1,0:T(8,128)S(1)} %get-tuple-element.11.own_plus), channel_id=1, source_target_pairs={{0,224},{32,0},{64,32},{96,64},{128,96},{160,128},{192,160},{224,1... | collective-permute-start | bytes 110600 | tf_op jit(solution)/shard_map/ppermute | solution.py:258
  22.1 3.1 %collective-permute-start = (bf16[32,128]{1,0:T(8,128)(2,1)S(1)}, bf16[32,128]{1,0:T(8,128)(2,1)S(1)}, u32[]{:S(2)}, u32[]{:S(2)}) collective-permute-start(bf16[32,128]{1,0:T(8,128)(2,1)S(1)} %get-tuple-element.10.own_minus), channel_id=1, source_target_pairs={{0,32},{32,64},{64,96},{96,128},{128,160},{160,192},{192,224},{224... | collective-permute-start | bytes 24584 | tf_op jit(solution)/shard_map/ppermute | solution.py:257
  44.8 16.5 %all-to-all-start.1 = ((bf16[32,32,128]{2,1,0:T(8,128)(2,1)}), bf16[32,32,128]{2,1,0:T(8,128)(2,1)S(1)}, u32[]{:S(2)}, u32[]{:S(2)}) async-start(bf16[32,32,128]{2,1,0:T(8,128)(2,1)} %get-tuple-element.13), calls=%async_computation.1 | async-start | bytes 524288 | tf_op jit(solution)/shard_map/all_to_all | solution.py:261
  48.9 3.1 %collective-permute-start.2 = (bf16[32,128]{1,0:T(8,128)(2,1)S(1)}, bf16[32,128]{1,0:T(8,128)(2,1)S(1)}, u32[]{:S(2)}, u32[]{:S(2)}) collective-permute-start(bf16[32,128]{1,0:T(8,128)(2,1)S(1)} %get-tuple-element.14.own_minus), channel_id=1, source_target_pairs={{0,32},{32,64},{64,96},{96,128},{128,160},{160,192},{192,224},{224... | collective-permute-start | bytes 24584 | tf_op jit(solution)/shard_map/ppermute | solution.py:257
  48.9 3.1 %collective-permute-start.3 = (bf16[32,128]{1,0:T(8,128)(2,1)S(1)}, bf16[32,128]{1,0:T(8,128)(2,1)S(1)}, u32[]{:S(2)}, u32[]{:S(2)}) collective-permute-start(bf16[32,128]{1,0:T(8,128)(2,1)S(1)} %get-tuple-element.15.own_plus), channel_id=1, source_target_pairs={{0,224},{32,0},{64,32},{96,64},{128,96},{160,128},{192,160},{224,1... | collective-permute-start | bytes 24584 | tf_op jit(solution)/shard_map/ppermute | solution.py:258

commit v2 on v1

v2 whole, which is shorter than its diff:
```python
import functools

import jax
import jax.numpy as jnp
from jax import lax
from jax.experimental import pallas as pl
from jax.experimental.pallas import tpu as pltpu
from jax.sharding import PartitionSpec as P

STEPS = 2
NEWTON = 4
IMPEDANCE = 1.0
FRICTION_A = 0.2
REGULARIZE = 0.25
TIME_STEP = 0.25

F32 = jnp.float32
BF16 = jnp.bfloat16

VALUES = 180
TRACE = 30
ROWS = 32
ELEMS = 1536
PEERS = 32
SLOTS = 128
POINTS = 16
NODES = 10
BLOCK = 256
TILES = ELEMS // BLOCK
LOCAL = 4 * TILES
REMOTE = PEERS * SLOTS // BLOCK
FAULTS = 2 * SLOTS
PARTS = 3
VMEM_LIMIT = 32 * 2**20


def inverse_sinh(value):
    return jnp.log(value + jnp.sqrt(value * value + 1.0))


def row_order():
    row = lax.broadcasted_iota(jnp.int32, (4 * ROWS, 4 * TRACE), 0)
    column = lax.broadcasted_iota(jnp.int32, (4 * ROWS, 4 * TRACE), 1)
    face = lax.shift_right_logical(row, 5)
    value = jnp.bitwise_and(row, ROWS - 1)
    return jnp.where(column == 4 * value + face, 1.0, 0.0).astype(BF16)


def make_traces(packed, ordered, table, first, tiles):
    made = jnp.dot(ordered, packed, preferred_element_type=F32).astype(BF16)
    for face in range(4):
        for tile in range(tiles):
            start = (face * TILES + first + tile) * ROWS
            table[start : start + ROWS, :] = made[face * ROWS : (face + 1) * ROWS, tile * BLOCK : (tile + 1) * BLOCK]


def order_rows(restriction):
    return lax.dot_general(
        row_order(), restriction, (((1,), (1,)), ((), ())), preferred_element_type=F32
    ).astype(BF16)


def pick(table, index, first, blocks):
    width = index.shape[1]
    low = jnp.bitwise_and(index, BLOCK - 1)
    high = jnp.broadcast_to(lax.shift_right_arithmetic(index, 8), (8, width))
    lanes = lax.broadcasted_iota(jnp.int32, (BLOCK, width), 0)
    selector = jnp.where(lanes == low, 1.0, 0.0).astype(BF16)
    product = jnp.dot(table[first * ROWS : (first + blocks) * ROWS, :], selector, preferred_element_type=F32)
    product = product.reshape(blocks, ROWS // 8, 8, width)
    picked = jnp.zeros((ROWS // 8, 8, width), F32)
    for block in range(blocks):
        here = jnp.broadcast_to((high == first + block)[None], picked.shape)
        picked = jnp.where(here, product[block], picked)
    return picked.reshape(ROWS, width)


def pick_sent(table, send_faces, plus_faces, minus_faces, sent, plus_out, minus_out, outgoing, sems):
    index = jnp.concatenate([plus_faces[...], minus_faces[...]], axis=1)
    picked = pick(table, index, 0, LOCAL).astype(BF16)
    plus_out[...] = picked[:, :SLOTS]
    minus_out[...] = picked[:, SLOTS:]

    def body(turn, carry):
        start = pl.multiple_of(turn * 8, 8)
        faces = send_faces[pl.ds(start, 8), :]
        for pair in range(4):
            index = jnp.concatenate([faces[2 * pair : 2 * pair + 1], faces[2 * pair + 1 : 2 * pair + 2]], axis=1)
            picked = pick(table, index, 0, LOCAL).astype(BF16)
            outgoing[start + 2 * pair] = picked[:, :SLOTS]
            outgoing[start + 2 * pair + 1] = picked[:, SLOTS:]
        part = pl.ds(start, 8)
        pltpu.make_async_copy(outgoing.at[part], sent.at[part], sems.at[turn]).start()
        return carry

    lax.fori_loop(0, PEERS // 8, body, 0)
    for turn in range(PEERS // 8):
        part = slice(turn * 8, turn * 8 + 8)
        pltpu.make_async_copy(outgoing.at[part], sent.at[part], sems.at[turn]).wait()


def friction(difference, stress, state, to_points, to_nodes, jump):
    weights = [jnp.broadcast_to(to_points[:, n : n + 1], stress.shape) for n in range(NODES)]
    at_points = []
    for component in range(3):
        total = weights[0] * difference[component * NODES : component * NODES + 1]
        for n in range(1, NODES):
            row = component * NODES + n
            total = total + weights[n] * difference[row : row + 1]
        at_points.append(total)
    magnitude = jnp.sqrt(at_points[1] * at_points[1] + at_points[2] * at_points[2] + REGULARIZE)
    rate_scale = 0.5 * jnp.exp(state)
    slip_rate = jnp.zeros_like(magnitude)
    for _ in range(NEWTON):
        scaled_rate = slip_rate * rate_scale
        residual_value = IMPEDANCE * (magnitude - slip_rate) - stress * FRICTION_A * inverse_sinh(scaled_rate)
        derivative = IMPEDANCE + stress * FRICTION_A * rate_scale / jnp.sqrt(1.0 + scaled_rate * scaled_rate)
        slip_rate = slip_rate + residual_value / derivative
    share = slip_rate / magnitude
    point_jump = [at_points[0], at_points[1] * share, at_points[2] * share]
    columns = [jnp.broadcast_to(to_nodes[:, q : q + 1], (NODES, stress.shape[1])) for q in range(POINTS)]
    for component in range(3):
        total = columns[0] * point_jump[component][0:1]
        for q in range(1, POINTS):
            total = total + columns[q] * point_jump[component][q : q + 1]
        jump[component * NODES : (component + 1) * NODES, :] = total
    return slip_rate


def first_kernel(
    element_state, send_faces, plus_faces, minus_faces, stress, state_variable, fault_count, restriction,
    sent, constants, plus_out, minus_out, table,
    state_here, send_here, plus_here, minus_here, restriction_here, outgoing, in_sems, out_sems,
):
    small = [
        (restriction, restriction_here),
        (plus_faces, plus_here),
        (minus_faces, minus_here),
        (send_faces, send_here),
        (stress, constants.at[0:POINTS, :]),
        (state_variable, constants.at[POINTS : 2 * POINTS, :]),
    ]
    copies = [pltpu.make_async_copy(here, there, in_sems.at[i]) for i, (here, there) in enumerate(small)]
    width = ELEMS // PARTS
    for part in range(PARTS):
        columns = slice(part * width, (part + 1) * width)
        copies.append(
            pltpu.make_async_copy(
                element_state.at[:, columns], state_here.at[:, columns], in_sems.at[len(small) + part]
            )
        )
    for copy in copies:
        copy.start()
    constants[2 * POINTS :, :] = jnp.full((8, SLOTS), fault_count[0], jnp.int32).astype(F32)
    copies[0].wait()
    ordered = order_rows(restriction_here[...])
    for part in range(PARTS):
        copies[len(small) + part].wait()
        packed = state_here[:, part * width : (part + 1) * width].astype(BF16)
        make_traces(packed, ordered, table, part * TILES // PARTS, TILES // PARTS)
    for copy in copies[1 : len(small)]:
        copy.wait()
    pick_sent(table, send_here, plus_here, minus_here, sent, plus_out, minus_out, outgoing, out_sems)


def local_kernel(
    element_state, table, face_source, geometry, volume_ops, base, difference,
):
    state = element_state[...]
    packed = state.astype(BF16)
    operators = volume_ops[...].astype(F32)
    change = None
    for direction in range(3):
        operator = operators[direction * VALUES : (direction + 1) * VALUES].astype(BF16)
        term = jnp.dot(operator, packed, preferred_element_type=F32) * geometry[direction : direction + 1, :]
        change = term if change is None else change + term
    base[...] = state + TIME_STEP * change

    def body(face, carry):
        rows = pl.ds(pl.multiple_of(face * ROWS, ROWS), ROWS)
        for tile in range(TILES):
            columns = slice(tile * BLOCK, (tile + 1) * BLOCK)
            own = table[pl.ds(pl.multiple_of((face * TILES + tile) * ROWS, ROWS), ROWS), :].astype(F32)
            difference[rows, columns] = own - pick(table, face_source[pl.ds(face, 1), columns], 0, LOCAL)
        return carry

    lax.fori_loop(0, 4, body, 0)


def step_kernel(
    last, base, difference, received, partner, next_plus, next_constants, face_source, send_faces, plus_faces,
    minus_faces, own_plus, own_minus, fault_count, stress, state_variable, face_area, restriction, lift_operator,
    to_points, to_nodes, *rest,
):
    if last:
        state_out, slip_out, arrived, jump, masked, override, scaled, state_here, out_sems = rest
    else:
        state_out, sent, plus_out, minus_out, table, arrived, jump, masked, override, scaled, outgoing, out_sems = rest
    for block in range(REMOTE):
        arrived[block * ROWS : (block + 1) * ROWS, :] = jnp.concatenate(
            [received[2 * block], received[2 * block + 1]], axis=1
        )

    plus_side = jnp.concatenate([own_plus[...].astype(F32), next_plus[...].astype(F32)], axis=1)
    minus_side = jnp.concatenate([partner[...].astype(F32), own_minus[...].astype(F32)], axis=1)
    both_stress = jnp.concatenate([stress[...], next_constants[0:POINTS, :]], axis=1)
    both_state = jnp.concatenate([state_variable[...], next_constants[POINTS : 2 * POINTS, :]], axis=1)
    slip_rate = friction(plus_side - minus_side, both_stress, both_state, to_points[...], to_nodes[...], jump)
    slot = lax.broadcasted_iota(jnp.int32, (1, SLOTS), 1)
    own_live = slot < fault_count[0]
    next_live = slot.astype(F32) < next_constants[2 * POINTS : 2 * POINTS + 1, :]
    sign = jnp.concatenate([jnp.where(own_live, 1.0, 0.0), jnp.where(next_live, -1.0, 0.0)], axis=1)
    if last:
        slip_out[...] = jnp.where(own_live, slip_rate[:, :SLOTS], 0.0)

    row = lax.broadcasted_iota(jnp.int32, (ROWS, FAULTS), 0)
    jump[TRACE : TRACE + 2, :] = jnp.zeros((2, FAULTS), F32)
    values = jnp.where(row < TRACE, jump[...] * sign, jnp.where(row == TRACE, jnp.abs(sign), 0.0))
    coarse = values.astype(BF16).astype(F32)
    parts = jnp.concatenate([coarse, values - coarse], axis=0)
    faces = jnp.concatenate([plus_faces[...], minus_faces[...]], axis=1)
    high = jnp.broadcast_to(lax.shift_right_logical(faces, 8), parts.shape)
    for block in range(LOCAL):
        masked[block * 2 * ROWS : (block + 1) * 2 * ROWS, :] = jnp.where(high == block, parts, 0.0).astype(BF16)
    lanes = lax.broadcasted_iota(jnp.int32, (BLOCK, FAULTS), 0)
    selector = jnp.where(lanes == jnp.bitwise_and(faces, BLOCK - 1), 1.0, 0.0).astype(BF16)
    override[...] = lax.dot_general(masked[...], selector, (((1,), (1,)), ((), ())), preferred_element_type=F32)

    def body(face, carry):
        rows = pl.ds(pl.multiple_of(face * ROWS, ROWS), ROWS)
        for tile in range(TILES):
            columns = slice(tile * BLOCK, (tile + 1) * BLOCK)
            exterior = pick(arrived, face_source[pl.ds(face, 1), columns] - 4 * ELEMS, 0, REMOTE)
            start = (face * TILES + tile) * 2 * ROWS
            changed = (
                override[pl.ds(pl.multiple_of(start, ROWS), ROWS), :]
                + override[pl.ds(pl.multiple_of(start + ROWS, ROWS), ROWS), :]
            )
            plain = difference[rows, columns] - exterior
            face_jump = jnp.where(changed[TRACE : TRACE + 1] > 0.5, changed, plain)
            scaled[rows, columns] = (face_jump * face_area[pl.ds(face, 1), columns]).astype(BF16)
        return carry

    lax.fori_loop(0, 4, body, 0)

    lift = lax.dot_general(
        lift_operator[...], row_order(), (((1,), (1,)), ((), ())), preferred_element_type=F32
    ).astype(BF16)
    if not last:
        state = base[...] - TIME_STEP * jnp.dot(lift, scaled[...], preferred_element_type=F32)
        state_out[...] = state
        make_traces(state.astype(BF16), order_rows(restriction[...]), table, 0, TILES)
        pick_sent(table, send_faces, plus_faces, minus_faces, sent, plus_out, minus_out, outgoing, out_sems)
        return
    width = ELEMS // PARTS
    copies = []
    for part in range(PARTS):
        columns = slice(part * width, (part + 1) * width)
        lifted = jnp.dot(lift, scaled[:, columns], preferred_element_type=F32)
        state_here[:, columns] = base[:, columns] - TIME_STEP * lifted
        copies.append(pltpu.make_async_copy(state_here.at[:, columns], state_out.at[:, columns], out_sems.at[part]))
        copies[-1].start()
    for copy in copies:
        copy.wait()


VMEM = pl.BlockSpec(memory_space=pltpu.VMEM)
SMEM = pl.BlockSpec(memory_space=pltpu.SMEM)
ANY = pl.BlockSpec(memory_space=pl.ANY)


def call(kernel, name, args, specs, outs, out_specs, scratch, flops):
    return pl.pallas_call(
        kernel,
        out_shape=[jax.ShapeDtypeStruct(shape, dtype) for shape, dtype in outs],
        in_specs=specs,
        out_specs=out_specs,
        scratch_shapes=scratch,
        compiler_params=pltpu.CompilerParams(vmem_limit_bytes=VMEM_LIMIT),
        cost_estimate=pl.CostEstimate(flops=flops, bytes_accessed=4 * 2**20, transcendentals=0),
        name=name,
    )(*args)


def shards(
    element_state,
    face_source,
    send_faces,
    plus_faces,
    minus_faces,
    fault_count,
    normal_stress,
    state_variable,
    geometry,
    face_area,
    restriction,
    volume_ops,
    lift_operator,
    to_points,
    to_nodes,
):
    segments = lax.axis_size("seg")
    up = [(s, (s + 1) % segments) for s in range(segments)]
    down = [(s, (s - 1) % segments) for s in range(segments)]
    plus_faces = plus_faces.reshape(1, SLOTS)
    minus_faces = minus_faces.reshape(1, SLOTS)
    restriction = restriction.T
    side = ((ROWS, SLOTS), BF16)
    sent_shape = ((PEERS, ROWS, SLOTS), BF16)
    table_shape = ((LOCAL * ROWS, BLOCK), BF16)
    state_shape = (element_state.shape, F32)
    sent, constants, plus, minus, table = call(
        first_kernel,
        "first",
        (element_state, send_faces, plus_faces, minus_faces, normal_stress, state_variable, fault_count, restriction),
        [ANY] * 6 + [SMEM, ANY],
        [sent_shape, ((2 * POINTS + 8, SLOTS), F32), side, side, table_shape],
        [ANY] + [VMEM] * 4,
        [
            pltpu.VMEM(element_state.shape, F32),
            pltpu.VMEM(send_faces.shape, jnp.int32),
            pltpu.VMEM(plus_faces.shape, jnp.int32),
            pltpu.VMEM(minus_faces.shape, jnp.int32),
            pltpu.VMEM(restriction.shape, BF16),
            pltpu.VMEM(*sent_shape),
            pltpu.SemaphoreType.DMA((6 + PARTS,)),
            pltpu.SemaphoreType.DMA((PEERS // 8,)),
        ],
        2 * 10**9,
    )
    next_constants = lax.ppermute(constants, "seg", down)
    for step in range(STEPS):
        last = step == STEPS - 1
        received = lax.all_to_all(sent, "dom", 0, 0, tiled=True)
        partner = lax.ppermute(minus, "seg", up)
        next_plus = lax.ppermute(plus, "seg", down)
        base, difference = call(
            local_kernel,
            "local",
            (element_state, table, face_source, geometry, volume_ops),
            [VMEM] * 5,
            [state_shape, ((4 * ROWS, ELEMS), F32)],
            [VMEM] * 2,
            [],
            4 * 10**9,
        )
        args = (
            base, difference, received, partner, next_plus, next_constants, face_source, send_faces, plus_faces,
            minus_faces, plus, minus, fault_count, normal_stress, state_variable, face_area, restriction,
            lift_operator, to_points, to_nodes,
        )
        specs = [SMEM if arg is fault_count else VMEM for arg in args]
        scratch = [
            pltpu.VMEM((REMOTE * ROWS, BLOCK), BF16),
            pltpu.VMEM((ROWS, FAULTS), F32),
            pltpu.VMEM((LOCAL * 2 * ROWS, FAULTS), BF16),
            pltpu.VMEM((LOCAL * 2 * ROWS, BLOCK), F32),
            pltpu.VMEM((4 * ROWS, ELEMS), BF16),
        ]
        kernel = functools.partial(step_kernel, last)
        if last:
            scratch += [pltpu.VMEM(*state_shape), pltpu.SemaphoreType.DMA((PARTS,))]
            outs = [state_shape, (normal_stress.shape, F32)]
            return tuple(call(kernel, "last", args, specs, outs, [ANY, VMEM], scratch, 4 * 10**9))
        scratch += [pltpu.VMEM(*sent_shape), pltpu.SemaphoreType.DMA((PEERS // 8,))]
        outs = [state_shape, sent_shape, side, side, table_shape]
        element_state, sent, plus, minus, table = call(
            kernel, "step", args, specs, outs, [VMEM, ANY, VMEM, VMEM, VMEM], scratch, 4 * 10**9
        )


def solution(mesh):
    placed = (
        P(None, ("seg", "dom")),
        P(None, ("seg", "dom")),
        P(None, ("seg", "dom")),
        P(("seg", "dom")),
        P(("seg", "dom")),
        P(("seg", "dom")),
        P(None, ("seg", "dom")),
        P(None, ("seg", "dom")),
        P(None, ("seg", "dom")),
        P(None, ("seg", "dom")),
        P(),
        P(),
        P(),
        P(),
        P(),
    )
    return jax.shard_map(
        shards,
        mesh=mesh,
        in_specs=placed,
        out_specs=(P(None, ("seg", "dom")), P(None, ("seg", "dom"))),
        check_vma=False,
    )
```

time: 69.3 us -> 68.4 us (0.987); the launches traced: 68.8 us -> 67 us
  waiting for transfers between devices: 22.6 us -> 11.6 us
  local copies, waits for them, and re-layouts: 5.77 us -> 10.9 us
  Pallas kernels: 21 us -> 23.8 us
  starting transfers between devices: 17.8 us -> 19.1 us
    all_to_all x2, waiting for transfers between devices: 18.8 us -> 11.5 us  [shards(): received = lax.all_to_all(sent, 'dom', 0, 0, tiled=True)]
    unnamed x40 -> x55, local copies, waits for them, and re-layouts: 5.77 us -> 10.9 us
    ppermute x2, waiting for transfers between devices: 3.76 us -> 0.01 us  [shards(): partner = lax.ppermute(minus, 'seg', up)]
    pallas_call x3 -> x5, Pallas kernels: 21 us -> 23.8 us  [call(): pl.pallas_call(kernel, out_shape=[jax.ShapeDtypeStruct(shape, dtype) for...]
    ppermute x2, starting transfers between devices: 1.75 us -> 3.47 us  [shards(): next_plus = lax.ppermute(plus, 'seg', down)]
  transfers between devices with their start and end apart: 6 -> 7, of which waited for: 4 -> 2; matrix products, arithmetic and copies ran while one was open for 0% -> 0% of each run, Pallas kernels for 0% -> 11%
where the time goes in v2:
time: 68.4 us; the launch traced here: 67 us
  Pallas kernels  23.8 us (35%)
  starting transfers between devices  19.1 us (28%)
  waiting for transfers between devices  11.6 us (17%)
  local copies, waits for them, and re-layouts  10.9 us (16%)
  between operations  1.58 us (2%)
    pallas_call x5, Pallas kernels, call(): pl.pallas_call(kernel, out_shape=[jax.ShapeDtypeStruct(shape, dtype) for...  23.8 us
    all_to_all x2, starting transfers between devices, shards(): received = lax.all_to_all(sent, 'dom', 0, 0, tiled=True)  15.6 us
    all_to_all x2, waiting for transfers between devices, shards(): received = lax.all_to_all(sent, 'dom', 0, 0, tiled=True)  11.5 us
    unnamed x55, local copies, waits for them, and re-layouts  10.9 us
    ppermute x2, starting transfers between devices, shards(): next_plus = lax.ppermute(plus, 'seg', down)  3.47 us
  transfers between devices with their start and end apart: 7, of which 2 were waited for; matrix products, arithmetic and copies ran while one was open for 0% of the time, Pallas kernels for 11%

profile of v2, /device:TPU:6, one launch (start us, length us, event | category | flops | bytes accessed | tf_op | source)
XLA Modules:
  0.0 67.0 jit_solution(4730152780133482105)
XLA Ops:
  1.3 0.0 copy-start
  1.3 1.2 %copy-done = f32[180,1536]{1,0:T(8,128)S(1)} copy-done((f32[180,1536]{1,0:T(8,128)S(1)}, f32[180,1536]{1,0:T(8,128)}, u32[]{:S(2)}) %copy-start) | copy-done | bytes 1105944
  2.5 0.8 %copy-done.2 = bf16[120,180]{0,1:T(8,128)(2,1)S(1)} copy-done((bf16[120,180]{0,1:T(8,128)(2,1)S(1)}, bf16[120,180]{0,1:T(8,128)(2,1)}, u32[]{:S(2)}) %copy-start.2) | copy-done | bytes 43224
  3.3 0.7 %copy-done.8 = s32[32,128]{1,0:T(8,128)S(1)} copy-done((s32[32,128]{1,0:T(8,128)S(1)}, s32[32,128]{1,0:T(8,128)}, u32[]{:S(2)}) %copy-start.8) | copy-done | bytes 16408
  4.0 0.7 %copy-done.10 = f32[16,128]{1,0:T(8,128)S(1)} copy-done((f32[16,128]{1,0:T(8,128)S(1)}, f32[16,128]{1,0:T(8,128)}, u32[]{:S(2)}) %copy-start.10) | copy-done | bytes 8216
  4.7 0.7 %copy-done.12 = f32[16,128]{1,0:T(8,128)S(1)} copy-done((f32[16,128]{1,0:T(8,128)S(1)}, f32[16,128]{1,0:T(8,128)}, u32[]{:S(2)}) %copy-start.12) | copy-done | bytes 8216
  5.4 0.7 copy-done.16
  6.1 0.7 copy-done.18
  6.8 4.3 %first.1 = (bf16[32,32,128]{2,1,0:T(8,128)(2,1)}, f32[40,128]{1,0:T(8,128)S(1)}, bf16[32,128]{1,0:T(8,128)(2,1)S(1)}, bf16[32,128]{1,0:T(8,128)(2,1)S(1)}, bf16[768,256]{1,0:T(8,128)(2,1)S(1)}) custom-call(f32[180,1536]{1,0:T(8,128)S(1)} %copy-done, s32[32,128]{1,0:T(8,128)S(1)} %copy-done.8, s32[1,128]{1,0:T(1,128)S(1)} %bitcast.6, s32[1,128]{1,0:T(1,128)S(1)} %bitcast.9, ...), custom_call_target="tpu_custom_call" | custom-call | flops 2000000000 | bytes 4194304 | tf_op jit(solution)/shard_map/first/pallas_call | solution.py:273
  11.1 11.5 %all-to-all-start = ((bf16[32,32,128]{2,1,0:T(8,128)(2,1)}), bf16[32,32,128]{2,1,0:T(8,128)(2,1)S(1)}, u32[]{:S(2)}, u32[]{:S(2)}) async-start(bf16[32,32,128]{2,1,0:T(8,128)(2,1)} %get-tuple-element.19), calls=%async_computation | async-start | bytes 524288 | tf_op jit(solution)/shard_map/all_to_all | solution.py:334
  22.6 0.0 collective-permute-start
  22.6 1.7 %collective-permute-start.1 = (bf16[32,128]{1,0:T(8,128)(2,1)S(1)}, bf16[32,128]{1,0:T(8,128)(2,1)S(1)}, u32[]{:S(2)}, u32[]{:S(2)}) collective-permute-start(bf16[32,128]{1,0:T(8,128)(2,1)S(1)} %get-tuple-element.21.own_plus), channel_id=1, source_target_pairs={{0,224},{32,0},{64,32},{96,64},{128,96},{160,128},{192,160},{224,1... | collective-permute-start | bytes 24584 | tf_op jit(solution)/shard_map/ppermute | solution.py:336
  24.4 0.0 collective-permute-start.2
  24.4 0.0 copy-done.26
  24.4 0.2 copy.17.volume_ops
  24.6 0.0 copy-start.3
  24.6 0.0 copy-start.4
  24.6 0.0 copy-start.7
  24.6 0.0 copy-start.9
  24.7 0.0 copy-start.11
  24.7 0.0 copy-start.13
  24.7 0.0 copy-start.14
  24.7 0.0 copy-start.15
  24.7 0.0 copy-start.17
  24.7 0.0 copy-start.19
  24.7 3.8 %local.2 = (f32[180,1536]{1,0:T(8,128)S(1)}, f32[128,1536]{1,0:T(8,128)S(1)}) custom-call(f32[180,1536]{1,0:T(8,128)S(1)} %copy-done.1, bf16[768,256]{1,0:T(8,128)(2,1)S(1)} %get-tuple-element.16.table, s32[4,1536]{1,0:T(4,128)S(1)} %copy-done.6, f32[3,1536]{1,0:T(4,128)S(1)} %copy-done.5, bf16[540,180]{1,0:T(8,128)(2,1)S(1)} %copy.17.volume_ops), custom_call_target="tpu_custom_call" | custom-call | flops 4000000000 | bytes 4194304 | tf_op jit(solution)/shard_map/local/pallas_call | solution.py:273
  28.5 0.0 copy-start.22
  28.5 0.9 %copy-done.22 = f32[128,1536]{1,0:T(8,128)} copy-done((f32[128,1536]{1,0:T(8,128)}, f32[128,1536]{1,0:T(8,128)S(1)}, u32[]{:S(2)}) %copy-start.22) | copy-done | bytes 786456
  29.4 0.0 collective-permute-done.partner
  29.4 0.0 collective-permute-done.1.next_plus
  29.4 0.0 collective-permute-done.2.next_constants
  29.4 5.9 %all-to-all-done.received = bf16[32,32,128]{2,1,0:T(8,128)(2,1)S(1)} async-done(((bf16[32,32,128]{2,1,0:T(8,128)(2,1)}), bf16[32,32,128]{2,1,0:T(8,128)(2,1)S(1)}, u32[]{:S(2)}, u32[]{:S(2)}) %all-to-all-start) | async-done | bytes 262176 | tf_op jit(solution)/shard_map/all_to_all | solution.py:334
  35.3 0.0 copy-done.3
  35.4 0.0 copy-start.23
  35.4 1.1 %copy-done.23 = f32[128,1536]{1,0:T(8,128)S(1)} copy-done((f32[128,1536]{1,0:T(8,128)S(1)}, f32[128,1536]{1,0:T(8,128)}, u32[]{:S(2)}) %copy-start.23) | copy-done | bytes 786456
  36.5 6.9 %step.1 = (f32[180,1536]{1,0:T(8,128)S(1)}, bf16[32,32,128]{2,1,0:T(8,128)(2,1)}, bf16[32,128]{1,0:T(8,128)(2,1)S(1)}, bf16[32,128]{1,0:T(8,128)(2,1)S(1)}, bf16[768,256]{1,0:T(8,128)(2,1)S(1)}) custom-call(f32[180,1536]{1,0:T(8,128)S(1)} %get-tuple-element.17.base, f32[128,1536]{1,0:T(8,128)S(1)} %copy-done.23, ...), custom_call_target="tpu_custom_call" | custom-call | flops 4000000000 | bytes 4194304 | tf_op jit(solution)/shard_map/step/pallas_call | solution.py:273
  43.4 0.0 copy-start.20
  43.5 1.0 %copy-done.20 = f32[180,1536]{1,0:T(8,128)} copy-done((f32[180,1536]{1,0:T(8,128)}, f32[180,1536]{1,0:T(8,128)S(1)}, u32[]{:S(2)}) %copy-start.20) | copy-done | bytes 1105944
  44.4 4.1 %all-to-all-start.1 = ((bf16[32,32,128]{2,1,0:T(8,128)(2,1)}), bf16[32,32,128]{2,1,0:T(8,128)(2,1)S(1)}, u32[]{:S(2)}, u32[]{:S(2)}) async-start(bf16[32,32,128]{2,1,0:T(8,128)(2,1)} %get-tuple-element.27), calls=%async_computation.1 | async-start | bytes 524288 | tf_op jit(solution)/shard_map/all_to_all | solution.py:334
  48.6 0.0 collective-permute-start.3
  48.6 1.7 %collective-permute-start.4 = (bf16[32,128]{1,0:T(8,128)(2,1)S(1)}, bf16[32,128]{1,0:T(8,128)(2,1)S(1)}, u32[]{:S(2)}, u32[]{:S(2)}) collective-permute-start(bf16[32,128]{1,0:T(8,128)(2,1)S(1)} %get-tuple-element.29.own_plus), channel_id=1, source_target_pairs={{0,224},{32,0},{64,32},{96,64},{128,96},{160,128},{192,160},{224,1... | collective-permute-start | bytes 24584 | tf_op jit(solution)/shard_map/ppermute | solution.py:336
  50.3 1.3 %copy-done.21 = f32[180,1536]{1,0:T(8,128)S(1)} copy-done((f32[180,1536]{1,0:T(8,128)S(1)}, f32[180,1536]{1,0:T(8,128)}, u32[]{:S(2)}) %copy-start.21) | copy-done | bytes 1105944
  51.6 1.0 %copy-done.25 = bf16[768,256]{1,0:T(8,128)(2,1)S(1)} copy-done((bf16[768,256]{1,0:T(8,128)(2,1)S(1)}, bf16[768,256]{1,0:T(8,128)(2,1)}, u32[]{:S(2)}) %copy-start.25) | copy-done | bytes 393240
  52.6 3.8 %local.3 = (f32[180,1536]{1,0:T(8,128)S(1)}, f32[128,1536]{1,0:T(8,128)S(1)}) custom-call(f32[180,1536]{1,0:T(8,128)S(1)} %copy-done.21, bf16[768,256]{1,0:T(8,128)(2,1)S(1)} %copy-done.25, s32[4,1536]{1,0:T(4,128)S(1)} %copy-done.6, f32[3,1536]{1,0:T(4,128)S(1)} %copy-done.5, bf16[540,180]{1,0:T(8,128)(2,1)S(1)} %copy.17.volume_ops), custom_call_target="tpu_custom_call" | custom-call | flops 4000000000 | bytes 4194304 | tf_op jit(solution)/shard_map/local/pallas_call | solution.py:273
  56.4 0.0 collective-permute-done.3.partner
  56.4 0.0 collective-permute-done.4.next_plus
  56.4 5.7 %all-to-all-done.1.received = bf16[32,32,128]{2,1,0:T(8,128)(2,1)S(1)} async-done(((bf16[32,32,128]{2,1,0:T(8,128)(2,1)}), bf16[32,32,128]{2,1,0:T(8,128)(2,1)S(1)}, u32[]{:S(2)}, u32[]{:S(2)}) %all-to-all-start.1) | async-done | bytes 262176 | tf_op jit(solution)/shard_map/all_to_all | solution.py:334
  62.0 5.0 %last.1 = (f32[180,1536]{1,0:T(8,128)}, f32[16,128]{1,0:T(8,128)}) custom-call(f32[180,1536]{1,0:T(8,128)S(1)} %get-tuple-element.25.base, f32[128,1536]{1,0:T(8,128)S(1)} %get-tuple-element.26.difference, bf16[32,32,128]{2,1,0:T(8,128)(2,1)S(1)} %all-to-all-done.1.received, bf16[32,128]{1,0:T(8,128)(2,1)S(1)} %collective-permute-done.3.partner, ...), custom_call_target="tpu_custom_call" | custom-call | flops 4000000000 | bytes 4194304 | tf_op jit(solution)/shard_map/last/pallas_call | solution.py:273
  (26 shorter events, 0.0 us)
Async XLA Ops:
  1.3 1.3 %copy-start = (f32[180,1536]{1,0:T(8,128)S(1)}, f32[180,1536]{1,0:T(8,128)}, u32[]{:S(2)}) copy-start(f32[180,1536]{1,0:T(8,128)} %element_state.3) | copy-start | bytes 3317764
  2.5 0.8 %copy-start.2 = (bf16[120,180]{0,1:T(8,128)(2,1)S(1)}, bf16[120,180]{0,1:T(8,128)(2,1)}, u32[]{:S(2)}) copy-start(bf16[120,180]{0,1:T(8,128)(2,1)} %param.25) | copy-start | bytes 129604
  3.3 0.7 %copy-start.8 = (s32[32,128]{1,0:T(8,128)S(1)}, s32[32,128]{1,0:T(8,128)}, u32[]{:S(2)}) copy-start(s32[32,128]{1,0:T(8,128)} %send_faces.5) | copy-start | bytes 49156
  4.0 0.7 %copy-start.10 = (f32[16,128]{1,0:T(8,128)S(1)}, f32[16,128]{1,0:T(8,128)}, u32[]{:S(2)}) copy-start(f32[16,128]{1,0:T(8,128)} %stress.5) | copy-start | bytes 24580
  4.7 0.7 %copy-start.12 = (f32[16,128]{1,0:T(8,128)S(1)}, f32[16,128]{1,0:T(8,128)}, u32[]{:S(2)}) copy-start(f32[16,128]{1,0:T(8,128)} %state_variable.5) | copy-start | bytes 24580
  5.4 0.7 copy-start.16
  6.1 0.7 copy-start.18
  6.7 17.7 %copy-start.26 = (bf16[540,180]{0,1:T(8,128)(2,1)S(1)}, bf16[540,180]{0,1:T(8,128)(2,1)}, u32[]{:S(2)}) copy-start(bf16[540,180]{0,1:T(8,128)(2,1)} %param.26) | copy-start | bytes 583204
  6.8 17.8 %copy-start.1 = (f32[180,1536]{1,0:T(8,128)S(1)}, f32[180,1536]{1,0:T(8,128)}, u32[]{:S(2)}) copy-start(f32[180,1536]{1,0:T(8,128)} %element_state.3) | copy-start | bytes 3317764
  6.8 17.8 %copy-start.5 = (f32[3,1536]{1,0:T(4,128)S(1)}, f32[3,1536]{1,0:T(4,128)}, u32[]{:S(2)}) copy-start(f32[3,1536]{1,0:T(4,128)} %geometry.3) | copy-start | bytes 55300
  6.8 17.8 %copy-start.6 = (s32[4,1536]{1,0:T(4,128)S(1)}, s32[4,1536]{1,0:T(4,128)}, u32[]{:S(2)}) copy-start(s32[4,1536]{1,0:T(4,128)} %face_source.7) | copy-start | bytes 73732
  11.1 24.2 %all-to-all-start = ((bf16[32,32,128]{2,1,0:T(8,128)(2,1)}), bf16[32,32,128]{2,1,0:T(8,128)(2,1)S(1)}, u32[]{:S(2)}, u32[]{:S(2)}) async-start(bf16[32,32,128]{2,1,0:T(8,128)(2,1)} %get-tuple-element.19), calls=%async_computation | async-start | bytes 524288 | tf_op jit(solution)/shard_map/all_to_all | solution.py:334
  22.6 6.8 %collective-permute-start = (bf16[32,128]{1,0:T(8,128)(2,1)S(1)}, bf16[32,128]{1,0:T(8,128)(2,1)S(1)}, u32[]{:S(2)}, u32[]{:S(2)}) collective-permute-start(bf16[32,128]{1,0:T(8,128)(2,1)S(1)} %get-tuple-element.20.own_minus), channel_id=1, source_target_pairs={{0,32},{32,64},{64,96},{96,128},{128,160},{160,192},{192,224},{224... | collective-permute-start | bytes 24584 | tf_op jit(solution)/shard_map/ppermute | solution.py:335
  22.6 6.8 %collective-permute-start.1 = (bf16[32,128]{1,0:T(8,128)(2,1)S(1)}, bf16[32,128]{1,0:T(8,128)(2,1)S(1)}, u32[]{:S(2)}, u32[]{:S(2)}) collective-permute-start(bf16[32,128]{1,0:T(8,128)(2,1)S(1)} %get-tuple-element.21.own_plus), channel_id=1, source_target_pairs={{0,224},{32,0},{64,32},{96,64},{128,96},{160,128},{192,160},{224,1... | collective-permute-start | bytes 24584 | tf_op jit(solution)/shard_map/ppermute | solution.py:336
  24.4 5.0 %collective-permute-start.2 = (f32[40,128]{1,0:T(8,128)S(1)}, f32[40,128]{1,0:T(8,128)S(1)}, u32[]{:S(2)}, u32[]{:S(2)}) collective-permute-start(f32[40,128]{1,0:T(8,128)S(1)} %get-tuple-element.22), channel_id=1, source_target_pairs={{0,224},{32,0},{64,32},{96,64},{128,96},{160,128},{192,160},{224,1... | collective-permute-start | bytes 61448 | tf_op jit(solution)/shard_map/ppermute | solution.py:331
  24.6 10.7 %copy-start.3 = (bf16[120,180]{0,1:T(8,128)(2,1)S(1)}, bf16[120,180]{0,1:T(8,128)(2,1)}, u32[]{:S(2)}) copy-start(bf16[120,180]{0,1:T(8,128)(2,1)} %param.25) | copy-start | bytes 129604
  24.6 10.7 %copy-start.4 = (bf16[180,120]{1,0:T(8,128)(2,1)S(1)}, bf16[180,120]{1,0:T(8,128)(2,1)}, u32[]{:S(2)}) copy-start(bf16[180,120]{1,0:T(8,128)(2,1)} %lift_operator.3) | copy-start | bytes 129604
  24.6 10.7 %copy-start.7 = (f32[4,1536]{1,0:T(4,128)S(1)}, f32[4,1536]{1,0:T(4,128)}, u32[]{:S(2)}) copy-start(f32[4,1536]{1,0:T(4,128)} %face_area.3) | copy-start | bytes 73732
  24.6 10.7 %copy-start.9 = (s32[32,128]{1,0:T(8,128)S(1)}, s32[32,128]{1,0:T(8,128)}, u32[]{:S(2)}) copy-start(s32[32,128]{1,0:T(8,128)} %send_faces.5) | copy-start | bytes 49156
  24.7 10.7 %copy-start.11 = (f32[16,128]{1,0:T(8,128)S(1)}, f32[16,128]{1,0:T(8,128)}, u32[]{:S(2)}) copy-start(f32[16,128]{1,0:T(8,128)} %stress.5) | copy-start | bytes 24580
  24.7 10.7 %copy-start.13 = (f32[16,128]{1,0:T(8,128)S(1)}, f32[16,128]{1,0:T(8,128)}, u32[]{:S(2)}) copy-start(f32[16,128]{1,0:T(8,128)} %state_variable.5) | copy-start | bytes 24580
  24.7 10.7 %copy-start.14 = (f32[16,10]{1,0:T(8,128)S(1)}, f32[16,10]{1,0:T(8,128)}, u32[]{:S(2)}) copy-start(f32[16,10]{1,0:T(8,128)} %to_points.3) | copy-start | bytes 1924
  24.7 10.7 %copy-start.15 = (f32[10,16]{1,0:T(8,128)S(1)}, f32[10,16]{1,0:T(8,128)}, u32[]{:S(2)}) copy-start(f32[10,16]{1,0:T(8,128)} %to_nodes.3) | copy-start | bytes 1924
  24.7 10.7 %copy-start.17 = (s32[128]{0:T(128)S(1)}, s32[128]{0:T(128)}, u32[]{:S(2)}) copy-start(s32[128]{0:T(128)} %param.18) | copy-start | bytes 1540
  24.7 10.7 %copy-start.19 = (s32[128]{0:T(128)S(1)}, s32[128]{0:T(128)}, u32[]{:S(2)}) copy-start(s32[128]{0:T(128)} %param.19) | copy-start | bytes 1540
  28.5 0.9 %copy-start.22 = (f32[128,1536]{1,0:T(8,128)}, f32[128,1536]{1,0:T(8,128)S(1)}, u32[]{:S(2)}) copy-start(f32[128,1536]{1,0:T(8,128)S(1)} %get-tuple-element.18.difference) | copy-start | bytes 2359300
  35.4 1.1 %copy-start.23 = (f32[128,1536]{1,0:T(8,128)S(1)}, f32[128,1536]{1,0:T(8,128)}, u32[]{:S(2)}) copy-start(f32[128,1536]{1,0:T(8,128)} %copy-done.22) | copy-start | bytes 2359300
  43.4 1.0 %copy-start.20 = (f32[180,1536]{1,0:T(8,128)}, f32[180,1536]{1,0:T(8,128)S(1)}, u32[]{:S(2)}) copy-start(f32[180,1536]{1,0:T(8,128)S(1)} %get-tuple-element.23.element_state) | copy-start | bytes 3317764
  44.4 5.9 %copy-start.24 = (bf16[768,256]{1,0:T(8,128)(2,1)}, bf16[768,256]{1,0:T(8,128)(2,1)S(1)}, u32[]{:S(2)}) copy-start(bf16[768,256]{1,0:T(8,128)(2,1)S(1)} %get-tuple-element.24.table) | copy-start | bytes 1179652
  44.4 17.6 %all-to-all-start.1 = ((bf16[32,32,128]{2,1,0:T(8,128)(2,1)}), bf16[32,32,128]{2,1,0:T(8,128)(2,1)S(1)}, u32[]{:S(2)}, u32[]{:S(2)}) async-start(bf16[32,32,128]{2,1,0:T(8,128)(2,1)} %get-tuple-element.27), calls=%async_computation.1 | async-start | bytes 524288 | tf_op jit(solution)/shard_map/all_to_all | solution.py:334
  48.6 7.8 %collective-permute-start.3 = (bf16[32,128]{1,0:T(8,128)(2,1)S(1)}, bf16[32,128]{1,0:T(8,128)(2,1)S(1)}, u32[]{:S(2)}, u32[]{:S(2)}) collective-permute-start(bf16[32,128]{1,0:T(8,128)(2,1)S(1)} %get-tuple-element.28.own_minus), channel_id=1, source_target_pairs={{0,32},{32,64},{64,96},{96,128},{128,160},{160,192},{192,224},{224... | collective-permute-start | bytes 24584 | tf_op jit(solution)/shard_map/ppermute | solution.py:335
  48.6 7.8 %collective-permute-start.4 = (bf16[32,128]{1,0:T(8,128)(2,1)S(1)}, bf16[32,128]{1,0:T(8,128)(2,1)S(1)}, u32[]{:S(2)}, u32[]{:S(2)}) collective-permute-start(bf16[32,128]{1,0:T(8,128)(2,1)S(1)} %get-tuple-element.29.own_plus), channel_id=1, source_target_pairs={{0,224},{32,0},{64,32},{96,64},{128,96},{160,128},{192,160},{224,1... | collective-permute-start | bytes 24584 | tf_op jit(solution)/shard_map/ppermute | solution.py:336
  50.3 1.3 %copy-start.21 = (f32[180,1536]{1,0:T(8,128)S(1)}, f32[180,1536]{1,0:T(8,128)}, u32[]{:S(2)}) copy-start(f32[180,1536]{1,0:T(8,128)} %copy-done.20) | copy-start | bytes 3317764
  51.6 1.0 %copy-start.25 = (bf16[768,256]{1,0:T(8,128)(2,1)S(1)}, bf16[768,256]{1,0:T(8,128)(2,1)}, u32[]{:S(2)}) copy-start(bf16[768,256]{1,0:T(8,128)(2,1)} %copy-done.24) | copy-start | bytes 1179652

commit v3 on v2

--- a/solution.py
+++ b/solution.py
@@ -31,6 +31,7 @@
 REMOTE = PEERS * SLOTS // BLOCK
 FAULTS = 2 * SLOTS
 PARTS = 3
+EARLY = 2
 VMEM_LIMIT = 32 * 2**20
 
 
@@ -54,10 +55,8 @@
             table[start : start + ROWS, :] = made[face * ROWS : (face + 1) * ROWS, tile * BLOCK : (tile + 1) * BLOCK]
 
 
-def order_rows(restriction):
-    return lax.dot_general(
-        row_order(), restriction, (((1,), (1,)), ((), ())), preferred_element_type=F32
-    ).astype(BF16)
+def order_rows(order, restriction):
+    return lax.dot_general(order, restriction, (((1,), (1,)), ((), ())), preferred_element_type=F32).astype(BF16)
 
 
 def pick(table, index, first, blocks):
@@ -75,14 +74,17 @@
     return picked.reshape(ROWS, width)
 
 
-def pick_sent(table, send_faces, plus_faces, minus_faces, sent, plus_out, minus_out, outgoing, sems):
+def pick_sent(table, send_faces, plus_faces, minus_faces, sent, sides_out, outgoing, sides, sems):
     index = jnp.concatenate([plus_faces[...], minus_faces[...]], axis=1)
     picked = pick(table, index, 0, LOCAL).astype(BF16)
-    plus_out[...] = picked[:, :SLOTS]
-    minus_out[...] = picked[:, SLOTS:]
+    copies = []
+    for i in range(2):
+        sides[i] = picked[:, i * SLOTS : (i + 1) * SLOTS]
+        copies.append(pltpu.make_async_copy(sides.at[i], sides_out[i], sems.at[PEERS // 8 + i]))
+        copies[-1].start()
 
     def body(turn, carry):
-        start = pl.multiple_of(turn * 8, 8)
+        start = turn * 8
         faces = send_faces[pl.ds(start, 8), :]
         for pair in range(4):
             index = jnp.concatenate([faces[2 * pair : 2 * pair + 1], faces[2 * pair + 1 : 2 * pair + 2]], axis=1)
@@ -93,10 +95,13 @@
         pltpu.make_async_copy(outgoing.at[part], sent.at[part], sems.at[turn]).start()
         return carry
 
-    lax.fori_loop(0, PEERS // 8, body, 0)
+    for turn in range(PEERS // 8):
+        body(turn, 0)
     for turn in range(PEERS // 8):
         part = slice(turn * 8, turn * 8 + 8)
-        pltpu.make_async_copy(outgoing.at[part], sent.at[part], sems.at[turn]).wait()
+        copies.append(pltpu.make_async_copy(outgoing.at[part], sent.at[part], sems.at[turn]))
+    for copy in copies:
+        copy.wait()
 
 
 def friction(difference, stress, state, to_points, to_nodes, jump):
@@ -127,48 +132,25 @@
     return slip_rate
 
 
+def order_kernel(order):
+    order[...] = row_order()
+
+
 def first_kernel(
-    element_state, send_faces, plus_faces, minus_faces, stress, state_variable, fault_count, restriction,
-    sent, constants, plus_out, minus_out, table,
-    state_here, send_here, plus_here, minus_here, restriction_here, outgoing, in_sems, out_sems,
+    order, element_state, send_faces, plus_faces, minus_faces, stress, state_variable, fault_count, restriction,
+    sent, constants, plus_out, minus_out, table, outgoing, sides, sems,
 ):
-    small = [
-        (restriction, restriction_here),
-        (plus_faces, plus_here),
-        (minus_faces, minus_here),
-        (send_faces, send_here),
-        (stress, constants.at[0:POINTS, :]),
-        (state_variable, constants.at[POINTS : 2 * POINTS, :]),
-    ]
-    copies = [pltpu.make_async_copy(here, there, in_sems.at[i]) for i, (here, there) in enumerate(small)]
-    width = ELEMS // PARTS
-    for part in range(PARTS):
-        columns = slice(part * width, (part + 1) * width)
-        copies.append(
-            pltpu.make_async_copy(
-                element_state.at[:, columns], state_here.at[:, columns], in_sems.at[len(small) + part]
-            )
-        )
-    for copy in copies:
-        copy.start()
+    make_traces(element_state[...].astype(BF16), order_rows(order[...], restriction[...]), table, 0, TILES)
+    constants[0:POINTS, :] = stress[...]
+    constants[POINTS : 2 * POINTS, :] = state_variable[...]
     constants[2 * POINTS :, :] = jnp.full((8, SLOTS), fault_count[0], jnp.int32).astype(F32)
-    copies[0].wait()
-    ordered = order_rows(restriction_here[...])
-    for part in range(PARTS):
-        copies[len(small) + part].wait()
-        packed = state_here[:, part * width : (part + 1) * width].astype(BF16)
-        make_traces(packed, ordered, table, part * TILES // PARTS, TILES // PARTS)
-    for copy in copies[1 : len(small)]:
-        copy.wait()
-    pick_sent(table, send_here, plus_here, minus_here, sent, plus_out, minus_out, outgoing, out_sems)
-
-
-def local_kernel(
-    element_state, table, face_source, geometry, volume_ops, base, difference,
-):
+    pick_sent(table, send_faces, plus_faces, minus_faces, sent, [plus_out, minus_out], outgoing, sides, sems)
+
+
+def early_kernel(element_state, table, face_source, geometry, volume_ops, base, difference):
     state = element_state[...]
     packed = state.astype(BF16)
-    operators = volume_ops[...].astype(F32)
+    operators = volume_ops[...].astype(F32).T
     change = None
     for direction in range(3):
         operator = operators[direction * VALUES : (direction + 1) * VALUES].astype(BF16)
@@ -177,27 +159,31 @@
     base[...] = state + TIME_STEP * change
 
     def body(face, carry):
-        rows = pl.ds(pl.multiple_of(face * ROWS, ROWS), ROWS)
+        rows = pl.ds(face * ROWS, ROWS)
         for tile in range(TILES):
             columns = slice(tile * BLOCK, (tile + 1) * BLOCK)
-            own = table[pl.ds(pl.multiple_of((face * TILES + tile) * ROWS, ROWS), ROWS), :].astype(F32)
+            own = table[pl.ds((face * TILES + tile) * ROWS, ROWS), :].astype(F32)
             difference[rows, columns] = own - pick(table, face_source[pl.ds(face, 1), columns], 0, LOCAL)
         return carry
 
-    lax.fori_loop(0, 4, body, 0)
+    for face in range(EARLY):
+        body(face, 0)
 
 
 def step_kernel(
-    last, base, difference, received, partner, next_plus, next_constants, face_source, send_faces, plus_faces,
+    last, order, base, difference, table_in, received, partner, next_plus, next_constants, face_source, send_faces, plus_faces,
     minus_faces, own_plus, own_minus, fault_count, stress, state_variable, face_area, restriction, lift_operator,
     to_points, to_nodes, *rest,
 ):
     if last:
-        state_out, slip_out, arrived, jump, masked, override, scaled, state_here, out_sems = rest
+        state_out, slip_out, table, jump, masked, override, scaled, state, out_sems = rest
     else:
-        state_out, sent, plus_out, minus_out, table, arrived, jump, masked, override, scaled, outgoing, out_sems = rest
+        state_out, sent, plus_out, minus_out, table_out = rest[:5]
+        table, jump, masked, override, scaled, outgoing, sides, own_sems = rest[5:]
+        state = state_out
+    table[0 : LOCAL * ROWS, :] = table_in[...]
     for block in range(REMOTE):
-        arrived[block * ROWS : (block + 1) * ROWS, :] = jnp.concatenate(
+        table[(LOCAL + block) * ROWS : (LOCAL + block + 1) * ROWS, :] = jnp.concatenate(
             [received[2 * block], received[2 * block + 1]], axis=1
         )
 
@@ -226,39 +212,44 @@
     selector = jnp.where(lanes == jnp.bitwise_and(faces, BLOCK - 1), 1.0, 0.0).astype(BF16)
     override[...] = lax.dot_general(masked[...], selector, (((1,), (1,)), ((), ())), preferred_element_type=F32)
 
-    def body(face, carry):
-        rows = pl.ds(pl.multiple_of(face * ROWS, ROWS), ROWS)
+    def body(early, face, carry):
+        rows = pl.ds(face * ROWS, ROWS)
         for tile in range(TILES):
             columns = slice(tile * BLOCK, (tile + 1) * BLOCK)
-            exterior = pick(arrived, face_source[pl.ds(face, 1), columns] - 4 * ELEMS, 0, REMOTE)
+            index = face_source[pl.ds(face, 1), columns]
+            if early:
+                plain = difference[rows, columns] - pick(table, index, LOCAL, REMOTE)
+            else:
+                own = table_in[pl.ds((face * TILES + tile) * ROWS, ROWS), :].astype(F32)
+                plain = own - pick(table, index, 0, LOCAL + REMOTE)
             start = (face * TILES + tile) * 2 * ROWS
             changed = (
-                override[pl.ds(pl.multiple_of(start, ROWS), ROWS), :]
-                + override[pl.ds(pl.multiple_of(start + ROWS, ROWS), ROWS), :]
+                override[pl.ds(start, ROWS), :]
+                + override[pl.ds(start + ROWS, ROWS), :]
             )
-            plain = difference[rows, columns] - exterior
             face_jump = jnp.where(changed[TRACE : TRACE + 1] > 0.5, changed, plain)
             scaled[rows, columns] = (face_jump * face_area[pl.ds(face, 1), columns]).astype(BF16)
         return carry
 
-    lax.fori_loop(0, 4, body, 0)
+    for face in range(4):
+        body(face < EARLY, face, 0)
 
     lift = lax.dot_general(
-        lift_operator[...], row_order(), (((1,), (1,)), ((), ())), preferred_element_type=F32
+        lift_operator[...], order[...], (((1,), (1,)), ((), ())), preferred_element_type=F32
     ).astype(BF16)
     if not last:
-        state = base[...] - TIME_STEP * jnp.dot(lift, scaled[...], preferred_element_type=F32)
-        state_out[...] = state
-        make_traces(state.astype(BF16), order_rows(restriction[...]), table, 0, TILES)
-        pick_sent(table, send_faces, plus_faces, minus_faces, sent, plus_out, minus_out, outgoing, out_sems)
+        state[...] = base[...] - TIME_STEP * jnp.dot(lift, scaled[...], preferred_element_type=F32)
+        make_traces(state[...].astype(BF16), order_rows(order[...], restriction[...]), table, 0, TILES)
+        table_out[...] = table[0 : LOCAL * ROWS, :]
+        pick_sent(table, send_faces, plus_faces, minus_faces, sent, [plus_out, minus_out], outgoing, sides, own_sems)
         return
     width = ELEMS // PARTS
     copies = []
     for part in range(PARTS):
         columns = slice(part * width, (part + 1) * width)
         lifted = jnp.dot(lift, scaled[:, columns], preferred_element_type=F32)
-        state_here[:, columns] = base[:, columns] - TIME_STEP * lifted
-        copies.append(pltpu.make_async_copy(state_here.at[:, columns], state_out.at[:, columns], out_sems.at[part]))
+        state[:, columns] = base[:, columns] - TIME_STEP * lifted
+        copies.append(pltpu.make_async_copy(state.at[:, columns], state_out.at[:, columns], out_sems.at[part]))
         copies[-1].start()
     for copy in copies:
         copy.wait()
@@ -266,7 +257,7 @@
 
 VMEM = pl.BlockSpec(memory_space=pltpu.VMEM)
 SMEM = pl.BlockSpec(memory_space=pltpu.SMEM)
-ANY = pl.BlockSpec(memory_space=pl.ANY)
+HBM = pl.BlockSpec(memory_space=pltpu.HBM)
 
 
 def call(kernel, name, args, specs, outs, out_specs, scratch, flops):
@@ -305,26 +296,26 @@
     plus_faces = plus_faces.reshape(1, SLOTS)
     minus_faces = minus_faces.reshape(1, SLOTS)
     restriction = restriction.T
+    volume_ops = volume_ops.T
     side = ((ROWS, SLOTS), BF16)
     sent_shape = ((PEERS, ROWS, SLOTS), BF16)
     table_shape = ((LOCAL * ROWS, BLOCK), BF16)
     state_shape = (element_state.shape, F32)
+    (order,) = call(order_kernel, "order", (), [], [((4 * ROWS, 4 * TRACE), BF16)], [VMEM], [], 4 * 10**9)
     sent, constants, plus, minus, table = call(
         first_kernel,
         "first",
-        (element_state, send_faces, plus_faces, minus_faces, normal_stress, state_variable, fault_count, restriction),
-        [ANY] * 6 + [SMEM, ANY],
+        (
+            order, element_state, send_faces, plus_faces, minus_faces, normal_stress, state_variable, fault_count,
+            restriction,
+        ),
+        [VMEM] * 7 + [SMEM, VMEM],
         [sent_shape, ((2 * POINTS + 8, SLOTS), F32), side, side, table_shape],
-        [ANY] + [VMEM] * 4,
+        [HBM, VMEM, HBM, HBM, VMEM],
         [
-            pltpu.VMEM(element_state.shape, F32),
-            pltpu.VMEM(send_faces.shape, jnp.int32),
-            pltpu.VMEM(plus_faces.shape, jnp.int32),
-            pltpu.VMEM(minus_faces.shape, jnp.int32),
-            pltpu.VMEM(restriction.shape, BF16),
             pltpu.VMEM(*sent_shape),
-            pltpu.SemaphoreType.DMA((6 + PARTS,)),
-            pltpu.SemaphoreType.DMA((PEERS // 8,)),
+            pltpu.VMEM((2, ROWS, SLOTS), BF16),
+            pltpu.SemaphoreType.DMA((PEERS // 8 + 2,)),
         ],
         2 * 10**9,
     )
@@ -335,23 +326,23 @@
         partner = lax.ppermute(minus, "seg", up)
         next_plus = lax.ppermute(plus, "seg", down)
         base, difference = call(
-            local_kernel,
-            "local",
+            early_kernel,
+            "early",
             (element_state, table, face_source, geometry, volume_ops),
             [VMEM] * 5,
-            [state_shape, ((4 * ROWS, ELEMS), F32)],
+            [state_shape, ((EARLY * ROWS, ELEMS), F32)],
             [VMEM] * 2,
             [],
-            4 * 10**9,
+            2 * 10**9,
         )
         args = (
-            base, difference, received, partner, next_plus, next_constants, face_source, send_faces, plus_faces,
+            order, base, difference, table, received, partner, next_plus, next_constants, face_source, send_faces, plus_faces,
             minus_faces, plus, minus, fault_count, normal_stress, state_variable, face_area, restriction,
             lift_operator, to_points, to_nodes,
         )
         specs = [SMEM if arg is fault_count else VMEM for arg in args]
         scratch = [
-            pltpu.VMEM((REMOTE * ROWS, BLOCK), BF16),
+            pltpu.VMEM(((LOCAL + REMOTE) * ROWS, BLOCK), BF16),
             pltpu.VMEM((ROWS, FAULTS), F32),
             pltpu.VMEM((LOCAL * 2 * ROWS, FAULTS), BF16),
             pltpu.VMEM((LOCAL * 2 * ROWS, BLOCK), F32),
@@ -361,11 +352,15 @@
         if last:
             scratch += [pltpu.VMEM(*state_shape), pltpu.SemaphoreType.DMA((PARTS,))]
             outs = [state_shape, (normal_stress.shape, F32)]
-            return tuple(call(kernel, "last", args, specs, outs, [ANY, VMEM], scratch, 4 * 10**9))
-        scratch += [pltpu.VMEM(*sent_shape), pltpu.SemaphoreType.DMA((PEERS // 8,))]
+            return tuple(call(kernel, "last", args, specs, outs, [HBM, VMEM], scratch, 4 * 10**9))
+        scratch += [
+            pltpu.VMEM(*sent_shape),
+            pltpu.VMEM((2, ROWS, SLOTS), BF16),
+            pltpu.SemaphoreType.DMA((PEERS // 8 + 2,)),
+        ]
         outs = [state_shape, sent_shape, side, side, table_shape]
         element_state, sent, plus, minus, table = call(
-            kernel, "step", args, specs, outs, [VMEM, ANY, VMEM, VMEM, VMEM], scratch, 4 * 10**9
+            kernel, "step", args, specs, outs, [VMEM, HBM, HBM, HBM, VMEM], scratch, 4 * 10**9
         )
 
 

time: 68.4 us -> 61.4 us (0.90); the launches traced: 67 us -> 61 us
  local copies, waits for them, and re-layouts: 10.9 us -> 5.5 us
  Pallas kernels: 23.8 us -> 19.2 us
  waiting for transfers between devices: 11.6 us -> 15.2 us
    unnamed x55 -> x40, local copies, waits for them, and re-layouts: 10.9 us -> 5.5 us
    pallas_call x5 -> x6, Pallas kernels: 23.8 us -> 19.2 us  [call(): pl.pallas_call(kernel, out_shape=[jax.ShapeDtypeStruct(shape, dtype) for...]
    all_to_all x2, waiting for transfers between devices: 11.5 us -> 15.2 us  [shards(): received = lax.all_to_all(sent, 'dom', 0, 0, tiled=True)]
  transfers between devices with their start and end apart: 7 -> 7, of which waited for: 2 -> 2; matrix products, arithmetic and copies ran while one was open for 0% -> 0% of each run, Pallas kernels for 11% -> 7%
where the time goes in v3:
time: 61.4 us; the launch traced here: 61 us
  starting transfers between devices  19.3 us (31%)
  Pallas kernels  19.2 us (31%)
  waiting for transfers between devices  15.2 us (25%)
  local copies, waits for them, and re-layouts  5.5 us (9%)
  between operations  1.8 us (3%)
    pallas_call x6, Pallas kernels, call(): pl.pallas_call(kernel, out_shape=[jax.ShapeDtypeStruct(shape, dtype) for...  19.2 us
    all_to_all x2, starting transfers between devices, shards(): received = lax.all_to_all(sent, 'dom', 0, 0, tiled=True)  15.8 us
    all_to_all x2, waiting for transfers between devices, shards(): received = lax.all_to_all(sent, 'dom', 0, 0, tiled=True)  15.2 us
    unnamed x40, local copies, waits for them, and re-layouts  5.5 us
    ppermute x2, starting transfers between devices, shards(): next_plus = lax.ppermute(plus, 'seg', down)  3.47 us
  transfers between devices with their start and end apart: 7, of which 2 were waited for; matrix products, arithmetic and copies ran while one was open for 0% of the time, Pallas kernels for 7%

profile of v3, /device:TPU:6, one launch (start us, length us, event | category | flops | bytes accessed | tf_op | source)
XLA Modules:
  0.0 61.0 jit_solution(8559550733203679197)
XLA Ops:
  0.6 0.0 copy-start.9
  0.6 0.0 copy-start.8
  0.7 0.0 copy-start.7
  0.7 0.0 copy-start
  0.7 0.0 copy-start.2
  0.7 0.0 copy-start.13
  0.7 0.0 copy-start.12
  1.5 0.0 copy-done.9
  1.5 0.0 copy-done.8
  1.5 0.0 copy-done.7
  1.5 0.5 copy-done
  2.0 0.0 copy-done.2
  2.0 0.0 copy-done.13
  2.0 0.0 copy-done.12
  2.0 0.0 copy-start.4
  2.0 0.0 copy-start.5
  2.0 3.1 %first.1 = (bf16[32,32,128]{2,1,0:T(8,128)(2,1)}, f32[40,128]{1,0:T(8,128)S(1)}, bf16[32,128]{1,0:T(8,128)(2,1)S(1)}, bf16[32,128]{1,0:T(8,128)(2,1)S(1)}, bf16[768,256]{1,0:T(8,128)(2,1)S(1)}) custom-call(bf16[128,120]{1,0:T(8,128)(2,1)S(1)} %order.1, f32[180,1536]{1,0:T(8,128)S(1)} %copy-done, s32[32,128]{1,0:T(8,128)S(1)} %copy-done.7, ...), custom_call_target="tpu_custom_call" | custom-call | flops 2000000000 | bytes 4194304 | tf_op jit(solution)/shard_map/first/pallas_call | solution.py:264
  5.1 0.0 copy-start.16
  5.1 11.5 %all-to-all-start = ((bf16[32,32,128]{2,1,0:T(8,128)(2,1)}), bf16[32,32,128]{2,1,0:T(8,128)(2,1)S(1)}, u32[]{:S(2)}, u32[]{:S(2)}) async-start(bf16[32,32,128]{2,1,0:T(8,128)(2,1)} %get-tuple-element.19), calls=%async_computation | async-start | bytes 524288 | tf_op jit(solution)/shard_map/all_to_all | solution.py:325
  16.6 0.0 collective-permute-start
  16.7 1.7 %collective-permute-start.1 = (bf16[32,128]{1,0:T(8,128)(2,1)S(1)}, bf16[32,128]{1,0:T(8,128)(2,1)S(1)}, u32[]{:S(2)}, u32[]{:S(2)}) collective-permute-start(bf16[32,128]{1,0:T(8,128)(2,1)S(1)} %get-tuple-element.21.own_plus), channel_id=1, source_target_pairs={{0,224},{32,0},{64,32},{96,64},{128,96},{160,128},{192,160},{224,1... | collective-permute-start | bytes 24584 | tf_op jit(solution)/shard_map/ppermute | solution.py:327
  18.4 0.0 collective-permute-start.2
  18.4 0.0 copy-done.1
  18.4 0.0 copy-start.6
  18.4 0.0 copy-start.10
  18.5 0.0 copy-start.11
  18.5 2.0 %early.2 = (f32[180,1536]{1,0:T(8,128)S(1)}, f32[64,1536]{1,0:T(8,128)S(1)}) custom-call(f32[180,1536]{1,0:T(8,128)S(1)} %copy-done, bf16[768,256]{1,0:T(8,128)(2,1)S(1)} %get-tuple-element.16.table.table_in, s32[4,1536]{1,0:T(4,128)S(1)} %copy-done.5, f32[3,1536]{1,0:T(4,128)S(1)} %copy-done.4, bf16[180,540]{1,0:T(8,128)(2,1)S(1)} %bitcast.4), custom_call_target="tpu_custom_call" | custom-call | flops 2000000000 | bytes 4194304 | tf_op jit(solution)/shard_map/early/pallas_call | solution.py:264
  20.5 0.0 copy-start.18
  20.5 0.7 %copy-done.18 = f32[64,1536]{1,0:T(8,128)} copy-done((f32[64,1536]{1,0:T(8,128)}, f32[64,1536]{1,0:T(8,128)S(1)}, u32[]{:S(2)}) %copy-start.18) | copy-done | bytes 393240
  21.3 0.0 collective-permute-done.partner
  21.3 0.0 collective-permute-done.1.next_plus
  21.3 0.0 collective-permute-done.2.next_constants
  21.3 8.0 %all-to-all-done.received = bf16[32,32,128]{2,1,0:T(8,128)(2,1)S(1)} async-done(((bf16[32,32,128]{2,1,0:T(8,128)(2,1)}), bf16[32,32,128]{2,1,0:T(8,128)(2,1)S(1)}, u32[]{:S(2)}, u32[]{:S(2)}) %all-to-all-start) | async-done | bytes 262176 | tf_op jit(solution)/shard_map/all_to_all | solution.py:325
  29.3 0.0 copy-done.6
  29.3 1.0 %copy-done.17 = bf16[768,256]{1,0:T(8,128)(2,1)S(1)} copy-done((bf16[768,256]{1,0:T(8,128)(2,1)S(1)}, bf16[768,256]{1,0:T(8,128)(2,1)}, u32[]{:S(2)}) %copy-start.17) | copy-done | bytes 393240
  30.3 1.0 %copy-done.19 = f32[64,1536]{1,0:T(8,128)S(1)} copy-done((f32[64,1536]{1,0:T(8,128)S(1)}, f32[64,1536]{1,0:T(8,128)}, u32[]{:S(2)}) %copy-start.19) | copy-done | bytes 393240
  31.3 6.6 %step.1 = (f32[180,1536]{1,0:T(8,128)S(1)}, bf16[32,32,128]{2,1,0:T(8,128)(2,1)}, bf16[32,128]{1,0:T(8,128)(2,1)S(1)}, bf16[32,128]{1,0:T(8,128)(2,1)S(1)}, bf16[768,256]{1,0:T(8,128)(2,1)S(1)}) custom-call(bf16[128,120]{1,0:T(8,128)(2,1)S(1)} %order.1, f32[180,1536]{1,0:T(8,128)S(1)} %get-tuple-element.17.base, f32[64,1536]{1,0:T(8,128)S(1)} %copy-done.19, ...), custom_call_target="tpu_custom_call" | custom-call | flops 4000000000 | bytes 4194304 | tf_op jit(solution)/shard_map/step/pallas_call | solution.py:264
  38.0 0.0 copy-start.14
  38.0 1.0 %copy-done.14 = f32[180,1536]{1,0:T(8,128)} copy-done((f32[180,1536]{1,0:T(8,128)}, f32[180,1536]{1,0:T(8,128)S(1)}, u32[]{:S(2)}) %copy-start.14) | copy-done | bytes 1105944
  39.0 4.3 %all-to-all-start.1 = ((bf16[32,32,128]{2,1,0:T(8,128)(2,1)}), bf16[32,32,128]{2,1,0:T(8,128)(2,1)S(1)}, u32[]{:S(2)}, u32[]{:S(2)}) async-start(bf16[32,32,128]{2,1,0:T(8,128)(2,1)} %get-tuple-element.27), calls=%async_computation.1 | async-start | bytes 524288 | tf_op jit(solution)/shard_map/all_to_all | solution.py:325
  43.3 0.0 collective-permute-start.3
  43.3 1.7 %collective-permute-start.4 = (bf16[32,128]{1,0:T(8,128)(2,1)S(1)}, bf16[32,128]{1,0:T(8,128)(2,1)S(1)}, u32[]{:S(2)}, u32[]{:S(2)}) collective-permute-start(bf16[32,128]{1,0:T(8,128)(2,1)S(1)} %get-tuple-element.29.own_plus), channel_id=1, source_target_pairs={{0,224},{32,0},{64,32},{96,64},{128,96},{160,128},{192,160},{224,1... | collective-permute-start | bytes 24584 | tf_op jit(solution)/shard_map/ppermute | solution.py:327
  45.0 1.3 %copy-done.15 = f32[180,1536]{1,0:T(8,128)S(1)} copy-done((f32[180,1536]{1,0:T(8,128)S(1)}, f32[180,1536]{1,0:T(8,128)}, u32[]{:S(2)}) %copy-start.15) | copy-done | bytes 1105944
  46.3 2.0 %early.3 = (f32[180,1536]{1,0:T(8,128)S(1)}, f32[64,1536]{1,0:T(8,128)S(1)}) custom-call(f32[180,1536]{1,0:T(8,128)S(1)} %copy-done.15, bf16[768,256]{1,0:T(8,128)(2,1)S(1)} %get-tuple-element.24.table.table_in, s32[4,1536]{1,0:T(4,128)S(1)} %copy-done.5, f32[3,1536]{1,0:T(4,128)S(1)} %copy-done.4, bf16[180,540]{1,0:T(8,128)(2,1)S(1)} %bitcast.5), custom_call_target="tpu_custom_call" | custom-call | flops 2000000000 | bytes 4194304 | tf_op jit(solution)/shard_map/early/pallas_call | solution.py:264
  48.3 0.0 collective-permute-done.3.partner
  48.3 0.0 collective-permute-done.4.next_plus
  48.3 7.1 %all-to-all-done.1.received = bf16[32,32,128]{2,1,0:T(8,128)(2,1)S(1)} async-done(((bf16[32,32,128]{2,1,0:T(8,128)(2,1)}), bf16[32,32,128]{2,1,0:T(8,128)(2,1)S(1)}, u32[]{:S(2)}, u32[]{:S(2)}) %all-to-all-start.1) | async-done | bytes 262176 | tf_op jit(solution)/shard_map/all_to_all | solution.py:325
  55.5 5.4 %last.1 = (f32[180,1536]{1,0:T(8,128)}, f32[16,128]{1,0:T(8,128)}) custom-call(bf16[128,120]{1,0:T(8,128)(2,1)S(1)} %order.1, f32[180,1536]{1,0:T(8,128)S(1)} %get-tuple-element.25.base, f32[64,1536]{1,0:T(8,128)S(1)} %get-tuple-element.26.difference, bf16[768,256]{1,0:T(8,128)(2,1)S(1)} %get-tuple-element.24.table.table_in, ...), custom_call_target="tpu_custom_call" | custom-call | flops 4000000000 | bytes 4194304 | tf_op jit(solution)/shard_map/last/pallas_call | solution.py:264
  (12 shorter events, 0.0 us)
Async XLA Ops:
  0.6 0.8 %copy-start.9 = (f32[16,128]{1,0:T(8,128)S(1)}, f32[16,128]{1,0:T(8,128)}, u32[]{:S(2)}) copy-start(f32[16,128]{1,0:T(8,128)} %state_variable.5) | copy-start | bytes 24580
  0.6 0.8 %copy-start.8 = (f32[16,128]{1,0:T(8,128)S(1)}, f32[16,128]{1,0:T(8,128)}, u32[]{:S(2)}) copy-start(f32[16,128]{1,0:T(8,128)} %stress.5) | copy-start | bytes 24580
  0.7 0.8 %copy-start.7 = (s32[32,128]{1,0:T(8,128)S(1)}, s32[32,128]{1,0:T(8,128)}, u32[]{:S(2)}) copy-start(s32[32,128]{1,0:T(8,128)} %send_faces.5) | copy-start | bytes 49156
  0.7 1.3 %copy-start = (f32[180,1536]{1,0:T(8,128)S(1)}, f32[180,1536]{1,0:T(8,128)}, u32[]{:S(2)}) copy-start(f32[180,1536]{1,0:T(8,128)} %element_state.3) | copy-start | bytes 3317764
  0.7 1.3 %copy-start.2 = (bf16[120,180]{0,1:T(8,128)(2,1)S(1)}, bf16[120,180]{0,1:T(8,128)(2,1)}, u32[]{:S(2)}) copy-start(bf16[120,180]{0,1:T(8,128)(2,1)} %param.25) | copy-start | bytes 129604
  0.7 1.3 %copy-start.13 = (s32[128]{0:T(128)S(1)}, s32[128]{0:T(128)}, u32[]{:S(2)}) copy-start(s32[128]{0:T(128)} %param.19) | copy-start | bytes 1540
  0.7 1.3 %copy-start.12 = (s32[128]{0:T(128)S(1)}, s32[128]{0:T(128)}, u32[]{:S(2)}) copy-start(s32[128]{0:T(128)} %param.18) | copy-start | bytes 1540
  2.0 16.5 %copy-start.1 = (bf16[540,180]{0,1:T(8,128)(2,1)S(1)}, bf16[540,180]{0,1:T(8,128)(2,1)}, u32[]{:S(2)}) copy-start(bf16[540,180]{0,1:T(8,128)(2,1)} %param.26) | copy-start | bytes 583204
  2.0 16.5 %copy-start.4 = (f32[3,1536]{1,0:T(4,128)S(1)}, f32[3,1536]{1,0:T(4,128)}, u32[]{:S(2)}) copy-start(f32[3,1536]{1,0:T(4,128)} %geometry.3) | copy-start | bytes 55300
  2.0 16.4 %copy-start.5 = (s32[4,1536]{1,0:T(4,128)S(1)}, s32[4,1536]{1,0:T(4,128)}, u32[]{:S(2)}) copy-start(s32[4,1536]{1,0:T(4,128)} %face_source.7) | copy-start | bytes 73732
  5.1 15.4 %copy-start.16 = (bf16[768,256]{1,0:T(8,128)(2,1)}, bf16[768,256]{1,0:T(8,128)(2,1)S(1)}, u32[]{:S(2)}) copy-start(bf16[768,256]{1,0:T(8,128)(2,1)S(1)} %get-tuple-element.16.table.table_in) | copy-start | bytes 1179652
  5.1 24.2 %all-to-all-start = ((bf16[32,32,128]{2,1,0:T(8,128)(2,1)}), bf16[32,32,128]{2,1,0:T(8,128)(2,1)S(1)}, u32[]{:S(2)}, u32[]{:S(2)}) async-start(bf16[32,32,128]{2,1,0:T(8,128)(2,1)} %get-tuple-element.19), calls=%async_computation | async-start | bytes 524288 | tf_op jit(solution)/shard_map/all_to_all | solution.py:325
  16.6 4.6 %collective-permute-start = (bf16[32,128]{1,0:T(8,128)(2,1)S(1)}, bf16[32,128]{1,0:T(8,128)(2,1)S(1)}, u32[]{:S(2)}, u32[]{:S(2)}) collective-permute-start(bf16[32,128]{1,0:T(8,128)(2,1)S(1)} %get-tuple-element.20.own_minus), channel_id=1, source_target_pairs={{0,32},{32,64},{64,96},{96,128},{128,160},{160,192},{192,224},{224... | collective-permute-start | bytes 24584 | tf_op jit(solution)/shard_map/ppermute | solution.py:326
  16.7 4.6 %collective-permute-start.1 = (bf16[32,128]{1,0:T(8,128)(2,1)S(1)}, bf16[32,128]{1,0:T(8,128)(2,1)S(1)}, u32[]{:S(2)}, u32[]{:S(2)}) collective-permute-start(bf16[32,128]{1,0:T(8,128)(2,1)S(1)} %get-tuple-element.21.own_plus), channel_id=1, source_target_pairs={{0,224},{32,0},{64,32},{96,64},{128,96},{160,128},{192,160},{224,1... | collective-permute-start | bytes 24584 | tf_op jit(solution)/shard_map/ppermute | solution.py:327
  18.4 2.9 %collective-permute-start.2 = (f32[40,128]{1,0:T(8,128)S(1)}, f32[40,128]{1,0:T(8,128)S(1)}, u32[]{:S(2)}, u32[]{:S(2)}) collective-permute-start(f32[40,128]{1,0:T(8,128)S(1)} %get-tuple-element.22), channel_id=1, source_target_pairs={{0,224},{32,0},{64,32},{96,64},{128,96},{160,128},{192,160},{224,1... | collective-permute-start | bytes 61448 | tf_op jit(solution)/shard_map/ppermute | solution.py:322
  18.4 10.9 %copy-start.3 = (bf16[180,120]{1,0:T(8,128)(2,1)S(1)}, bf16[180,120]{1,0:T(8,128)(2,1)}, u32[]{:S(2)}) copy-start(bf16[180,120]{1,0:T(8,128)(2,1)} %lift_operator.3) | copy-start | bytes 129604
  18.4 10.9 %copy-start.6 = (f32[4,1536]{1,0:T(4,128)S(1)}, f32[4,1536]{1,0:T(4,128)}, u32[]{:S(2)}) copy-start(f32[4,1536]{1,0:T(4,128)} %face_area.3) | copy-start | bytes 73732
  18.4 10.9 %copy-start.10 = (f32[16,10]{1,0:T(8,128)S(1)}, f32[16,10]{1,0:T(8,128)}, u32[]{:S(2)}) copy-start(f32[16,10]{1,0:T(8,128)} %to_points.3) | copy-start | bytes 1924
  18.5 10.9 %copy-start.11 = (f32[10,16]{1,0:T(8,128)S(1)}, f32[10,16]{1,0:T(8,128)}, u32[]{:S(2)}) copy-start(f32[10,16]{1,0:T(8,128)} %to_nodes.3) | copy-start | bytes 1924
  20.5 0.7 %copy-start.18 = (f32[64,1536]{1,0:T(8,128)}, f32[64,1536]{1,0:T(8,128)S(1)}, u32[]{:S(2)}) copy-start(f32[64,1536]{1,0:T(8,128)S(1)} %get-tuple-element.18.difference) | copy-start | bytes 1179652
  29.3 1.0 %copy-start.17 = (bf16[768,256]{1,0:T(8,128)(2,1)S(1)}, bf16[768,256]{1,0:T(8,128)(2,1)}, u32[]{:S(2)}) copy-start(bf16[768,256]{1,0:T(8,128)(2,1)} %copy-done.16) | copy-start | bytes 1179652
  30.3 1.0 %copy-start.19 = (f32[64,1536]{1,0:T(8,128)S(1)}, f32[64,1536]{1,0:T(8,128)}, u32[]{:S(2)}) copy-start(f32[64,1536]{1,0:T(8,128)} %copy-done.18) | copy-start | bytes 1179652
  38.0 1.0 %copy-start.14 = (f32[180,1536]{1,0:T(8,128)}, f32[180,1536]{1,0:T(8,128)S(1)}, u32[]{:S(2)}) copy-start(f32[180,1536]{1,0:T(8,128)S(1)} %get-tuple-element.23.element_state) | copy-start | bytes 3317764
  39.0 16.5 %all-to-all-start.1 = ((bf16[32,32,128]{2,1,0:T(8,128)(2,1)}), bf16[32,32,128]{2,1,0:T(8,128)(2,1)S(1)}, u32[]{:S(2)}, u32[]{:S(2)}) async-start(bf16[32,32,128]{2,1,0:T(8,128)(2,1)} %get-tuple-element.27), calls=%async_computation.1 | async-start | bytes 524288 | tf_op jit(solution)/shard_map/all_to_all | solution.py:325
  43.3 5.0 %collective-permute-start.3 = (bf16[32,128]{1,0:T(8,128)(2,1)S(1)}, bf16[32,128]{1,0:T(8,128)(2,1)S(1)}, u32[]{:S(2)}, u32[]{:S(2)}) collective-permute-start(bf16[32,128]{1,0:T(8,128)(2,1)S(1)} %get-tuple-element.28.own_minus), channel_id=1, source_target_pairs={{0,32},{32,64},{64,96},{96,128},{128,160},{160,192},{192,224},{224... | collective-permute-start | bytes 24584 | tf_op jit(solution)/shard_map/ppermute | solution.py:326
  43.3 5.0 %collective-permute-start.4 = (bf16[32,128]{1,0:T(8,128)(2,1)S(1)}, bf16[32,128]{1,0:T(8,128)(2,1)S(1)}, u32[]{:S(2)}, u32[]{:S(2)}) collective-permute-start(bf16[32,128]{1,0:T(8,128)(2,1)S(1)} %get-tuple-element.29.own_plus), channel_id=1, source_target_pairs={{0,224},{32,0},{64,32},{96,64},{128,96},{160,128},{192,160},{224,1... | collective-permute-start | bytes 24584 | tf_op jit(solution)/shard_map/ppermute | solution.py:327
  45.0 1.3 %copy-start.15 = (f32[180,1536]{1,0:T(8,128)S(1)}, f32[180,1536]{1,0:T(8,128)}, u32[]{:S(2)}) copy-start(f32[180,1536]{1,0:T(8,128)} %copy-done.14) | copy-start | bytes 3317764

commit v4 on v3

--- a/solution.py
+++ b/solution.py
@@ -31,7 +31,6 @@
 REMOTE = PEERS * SLOTS // BLOCK
 FAULTS = 2 * SLOTS
 PARTS = 3
-EARLY = 2
 VMEM_LIMIT = 32 * 2**20
 
 
@@ -74,32 +73,22 @@
     return picked.reshape(ROWS, width)
 
 
-def pick_sent(table, send_faces, plus_faces, minus_faces, sent, sides_out, outgoing, sides, sems):
+def pick_sent(table, send_faces, plus_faces, minus_faces, sent, plus_out, minus_out, outgoing, sems):
     index = jnp.concatenate([plus_faces[...], minus_faces[...]], axis=1)
     picked = pick(table, index, 0, LOCAL).astype(BF16)
+    plus_out[...] = picked[:, :SLOTS]
+    minus_out[...] = picked[:, SLOTS:]
     copies = []
-    for i in range(2):
-        sides[i] = picked[:, i * SLOTS : (i + 1) * SLOTS]
-        copies.append(pltpu.make_async_copy(sides.at[i], sides_out[i], sems.at[PEERS // 8 + i]))
+    for turn in range(PEERS // 8):
+        start = turn * 8
+        for pair in range(start, start + 8, 2):
+            index = jnp.concatenate([send_faces[pair : pair + 1, :], send_faces[pair + 1 : pair + 2, :]], axis=1)
+            picked = pick(table, index, 0, LOCAL).astype(BF16)
+            outgoing[pair] = picked[:, :SLOTS]
+            outgoing[pair + 1] = picked[:, SLOTS:]
+        part = slice(start, start + 8)
+        copies.append(pltpu.make_async_copy(outgoing.at[part], sent.at[part], sems.at[turn]))
         copies[-1].start()
-
-    def body(turn, carry):
-        start = turn * 8
-        faces = send_faces[pl.ds(start, 8), :]
-        for pair in range(4):
-            index = jnp.concatenate([faces[2 * pair : 2 * pair + 1], faces[2 * pair + 1 : 2 * pair + 2]], axis=1)
-            picked = pick(table, index, 0, LOCAL).astype(BF16)
-            outgoing[start + 2 * pair] = picked[:, :SLOTS]
-            outgoing[start + 2 * pair + 1] = picked[:, SLOTS:]
-        part = pl.ds(start, 8)
-        pltpu.make_async_copy(outgoing.at[part], sent.at[part], sems.at[turn]).start()
-        return carry
-
-    for turn in range(PEERS // 8):
-        body(turn, 0)
-    for turn in range(PEERS // 8):
-        part = slice(turn * 8, turn * 8 + 8)
-        copies.append(pltpu.make_async_copy(outgoing.at[part], sent.at[part], sems.at[turn]))
     for copy in copies:
         copy.wait()
 
@@ -138,52 +127,61 @@
 
 def first_kernel(
     order, element_state, send_faces, plus_faces, minus_faces, stress, state_variable, fault_count, restriction,
-    sent, constants, plus_out, minus_out, table, outgoing, sides, sems,
+    sent, constants, plus_out, minus_out, table, outgoing, sems,
 ):
     make_traces(element_state[...].astype(BF16), order_rows(order[...], restriction[...]), table, 0, TILES)
     constants[0:POINTS, :] = stress[...]
     constants[POINTS : 2 * POINTS, :] = state_variable[...]
     constants[2 * POINTS :, :] = jnp.full((8, SLOTS), fault_count[0], jnp.int32).astype(F32)
-    pick_sent(table, send_faces, plus_faces, minus_faces, sent, [plus_out, minus_out], outgoing, sides, sems)
-
-
-def early_kernel(element_state, table, face_source, geometry, volume_ops, base, difference):
-    state = element_state[...]
-    packed = state.astype(BF16)
+    pick_sent(table, send_faces, plus_faces, minus_faces, sent, plus_out, minus_out, outgoing, sems)
+
+
+def early_kernel(
+    element_state, table, face_source, geometry, volume_ops, base_out, difference, state, base, sems,
+):
+    state_copy = pltpu.make_async_copy(element_state, state, sems.at[0])
+    state_copy.start()
+
+    def take(face):
+        rows = slice(face * ROWS, (face + 1) * ROWS)
+        for tile in range(TILES):
+            columns = slice(tile * BLOCK, (tile + 1) * BLOCK)
+            start = (face * TILES + tile) * ROWS
+            own = table[start : start + ROWS, :].astype(F32)
+            difference[rows, columns] = own - pick(table, face_source[face : face + 1, columns], 0, LOCAL)
+
+    take(0)
+    take(1)
+    state_copy.wait()
+    packed = state[...].astype(BF16)
     operators = volume_ops[...].astype(F32).T
     change = None
     for direction in range(3):
         operator = operators[direction * VALUES : (direction + 1) * VALUES].astype(BF16)
         term = jnp.dot(operator, packed, preferred_element_type=F32) * geometry[direction : direction + 1, :]
         change = term if change is None else change + term
-    base[...] = state + TIME_STEP * change
-
-    def body(face, carry):
-        rows = pl.ds(face * ROWS, ROWS)
-        for tile in range(TILES):
-            columns = slice(tile * BLOCK, (tile + 1) * BLOCK)
-            own = table[pl.ds((face * TILES + tile) * ROWS, ROWS), :].astype(F32)
-            difference[rows, columns] = own - pick(table, face_source[pl.ds(face, 1), columns], 0, LOCAL)
-        return carry
-
-    for face in range(EARLY):
-        body(face, 0)
+    base[...] = state[...] + TIME_STEP * change
+    base_copy = pltpu.make_async_copy(base, base_out, sems.at[1])
+    base_copy.start()
+    take(2)
+    take(3)
+    base_copy.wait()
 
 
 def step_kernel(
-    last, order, base, difference, table_in, received, partner, next_plus, next_constants, face_source, send_faces, plus_faces,
+    last, order, base_in, difference, received, partner, next_plus, next_constants, face_source, send_faces, plus_faces,
     minus_faces, own_plus, own_minus, fault_count, stress, state_variable, face_area, restriction, lift_operator,
     to_points, to_nodes, *rest,
 ):
     if last:
-        state_out, slip_out, table, jump, masked, override, scaled, state, out_sems = rest
+        state_out, slip_out, arrived, jump, masked, override, scaled, base, state, sems = rest
     else:
-        state_out, sent, plus_out, minus_out, table_out = rest[:5]
-        table, jump, masked, override, scaled, outgoing, sides, own_sems = rest[5:]
-        state = state_out
-    table[0 : LOCAL * ROWS, :] = table_in[...]
+        state_out, sent, plus_out, minus_out, table = rest[:5]
+        arrived, jump, masked, override, scaled, base, state, sems, outgoing, own_sems = rest[5:]
+    base_copy = pltpu.make_async_copy(base_in, base, sems.at[PARTS])
+    base_copy.start()
     for block in range(REMOTE):
-        table[(LOCAL + block) * ROWS : (LOCAL + block + 1) * ROWS, :] = jnp.concatenate(
+        arrived[block * ROWS : (block + 1) * ROWS, :] = jnp.concatenate(
             [received[2 * block], received[2 * block + 1]], axis=1
         )
 
@@ -212,45 +210,32 @@
     selector = jnp.where(lanes == jnp.bitwise_and(faces, BLOCK - 1), 1.0, 0.0).astype(BF16)
     override[...] = lax.dot_general(masked[...], selector, (((1,), (1,)), ((), ())), preferred_element_type=F32)
 
-    def body(early, face, carry):
-        rows = pl.ds(face * ROWS, ROWS)
+    for face in range(4):
+        rows = slice(face * ROWS, (face + 1) * ROWS)
         for tile in range(TILES):
             columns = slice(tile * BLOCK, (tile + 1) * BLOCK)
-            index = face_source[pl.ds(face, 1), columns]
-            if early:
-                plain = difference[rows, columns] - pick(table, index, LOCAL, REMOTE)
-            else:
-                own = table_in[pl.ds((face * TILES + tile) * ROWS, ROWS), :].astype(F32)
-                plain = own - pick(table, index, 0, LOCAL + REMOTE)
+            index = face_source[face : face + 1, columns] - 4 * ELEMS
+            plain = difference[rows, columns] - pick(arrived, index, 0, REMOTE)
             start = (face * TILES + tile) * 2 * ROWS
-            changed = (
-                override[pl.ds(start, ROWS), :]
-                + override[pl.ds(start + ROWS, ROWS), :]
-            )
+            changed = override[start : start + ROWS, :] + override[start + ROWS : start + 2 * ROWS, :]
             face_jump = jnp.where(changed[TRACE : TRACE + 1] > 0.5, changed, plain)
-            scaled[rows, columns] = (face_jump * face_area[pl.ds(face, 1), columns]).astype(BF16)
-        return carry
-
-    for face in range(4):
-        body(face < EARLY, face, 0)
+            scaled[rows, columns] = (face_jump * face_area[face : face + 1, columns]).astype(BF16)
 
     lift = lax.dot_general(
         lift_operator[...], order[...], (((1,), (1,)), ((), ())), preferred_element_type=F32
     ).astype(BF16)
-    if not last:
-        state[...] = base[...] - TIME_STEP * jnp.dot(lift, scaled[...], preferred_element_type=F32)
-        make_traces(state[...].astype(BF16), order_rows(order[...], restriction[...]), table, 0, TILES)
-        table_out[...] = table[0 : LOCAL * ROWS, :]
-        pick_sent(table, send_faces, plus_faces, minus_faces, sent, [plus_out, minus_out], outgoing, sides, own_sems)
-        return
+    base_copy.wait()
     width = ELEMS // PARTS
     copies = []
     for part in range(PARTS):
         columns = slice(part * width, (part + 1) * width)
         lifted = jnp.dot(lift, scaled[:, columns], preferred_element_type=F32)
         state[:, columns] = base[:, columns] - TIME_STEP * lifted
-        copies.append(pltpu.make_async_copy(state.at[:, columns], state_out.at[:, columns], out_sems.at[part]))
+        copies.append(pltpu.make_async_copy(state.at[:, columns], state_out.at[:, columns], sems.at[part]))
         copies[-1].start()
+    if not last:
+        make_traces(state[...].astype(BF16), order_rows(order[...], restriction[...]), table, 0, TILES)
+        pick_sent(table, send_faces, plus_faces, minus_faces, sent, plus_out, minus_out, outgoing, own_sems)
     for copy in copies:
         copy.wait()
 
@@ -263,14 +248,17 @@
 def call(kernel, name, args, specs, outs, out_specs, scratch, flops):
     return pl.pallas_call(
         kernel,
-        out_shape=[jax.ShapeDtypeStruct(shape, dtype) for shape, dtype in outs],
+        out_shape=[
+            pltpu.HBM(shape, dtype) if spec is HBM else jax.ShapeDtypeStruct(shape, dtype)
+            for (shape, dtype), spec in zip(outs, out_specs, strict=True)
+        ],
         in_specs=specs,
         out_specs=out_specs,
         scratch_shapes=scratch,
         compiler_params=pltpu.CompilerParams(vmem_limit_bytes=VMEM_LIMIT),
         cost_estimate=pl.CostEstimate(flops=flops, bytes_accessed=4 * 2**20, transcendentals=0),
         name=name,
-    )(*args)
+    )(*[pltpu.with_memory_space_constraint(a, pltpu.HBM) if s is HBM else a for a, s in zip(args, specs, strict=True)])
 
 
 def shards(
@@ -311,11 +299,10 @@
         ),
         [VMEM] * 7 + [SMEM, VMEM],
         [sent_shape, ((2 * POINTS + 8, SLOTS), F32), side, side, table_shape],
-        [HBM, VMEM, HBM, HBM, VMEM],
+        [HBM, VMEM, VMEM, VMEM, VMEM],
         [
             pltpu.VMEM(*sent_shape),
-            pltpu.VMEM((2, ROWS, SLOTS), BF16),
-            pltpu.SemaphoreType.DMA((PEERS // 8 + 2,)),
+            pltpu.SemaphoreType.DMA((PEERS // 8,)),
         ],
         2 * 10**9,
     )
@@ -329,38 +316,39 @@
             early_kernel,
             "early",
             (element_state, table, face_source, geometry, volume_ops),
-            [VMEM] * 5,
-            [state_shape, ((EARLY * ROWS, ELEMS), F32)],
-            [VMEM] * 2,
-            [],
+            [HBM] + [VMEM] * 4,
+            [state_shape, ((4 * ROWS, ELEMS), F32)],
+            [HBM, VMEM],
+            [pltpu.VMEM(*state_shape), pltpu.VMEM(*state_shape), pltpu.SemaphoreType.DMA((2,))],
             2 * 10**9,
         )
         args = (
-            order, base, difference, table, received, partner, next_plus, next_constants, face_source, send_faces, plus_faces,
+            order, base, difference, received, partner, next_plus, next_constants, face_source, send_faces, plus_faces,
             minus_faces, plus, minus, fault_count, normal_stress, state_variable, face_area, restriction,
             lift_operator, to_points, to_nodes,
         )
-        specs = [SMEM if arg is fault_count else VMEM for arg in args]
+        specs = [HBM if arg is base else SMEM if arg is fault_count else VMEM for arg in args]
         scratch = [
-            pltpu.VMEM(((LOCAL + REMOTE) * ROWS, BLOCK), BF16),
+            pltpu.VMEM((REMOTE * ROWS, BLOCK), BF16),
             pltpu.VMEM((ROWS, FAULTS), F32),
             pltpu.VMEM((LOCAL * 2 * ROWS, FAULTS), BF16),
             pltpu.VMEM((LOCAL * 2 * ROWS, BLOCK), F32),
             pltpu.VMEM((4 * ROWS, ELEMS), BF16),
+            pltpu.VMEM(*state_shape),
+            pltpu.VMEM(*state_shape),
+            pltpu.SemaphoreType.DMA((PARTS + 1,)),
         ]
         kernel = functools.partial(step_kernel, last)
         if last:
-            scratch += [pltpu.VMEM(*state_shape), pltpu.SemaphoreType.DMA((PARTS,))]
             outs = [state_shape, (normal_stress.shape, F32)]
             return tuple(call(kernel, "last", args, specs, outs, [HBM, VMEM], scratch, 4 * 10**9))
         scratch += [
             pltpu.VMEM(*sent_shape),
-            pltpu.VMEM((2, ROWS, SLOTS), BF16),
-            pltpu.SemaphoreType.DMA((PEERS // 8 + 2,)),
+            pltpu.SemaphoreType.DMA((PEERS // 8,)),
         ]
         outs = [state_shape, sent_shape, side, side, table_shape]
         element_state, sent, plus, minus, table = call(
-            kernel, "step", args, specs, outs, [VMEM, HBM, HBM, HBM, VMEM], scratch, 4 * 10**9
+            kernel, "step", args, specs, outs, [HBM, HBM, VMEM, VMEM, VMEM], scratch, 4 * 10**9
         )
 
 

time: 61.4 us -> 56.9 us (0.927)
  local copies, waits for them, and re-layouts: 5.5 us -> 0.52 us
  Pallas kernels: 19.2 us -> 20.6 us
  waiting for transfers between devices: 15.2 us -> 14.3 us
    unnamed x40 -> x28, local copies, waits for them, and re-layouts: 5.5 us -> 0.52 us
    pallas_call x6, Pallas kernels: 19.2 us -> 20.6 us  [call(): pl.pallas_call(kernel, out_shape=[pltpu.HBM(shape, dtype) if spec is HBM...]
    all_to_all x2, waiting for transfers between devices: 15.2 us -> 14.3 us  [shards(): received = lax.all_to_all(sent, 'dom', 0, 0, tiled=True)]
  transfers between devices with their start and end apart: 7 -> 7, of which waited for: 2 -> 2; matrix products, arithmetic and copies ran while one was open for 0% -> 0% of each run, Pallas kernels for 7% -> 12%
where the time goes in v4:
time: 56.9 us; the launch traced here: 56.5 us
  Pallas kernels  20.6 us (36%)
  starting transfers between devices  19.3 us (34%)
  waiting for transfers between devices  14.3 us (25%)
  between operations  1.78 us (3%)
    pallas_call x6, Pallas kernels, call(): pl.pallas_call(kernel, out_shape=[pltpu.HBM(shape, dtype) if spec is HBM...  20.6 us
    all_to_all x2, starting transfers between devices, shards(): received = lax.all_to_all(sent, 'dom', 0, 0, tiled=True)  15.8 us
    all_to_all x2, waiting for transfers between devices, shards(): received = lax.all_to_all(sent, 'dom', 0, 0, tiled=True)  14.3 us
    ppermute x2, starting transfers between devices, shards(): next_plus = lax.ppermute(plus, 'seg', down)  3.47 us
  transfers between devices with their start and end apart: 7, of which 2 were waited for; matrix products, arithmetic and copies ran while one was open for 0% of the time, Pallas kernels for 12%

profile of v4, /device:TPU:6, one launch (start us, length us, event | category | flops | bytes accessed | tf_op | source)
XLA Modules:
  0.0 56.5 jit_solution(4547580744448301263)
XLA Ops:
  0.6 0.0 copy-start.9
  0.6 0.0 copy-start.8
  0.7 0.0 copy-start.7
  0.7 0.0 copy-start
  0.7 0.0 copy-start.2
  0.7 0.0 copy-start.13
  0.7 0.0 copy-start.12
  1.5 0.0 copy-done.9
  1.5 0.0 copy-done.8
  1.5 0.0 copy-done.7
  1.5 0.5 copy-done
  2.0 0.0 copy-done.2
  2.0 0.0 copy-done.13
  2.0 0.0 copy-done.12
  2.0 0.0 copy-start.1
  2.0 0.0 copy-start.4
  2.0 0.0 copy-start.5
  2.0 2.9 %first.1 = (bf16[32,32,128]{2,1,0:T(8,128)(2,1)}, f32[40,128]{1,0:T(8,128)S(1)}, bf16[32,128]{1,0:T(8,128)(2,1)S(1)}, bf16[32,128]{1,0:T(8,128)(2,1)S(1)}, bf16[768,256]{1,0:T(8,128)(2,1)S(1)}) custom-call(bf16[128,120]{1,0:T(8,128)(2,1)S(1)} %order.1, f32[180,1536]{1,0:T(8,128)S(1)} %copy-done, s32[32,128]{1,0:T(8,128)S(1)} %copy-done.7, ...), custom_call_target="tpu_custom_call" | custom-call | flops 2000000000 | bytes 4194304 | tf_op jit(solution)/shard_map/first/pallas_call | solution.py:249
  4.9 11.5 %all-to-all-start = ((bf16[32,32,128]{2,1,0:T(8,128)(2,1)}), bf16[32,32,128]{2,1,0:T(8,128)(2,1)S(1)}, u32[]{:S(2)}, u32[]{:S(2)}) async-start(bf16[32,32,128]{2,1,0:T(8,128)(2,1)} %get-tuple-element.19), calls=%async_computation | async-start | bytes 524288 | tf_op jit(solution)/shard_map/all_to_all | solution.py:312
  16.4 0.0 collective-permute-start
  16.4 1.7 %collective-permute-start.1 = (bf16[32,128]{1,0:T(8,128)(2,1)S(1)}, bf16[32,128]{1,0:T(8,128)(2,1)S(1)}, u32[]{:S(2)}, u32[]{:S(2)}) collective-permute-start(bf16[32,128]{1,0:T(8,128)(2,1)S(1)} %get-tuple-element.21.own_plus), channel_id=1, source_target_pairs={{0,224},{32,0},{64,32},{96,64},{128,96},{160,128},{192,160},{224,1... | collective-permute-start | bytes 24584 | tf_op jit(solution)/shard_map/ppermute | solution.py:314
  18.2 0.0 collective-permute-start.2
  18.2 0.0 copy-done.1
  18.2 0.0 copy-done.4
  18.2 0.0 copy-done.5
  18.2 0.0 copy-start.3
  18.2 0.0 copy-start.6
  18.2 0.0 copy-start.10
  18.2 0.0 copy-start.11
  18.3 3.4 %early.2 = (f32[180,1536]{1,0:T(8,128)}, f32[128,1536]{1,0:T(8,128)S(1)}) custom-call(f32[180,1536]{1,0:T(8,128)} %element_state.3, bf16[768,256]{1,0:T(8,128)(2,1)S(1)} %get-tuple-element.16.table, s32[4,1536]{1,0:T(4,128)S(1)} %copy-done.5, f32[3,1536]{1,0:T(4,128)S(1)} %copy-done.4, bf16[180,540]{1,0:T(8,128)(2,1)S(1)} %bitcast.4), custom_call_target="tpu_custom_call" | custom-call | flops 2000000000 | bytes 4194304 | tf_op jit(solution)/shard_map/early/pallas_call | solution.py:249
  21.7 0.0 collective-permute-done.partner
  21.7 0.0 collective-permute-done.1.next_plus
  21.7 0.0 collective-permute-done.2.next_constants
  21.7 7.4 %all-to-all-done.received = bf16[32,32,128]{2,1,0:T(8,128)(2,1)S(1)} async-done(((bf16[32,32,128]{2,1,0:T(8,128)(2,1)}), bf16[32,32,128]{2,1,0:T(8,128)(2,1)S(1)}, u32[]{:S(2)}, u32[]{:S(2)}) %all-to-all-start) | async-done | bytes 262176 | tf_op jit(solution)/shard_map/all_to_all | solution.py:312
  29.1 0.0 copy-done.3
  29.1 0.0 copy-done.6
  29.1 0.0 copy-done.10
  29.1 0.0 copy-done.11
  29.1 6.6 %step.1 = (f32[180,1536]{1,0:T(8,128)}, bf16[32,32,128]{2,1,0:T(8,128)(2,1)}, bf16[32,128]{1,0:T(8,128)(2,1)S(1)}, bf16[32,128]{1,0:T(8,128)(2,1)S(1)}, bf16[768,256]{1,0:T(8,128)(2,1)S(1)}) custom-call(bf16[128,120]{1,0:T(8,128)(2,1)S(1)} %order.1, f32[180,1536]{1,0:T(8,128)} %get-tuple-element.17.base_in, f32[128,1536]{1,0:T(8,128)S(1)} %get-tuple-element.18.difference, ...), custom_call_target="tpu_custom_call" | custom-call | flops 4000000000 | bytes 4194304 | tf_op jit(solution)/shard_map/step/pallas_call | solution.py:249
  35.7 4.3 %all-to-all-start.1 = ((bf16[32,32,128]{2,1,0:T(8,128)(2,1)}), bf16[32,32,128]{2,1,0:T(8,128)(2,1)S(1)}, u32[]{:S(2)}, u32[]{:S(2)}) async-start(bf16[32,32,128]{2,1,0:T(8,128)(2,1)} %get-tuple-element.27), calls=%async_computation.1 | async-start | bytes 524288 | tf_op jit(solution)/shard_map/all_to_all | solution.py:312
  40.0 0.0 collective-permute-start.3
  40.0 1.7 %collective-permute-start.4 = (bf16[32,128]{1,0:T(8,128)(2,1)S(1)}, bf16[32,128]{1,0:T(8,128)(2,1)S(1)}, u32[]{:S(2)}, u32[]{:S(2)}) collective-permute-start(bf16[32,128]{1,0:T(8,128)(2,1)S(1)} %get-tuple-element.29.own_plus), channel_id=1, source_target_pairs={{0,224},{32,0},{64,32},{96,64},{128,96},{160,128},{192,160},{224,1... | collective-permute-start | bytes 24584 | tf_op jit(solution)/shard_map/ppermute | solution.py:314
  41.7 3.4 %early.3 = (f32[180,1536]{1,0:T(8,128)}, f32[128,1536]{1,0:T(8,128)S(1)}) custom-call(f32[180,1536]{1,0:T(8,128)} %get-tuple-element.23.element_state, bf16[768,256]{1,0:T(8,128)(2,1)S(1)} %get-tuple-element.24.table, s32[4,1536]{1,0:T(4,128)S(1)} %copy-done.5, f32[3,1536]{1,0:T(4,128)S(1)} %copy-done.4, bf16[180,540]{1,0:T(8,128)(2,1)S(1)} %bitcast.5), custom_call_target="tpu_custom_call" | custom-call | flops 2000000000 | bytes 4194304 | tf_op jit(solution)/shard_map/early/pallas_call | solution.py:249
  45.2 0.0 collective-permute-done.3.partner
  45.2 0.0 collective-permute-done.4.next_plus
  45.2 7.0 %all-to-all-done.1.received = bf16[32,32,128]{2,1,0:T(8,128)(2,1)S(1)} async-done(((bf16[32,32,128]{2,1,0:T(8,128)(2,1)}), bf16[32,32,128]{2,1,0:T(8,128)(2,1)S(1)}, u32[]{:S(2)}, u32[]{:S(2)}) %all-to-all-start.1) | async-done | bytes 262176 | tf_op jit(solution)/shard_map/all_to_all | solution.py:312
  52.2 4.2 %last.1 = (f32[180,1536]{1,0:T(8,128)}, f32[16,128]{1,0:T(8,128)}) custom-call(bf16[128,120]{1,0:T(8,128)(2,1)S(1)} %order.1, f32[180,1536]{1,0:T(8,128)} %get-tuple-element.25.base_in, f32[128,1536]{1,0:T(8,128)S(1)} %get-tuple-element.26.difference, bf16[32,32,128]{2,1,0:T(8,128)(2,1)S(1)} %all-to-all-done.1.received, ...), custom_call_target="tpu_custom_call" | custom-call | flops 4000000000 | bytes 4194304 | tf_op jit(solution)/shard_map/last/pallas_call | solution.py:249
  (1 shorter events, 0.0 us)
Async XLA Ops:
  0.6 0.8 %copy-start.9 = (f32[16,128]{1,0:T(8,128)S(1)}, f32[16,128]{1,0:T(8,128)}, u32[]{:S(2)}) copy-start(f32[16,128]{1,0:T(8,128)} %state_variable.5) | copy-start | bytes 24580
  0.6 0.8 %copy-start.8 = (f32[16,128]{1,0:T(8,128)S(1)}, f32[16,128]{1,0:T(8,128)}, u32[]{:S(2)}) copy-start(f32[16,128]{1,0:T(8,128)} %stress.5) | copy-start | bytes 24580
  0.7 0.8 %copy-start.7 = (s32[32,128]{1,0:T(8,128)S(1)}, s32[32,128]{1,0:T(8,128)}, u32[]{:S(2)}) copy-start(s32[32,128]{1,0:T(8,128)} %send_faces.5) | copy-start | bytes 49156
  0.7 1.3 %copy-start = (f32[180,1536]{1,0:T(8,128)S(1)}, f32[180,1536]{1,0:T(8,128)}, u32[]{:S(2)}) copy-start(f32[180,1536]{1,0:T(8,128)} %element_state.3) | copy-start | bytes 3317764
  0.7 1.3 %copy-start.2 = (bf16[120,180]{0,1:T(8,128)(2,1)S(1)}, bf16[120,180]{0,1:T(8,128)(2,1)}, u32[]{:S(2)}) copy-start(bf16[120,180]{0,1:T(8,128)(2,1)} %param.25) | copy-start | bytes 129604
  0.7 1.3 %copy-start.13 = (s32[128]{0:T(128)S(1)}, s32[128]{0:T(128)}, u32[]{:S(2)}) copy-start(s32[128]{0:T(128)} %param.19) | copy-start | bytes 1540
  0.7 1.3 %copy-start.12 = (s32[128]{0:T(128)S(1)}, s32[128]{0:T(128)}, u32[]{:S(2)}) copy-start(s32[128]{0:T(128)} %param.18) | copy-start | bytes 1540
  2.0 16.2 %copy-start.1 = (bf16[540,180]{0,1:T(8,128)(2,1)S(1)}, bf16[540,180]{0,1:T(8,128)(2,1)}, u32[]{:S(2)}) copy-start(bf16[540,180]{0,1:T(8,128)(2,1)} %param.26) | copy-start | bytes 583204
  2.0 16.2 %copy-start.4 = (f32[3,1536]{1,0:T(4,128)S(1)}, f32[3,1536]{1,0:T(4,128)}, u32[]{:S(2)}) copy-start(f32[3,1536]{1,0:T(4,128)} %geometry.3) | copy-start | bytes 55300
  2.0 16.2 %copy-start.5 = (s32[4,1536]{1,0:T(4,128)S(1)}, s32[4,1536]{1,0:T(4,128)}, u32[]{:S(2)}) copy-start(s32[4,1536]{1,0:T(4,128)} %face_source.7) | copy-start | bytes 73732
  4.9 24.2 %all-to-all-start = ((bf16[32,32,128]{2,1,0:T(8,128)(2,1)}), bf16[32,32,128]{2,1,0:T(8,128)(2,1)S(1)}, u32[]{:S(2)}, u32[]{:S(2)}) async-start(bf16[32,32,128]{2,1,0:T(8,128)(2,1)} %get-tuple-element.19), calls=%async_computation | async-start | bytes 524288 | tf_op jit(solution)/shard_map/all_to_all | solution.py:312
  16.4 5.3 %collective-permute-start = (bf16[32,128]{1,0:T(8,128)(2,1)S(1)}, bf16[32,128]{1,0:T(8,128)(2,1)S(1)}, u32[]{:S(2)}, u32[]{:S(2)}) collective-permute-start(bf16[32,128]{1,0:T(8,128)(2,1)S(1)} %get-tuple-element.20.own_minus), channel_id=1, source_target_pairs={{0,32},{32,64},{64,96},{96,128},{128,160},{160,192},{192,224},{224... | collective-permute-start | bytes 24584 | tf_op jit(solution)/shard_map/ppermute | solution.py:313
  16.4 5.3 %collective-permute-start.1 = (bf16[32,128]{1,0:T(8,128)(2,1)S(1)}, bf16[32,128]{1,0:T(8,128)(2,1)S(1)}, u32[]{:S(2)}, u32[]{:S(2)}) collective-permute-start(bf16[32,128]{1,0:T(8,128)(2,1)S(1)} %get-tuple-element.21.own_plus), channel_id=1, source_target_pairs={{0,224},{32,0},{64,32},{96,64},{128,96},{160,128},{192,160},{224,1... | collective-permute-start | bytes 24584 | tf_op jit(solution)/shard_map/ppermute | solution.py:314
  18.2 3.6 %collective-permute-start.2 = (f32[40,128]{1,0:T(8,128)S(1)}, f32[40,128]{1,0:T(8,128)S(1)}, u32[]{:S(2)}, u32[]{:S(2)}) collective-permute-start(f32[40,128]{1,0:T(8,128)S(1)} %get-tuple-element.22), channel_id=1, source_target_pairs={{0,224},{32,0},{64,32},{96,64},{128,96},{160,128},{192,160},{224,1... | collective-permute-start | bytes 61448 | tf_op jit(solution)/shard_map/ppermute | solution.py:309
  18.2 10.9 %copy-start.3 = (bf16[180,120]{1,0:T(8,128)(2,1)S(1)}, bf16[180,120]{1,0:T(8,128)(2,1)}, u32[]{:S(2)}) copy-start(bf16[180,120]{1,0:T(8,128)(2,1)} %lift_operator.3) | copy-start | bytes 129604
  18.2 10.9 %copy-start.6 = (f32[4,1536]{1,0:T(4,128)S(1)}, f32[4,1536]{1,0:T(4,128)}, u32[]{:S(2)}) copy-start(f32[4,1536]{1,0:T(4,128)} %face_area.3) | copy-start | bytes 73732
  18.2 10.9 %copy-start.10 = (f32[16,10]{1,0:T(8,128)S(1)}, f32[16,10]{1,0:T(8,128)}, u32[]{:S(2)}) copy-start(f32[16,10]{1,0:T(8,128)} %to_points.3) | copy-start | bytes 1924
  18.2 10.9 %copy-start.11 = (f32[10,16]{1,0:T(8,128)S(1)}, f32[10,16]{1,0:T(8,128)}, u32[]{:S(2)}) copy-start(f32[10,16]{1,0:T(8,128)} %to_nodes.3) | copy-start | bytes 1924
  35.7 16.5 %all-to-all-start.1 = ((bf16[32,32,128]{2,1,0:T(8,128)(2,1)}), bf16[32,32,128]{2,1,0:T(8,128)(2,1)S(1)}, u32[]{:S(2)}, u32[]{:S(2)}) async-start(bf16[32,32,128]{2,1,0:T(8,128)(2,1)} %get-tuple-element.27), calls=%async_computation.1 | async-start | bytes 524288 | tf_op jit(solution)/shard_map/all_to_all | solution.py:312
  40.0 5.2 %collective-permute-start.3 = (bf16[32,128]{1,0:T(8,128)(2,1)S(1)}, bf16[32,128]{1,0:T(8,128)(2,1)S(1)}, u32[]{:S(2)}, u32[]{:S(2)}) collective-permute-start(bf16[32,128]{1,0:T(8,128)(2,1)S(1)} %get-tuple-element.28.own_minus), channel_id=1, source_target_pairs={{0,32},{32,64},{64,96},{96,128},{128,160},{160,192},{192,224},{224... | collective-permute-start | bytes 24584 | tf_op jit(solution)/shard_map/ppermute | solution.py:313
  40.0 5.2 %collective-permute-start.4 = (bf16[32,128]{1,0:T(8,128)(2,1)S(1)}, bf16[32,128]{1,0:T(8,128)(2,1)S(1)}, u32[]{:S(2)}, u32[]{:S(2)}) collective-permute-start(bf16[32,128]{1,0:T(8,128)(2,1)S(1)} %get-tuple-element.29.own_plus), channel_id=1, source_target_pairs={{0,224},{32,0},{64,32},{96,64},{128,96},{160,128},{192,160},{224,1... | collective-permute-start | bytes 24584 | tf_op jit(solution)/shard_map/ppermute | solution.py:314

commit v5 on v4

--- a/solution.py
+++ b/solution.py
@@ -30,7 +30,10 @@
 LOCAL = 4 * TILES
 REMOTE = PEERS * SLOTS // BLOCK
 FAULTS = 2 * SLOTS
-PARTS = 3
+PARTS = 6
+SEND_CHUNK = 24
+REMOTE_CHUNK = 8
+LOCAL_CHUNK = 24
 VMEM_LIMIT = 32 * 2**20
 
 
@@ -58,39 +61,33 @@
     return lax.dot_general(order, restriction, (((1,), (1,)), ((), ())), preferred_element_type=F32).astype(BF16)
 
 
-def pick(table, index, first, blocks):
+def pick(table, index, first, blocks, chunk):
     width = index.shape[1]
     low = jnp.bitwise_and(index, BLOCK - 1)
     high = jnp.broadcast_to(lax.shift_right_arithmetic(index, 8), (8, width))
     lanes = lax.broadcasted_iota(jnp.int32, (BLOCK, width), 0)
     selector = jnp.where(lanes == low, 1.0, 0.0).astype(BF16)
-    product = jnp.dot(table[first * ROWS : (first + blocks) * ROWS, :], selector, preferred_element_type=F32)
-    product = product.reshape(blocks, ROWS // 8, 8, width)
     picked = jnp.zeros((ROWS // 8, 8, width), F32)
-    for block in range(blocks):
-        here = jnp.broadcast_to((high == first + block)[None], picked.shape)
-        picked = jnp.where(here, product[block], picked)
+    for part in range(0, blocks, chunk):
+        start = (first + part) * ROWS
+        product = jnp.dot(table[start : start + chunk * ROWS, :], selector, preferred_element_type=F32)
+        product = product.reshape(chunk, ROWS // 8, 8, width)
+        for block in range(chunk):
+            here = jnp.broadcast_to((high == first + part + block)[None], picked.shape)
+            picked = jnp.where(here, product[block], picked)
     return picked.reshape(ROWS, width)
 
 
-def pick_sent(table, send_faces, plus_faces, minus_faces, sent, plus_out, minus_out, outgoing, sems):
+def pick_sent(table, send_faces, plus_faces, minus_faces, sent, plus_out, minus_out):
     index = jnp.concatenate([plus_faces[...], minus_faces[...]], axis=1)
-    picked = pick(table, index, 0, LOCAL).astype(BF16)
+    picked = pick(table, index, 0, LOCAL, SEND_CHUNK).astype(BF16)
     plus_out[...] = picked[:, :SLOTS]
     minus_out[...] = picked[:, SLOTS:]
-    copies = []
-    for turn in range(PEERS // 8):
-        start = turn * 8
-        for pair in range(start, start + 8, 2):
-            index = jnp.concatenate([send_faces[pair : pair + 1, :], send_faces[pair + 1 : pair + 2, :]], axis=1)
-            picked = pick(table, index, 0, LOCAL).astype(BF16)
-            outgoing[pair] = picked[:, :SLOTS]
-            outgoing[pair + 1] = picked[:, SLOTS:]
-        part = slice(start, start + 8)
-        copies.append(pltpu.make_async_copy(outgoing.at[part], sent.at[part], sems.at[turn]))
-        copies[-1].start()
-    for copy in copies:
-        copy.wait()
+    for pair in range(0, PEERS, 2):
+        index = jnp.concatenate([send_faces[pair : pair + 1, :], send_faces[pair + 1 : pair + 2, :]], axis=1)
+        picked = pick(table, index, 0, LOCAL, SEND_CHUNK).astype(BF16)
+        sent[pair] = picked[:, :SLOTS]
+        sent[pair + 1] = picked[:, SLOTS:]
 
 
 def friction(difference, stress, state, to_points, to_nodes, jump):
@@ -127,13 +124,13 @@
 
 def first_kernel(
     order, element_state, send_faces, plus_faces, minus_faces, stress, state_variable, fault_count, restriction,
-    sent, constants, plus_out, minus_out, table, outgoing, sems,
+    sent, constants, plus_out, minus_out, table,
 ):
     make_traces(element_state[...].astype(BF16), order_rows(order[...], restriction[...]), table, 0, TILES)
     constants[0:POINTS, :] = stress[...]
     constants[POINTS : 2 * POINTS, :] = state_variable[...]
     constants[2 * POINTS :, :] = jnp.full((8, SLOTS), fault_count[0], jnp.int32).astype(F32)
-    pick_sent(table, send_faces, plus_faces, minus_faces, sent, plus_out, minus_out, outgoing, sems)
+    pick_sent(table, send_faces, plus_faces, minus_faces, sent, plus_out, minus_out)
 
 
 def early_kernel(
@@ -148,7 +145,7 @@
             columns = slice(tile * BLOCK, (tile + 1) * BLOCK)
             start = (face * TILES + tile) * ROWS
             own = table[start : start + ROWS, :].astype(F32)
-            difference[rows, columns] = own - pick(table, face_source[face : face + 1, columns], 0, LOCAL)
+            difference[rows, columns] = own - pick(table, face_source[face : face + 1, columns], 0, LOCAL, LOCAL_CHUNK)
 
     take(0)
     take(1)
@@ -168,23 +165,10 @@
     base_copy.wait()
 
 
-def step_kernel(
-    last, order, base_in, difference, received, partner, next_plus, next_constants, face_source, send_faces, plus_faces,
-    minus_faces, own_plus, own_minus, fault_count, stress, state_variable, face_area, restriction, lift_operator,
-    to_points, to_nodes, *rest,
-):
-    if last:
-        state_out, slip_out, arrived, jump, masked, override, scaled, base, state, sems = rest
-    else:
-        state_out, sent, plus_out, minus_out, table = rest[:5]
-        arrived, jump, masked, override, scaled, base, state, sems, outgoing, own_sems = rest[5:]
-    base_copy = pltpu.make_async_copy(base_in, base, sems.at[PARTS])
-    base_copy.start()
-    for block in range(REMOTE):
-        arrived[block * ROWS : (block + 1) * ROWS, :] = jnp.concatenate(
-            [received[2 * block], received[2 * block + 1]], axis=1
-        )
-
+def fault_kernel(
+    difference, partner, next_plus, next_constants, face_source, plus_faces, minus_faces, own_plus, own_minus,
+    fault_count, stress, state_variable, to_points, to_nodes, plain, index_out, slip_out, jump, masked,
+):
     plus_side = jnp.concatenate([own_plus[...].astype(F32), next_plus[...].astype(F32)], axis=1)
     minus_side = jnp.concatenate([partner[...].astype(F32), own_minus[...].astype(F32)], axis=1)
     both_stress = jnp.concatenate([stress[...], next_constants[0:POINTS, :]], axis=1)
@@ -194,8 +178,7 @@
     own_live = slot < fault_count[0]
     next_live = slot.astype(F32) < next_constants[2 * POINTS : 2 * POINTS + 1, :]
     sign = jnp.concatenate([jnp.where(own_live, 1.0, 0.0), jnp.where(next_live, -1.0, 0.0)], axis=1)
-    if last:
-        slip_out[...] = jnp.where(own_live, slip_rate[:, :SLOTS], 0.0)
+    slip_out[...] = jnp.where(own_live, slip_rate[:, :SLOTS], 0.0)
 
     row = lax.broadcasted_iota(jnp.int32, (ROWS, FAULTS), 0)
     jump[TRACE : TRACE + 2, :] = jnp.zeros((2, FAULTS), F32)
@@ -208,19 +191,40 @@
         masked[block * 2 * ROWS : (block + 1) * 2 * ROWS, :] = jnp.where(high == block, parts, 0.0).astype(BF16)
     lanes = lax.broadcasted_iota(jnp.int32, (BLOCK, FAULTS), 0)
     selector = jnp.where(lanes == jnp.bitwise_and(faces, BLOCK - 1), 1.0, 0.0).astype(BF16)
-    override[...] = lax.dot_general(masked[...], selector, (((1,), (1,)), ((), ())), preferred_element_type=F32)
-
+    changed = lax.dot_general(masked[...], selector, (((1,), (1,)), ((), ())), preferred_element_type=F32)
     for face in range(4):
         rows = slice(face * ROWS, (face + 1) * ROWS)
         for tile in range(TILES):
             columns = slice(tile * BLOCK, (tile + 1) * BLOCK)
-            index = face_source[face : face + 1, columns] - 4 * ELEMS
-            plain = difference[rows, columns] - pick(arrived, index, 0, REMOTE)
             start = (face * TILES + tile) * 2 * ROWS
-            changed = override[start : start + ROWS, :] + override[start + ROWS : start + 2 * ROWS, :]
-            face_jump = jnp.where(changed[TRACE : TRACE + 1] > 0.5, changed, plain)
+            value = changed[start : start + ROWS, :] + changed[start + ROWS : start + 2 * ROWS, :]
+            here = value[TRACE : TRACE + 1] > 0.5
+            plain[rows, columns] = jnp.where(here, value, difference[rows, columns])
+            index_out[face : face + 1, columns] = jnp.where(
+                here, -1, face_source[face : face + 1, columns] - 4 * ELEMS
+            )
+
+
+def step_kernel(
+    last, order, base_in, plain, received, index, face_area, restriction, lift_operator, send_faces, plus_faces,
+    minus_faces, *rest,
+):
+    if last:
+        state_out, arrived, scaled, base, state, sems = rest
+    else:
+        state_out, sent, plus_out, minus_out, table, arrived, scaled, base, state, sems = rest
+    base_copy = pltpu.make_async_copy(base_in, base, sems.at[PARTS])
+    base_copy.start()
+    for block in range(REMOTE):
+        arrived[block * ROWS : (block + 1) * ROWS, :] = jnp.concatenate(
+            [received[2 * block], received[2 * block + 1]], axis=1
+        )
+    for face in range(4):
+        rows = slice(face * ROWS, (face + 1) * ROWS)
+        for tile in range(TILES):
+            columns = slice(tile * BLOCK, (tile + 1) * BLOCK)
+            face_jump = plain[rows, columns] - pick(arrived, index[face : face + 1, columns], 0, REMOTE, REMOTE_CHUNK)
             scaled[rows, columns] = (face_jump * face_area[face : face + 1, columns]).astype(BF16)
-
     lift = lax.dot_general(
         lift_operator[...], order[...], (((1,), (1,)), ((), ())), preferred_element_type=F32
     ).astype(BF16)
@@ -235,7 +239,7 @@
         copies[-1].start()
     if not last:
         make_traces(state[...].astype(BF16), order_rows(order[...], restriction[...]), table, 0, TILES)
-        pick_sent(table, send_faces, plus_faces, minus_faces, sent, plus_out, minus_out, outgoing, own_sems)
+        pick_sent(table, send_faces, plus_faces, minus_faces, sent, plus_out, minus_out)
     for copy in copies:
         copy.wait()
 
@@ -299,11 +303,8 @@
         ),
         [VMEM] * 7 + [SMEM, VMEM],
         [sent_shape, ((2 * POINTS + 8, SLOTS), F32), side, side, table_shape],
-        [HBM, VMEM, VMEM, VMEM, VMEM],
-        [
-            pltpu.VMEM(*sent_shape),
-            pltpu.SemaphoreType.DMA((PEERS // 8,)),
-        ],
+        [VMEM] * 5,
+        [],
         2 * 10**9,
     )
     next_constants = lax.ppermute(constants, "seg", down)
@@ -322,17 +323,26 @@
             [pltpu.VMEM(*state_shape), pltpu.VMEM(*state_shape), pltpu.SemaphoreType.DMA((2,))],
             2 * 10**9,
         )
+        plain, index, slip = call(
+            fault_kernel,
+            "fault",
+            (
+                difference, partner, next_plus, next_constants, face_source, plus_faces, minus_faces, plus, minus,
+                fault_count, normal_stress, state_variable, to_points, to_nodes,
+            ),
+            [VMEM] * 9 + [SMEM] + [VMEM] * 4,
+            [((4 * ROWS, ELEMS), F32), (face_source.shape, jnp.int32), (normal_stress.shape, F32)],
+            [VMEM] * 3,
+            [pltpu.VMEM((ROWS, FAULTS), F32), pltpu.VMEM((LOCAL * 2 * ROWS, FAULTS), BF16)],
+            10**9,
+        )
         args = (
-            order, base, difference, received, partner, next_plus, next_constants, face_source, send_faces, plus_faces,
-            minus_faces, plus, minus, fault_count, normal_stress, state_variable, face_area, restriction,
-            lift_operator, to_points, to_nodes,
-        )
-        specs = [HBM if arg is base else SMEM if arg is fault_count else VMEM for arg in args]
+            order, base, plain, received, index, face_area, restriction, lift_operator, send_faces, plus_faces,
+            minus_faces,
+        )
+        specs = [VMEM, HBM] + [VMEM] * 9
         scratch = [
             pltpu.VMEM((REMOTE * ROWS, BLOCK), BF16),
-            pltpu.VMEM((ROWS, FAULTS), F32),
-            pltpu.VMEM((LOCAL * 2 * ROWS, FAULTS), BF16),
-            pltpu.VMEM((LOCAL * 2 * ROWS, BLOCK), F32),
             pltpu.VMEM((4 * ROWS, ELEMS), BF16),
             pltpu.VMEM(*state_shape),
             pltpu.VMEM(*state_shape),
@@ -340,15 +350,11 @@
         ]
         kernel = functools.partial(step_kernel, last)
         if last:
-            outs = [state_shape, (normal_stress.shape, F32)]
-            return tuple(call(kernel, "last", args, specs, outs, [HBM, VMEM], scratch, 4 * 10**9))
-        scratch += [
-            pltpu.VMEM(*sent_shape),
-            pltpu.SemaphoreType.DMA((PEERS // 8,)),
-        ]
+            (element_state,) = call(kernel, "last", args, specs, [state_shape], [HBM], scratch, 4 * 10**9)
+            return element_state, slip
         outs = [state_shape, sent_shape, side, side, table_shape]
         element_state, sent, plus, minus, table = call(
-            kernel, "step", args, specs, outs, [HBM, HBM, VMEM, VMEM, VMEM], scratch, 4 * 10**9
+            kernel, "step", args, specs, outs, [HBM, VMEM, VMEM, VMEM, VMEM], scratch, 4 * 10**9
         )
 
 

time: 56.9 us -> 56.5 us (level)
  the two profiles are of different devices: /device:TPU:6 before, /device:TPU:1 now
where the time goes in v5:
time: 56.5 us; the launch traced here: 56.2 us
  starting transfers between devices  23.8 us (42%)
  Pallas kernels  20.8 us (37%)
  waiting for transfers between devices  9.33 us (17%)
  between operations  1.77 us (3%)
    pallas_call x8, Pallas kernels, call(): pl.pallas_call(kernel, out_shape=[pltpu.HBM(shape, dtype) if spec is HBM...  20.8 us
    all_to_all x2, starting transfers between devices, shards(): received = lax.all_to_all(sent, 'dom', 0, 0, tiled=True)  18.9 us
    all_to_all x2, waiting for transfers between devices, shards(): received = lax.all_to_all(sent, 'dom', 0, 0, tiled=True)  9.31 us
    ppermute x2, starting transfers between devices, shards(): partner = lax.ppermute(minus, 'seg', up)  3.07 us
    ppermute x1, starting transfers between devices, shards(): next_constants = lax.ppermute(constants, 'seg', down)  1.86 us
  transfers between devices with their start and end apart: 7, of which 2 were waited for; matrix products, arithmetic and copies ran while one was open for 0% of the time, Pallas kernels for 15%

profile of v5, /device:TPU:1, one launch (start us, length us, event | category | flops | bytes accessed | tf_op | source)
XLA Modules:
  0.0 56.2 jit_solution(1345869783377470084)
XLA Ops:
  0.6 0.0 copy-start.9
  0.6 0.0 copy-start.8
  0.7 0.0 copy-start.7
  0.7 0.0 copy-start
  0.7 0.0 copy-start.2
  0.7 0.0 copy-start.13
  0.7 0.0 copy-start.12
  1.5 0.0 copy-done.9
  1.5 0.0 copy-done.8
  1.5 0.0 copy-done.7
  1.5 0.5 copy-done
  2.0 0.0 copy-done.2
  2.0 0.0 copy-done.13
  2.0 0.0 copy-done.12
  2.0 0.0 copy-start.1
  2.0 0.0 copy-start.4
  2.0 0.0 copy-start.5
  2.0 3.0 %first.1 = (bf16[32,32,128]{2,1,0:T(8,128)(2,1)}, f32[40,128]{1,0:T(8,128)S(1)}, bf16[32,128]{1,0:T(8,128)(2,1)S(1)}, bf16[32,128]{1,0:T(8,128)(2,1)S(1)}, bf16[768,256]{1,0:T(8,128)(2,1)S(1)}) custom-call(bf16[128,120]{1,0:T(8,128)(2,1)S(1)} %order.1, f32[180,1536]{1,0:T(8,128)S(1)} %copy-done, s32[32,128]{1,0:T(8,128)S(1)} %copy-done.7, ...), custom_call_target="tpu_custom_call" | custom-call | flops 2000000000 | bytes 4194304 | tf_op jit(solution)/shard_map/first/pallas_call | solution.py:253
  5.0 12.0 %all-to-all-start = ((bf16[32,32,128]{2,1,0:T(8,128)(2,1)}), bf16[32,32,128]{2,1,0:T(8,128)(2,1)S(1)}, u32[]{:S(2)}, u32[]{:S(2)}) async-start(bf16[32,32,128]{2,1,0:T(8,128)(2,1)} %get-tuple-element.28), calls=%async_computation | async-start | bytes 524288 | tf_op jit(solution)/shard_map/all_to_all | solution.py:313
  17.0 2.1 %collective-permute-start = (bf16[32,128]{1,0:T(8,128)(2,1)S(1)}, bf16[32,128]{1,0:T(8,128)(2,1)S(1)}, u32[]{:S(2)}, u32[]{:S(2)}) collective-permute-start(bf16[32,128]{1,0:T(8,128)(2,1)S(1)} %get-tuple-element.24.own_minus), channel_id=1, source_target_pairs={{0,32},{32,64},{64,96},{96,128},{128,160},{160,192},{192,224},{224... | collective-permute-start | bytes 24584 | tf_op jit(solution)/shard_map/ppermute | solution.py:314
  19.1 0.0 collective-permute-start.1
  19.1 1.9 %collective-permute-start.2 = (f32[40,128]{1,0:T(8,128)S(1)}, f32[40,128]{1,0:T(8,128)S(1)}, u32[]{:S(2)}, u32[]{:S(2)}) collective-permute-start(f32[40,128]{1,0:T(8,128)S(1)} %get-tuple-element.26), channel_id=1, source_target_pairs={{0,224},{32,0},{64,32},{96,64},{128,96},{160,128},{192,160},{224,1... | collective-permute-start | bytes 61448 | tf_op jit(solution)/shard_map/ppermute | solution.py:310
  20.9 0.0 copy-done.1
  20.9 0.0 copy-done.4
  20.9 0.0 copy-done.5
  20.9 0.0 copy-start.11
  21.0 3.5 %early.2 = (f32[180,1536]{1,0:T(8,128)}, f32[128,1536]{1,0:T(8,128)S(1)}) custom-call(f32[180,1536]{1,0:T(8,128)} %element_state.3, bf16[768,256]{1,0:T(8,128)(2,1)S(1)} %get-tuple-element.21.table, s32[4,1536]{1,0:T(4,128)S(1)} %copy-done.5, f32[3,1536]{1,0:T(4,128)S(1)} %copy-done.4, bf16[180,540]{1,0:T(8,128)(2,1)S(1)} %bitcast.4), custom_call_target="tpu_custom_call" | custom-call | flops 2000000000 | bytes 4194304 | tf_op jit(solution)/shard_map/early/pallas_call | solution.py:253
  24.4 0.0 collective-permute-done.partner
  24.4 0.0 collective-permute-done.1.next_plus
  24.4 0.0 collective-permute-done.2.next_constants
  24.4 0.0 copy-done.10
  24.5 0.0 copy-done.11
  24.5 0.0 copy-start.3
  24.5 0.0 copy-start.6
  24.5 0.8 %fault.2 = (f32[128,1536]{1,0:T(8,128)S(1)}, s32[4,1536]{1,0:T(4,128)S(1)}, f32[16,128]{1,0:T(8,128)}) custom-call(f32[128,1536]{1,0:T(8,128)S(1)} %get-tuple-element.23.difference, bf16[32,128]{1,0:T(8,128)(2,1)S(1)} %collective-permute-done.partner, bf16[32,128]{1,0:T(8,128)(2,1)S(1)} %collective-permute-done.1.next_plus, ...), custom_call_target="tpu_custom_call" | custom-call | flops 1000000000 | bytes 4194304 | tf_op jit(solution)/shard_map/fault/pallas_call | solution.py:253
  25.3 2.9 %all-to-all-done.received = bf16[32,32,128]{2,1,0:T(8,128)(2,1)S(1)} async-done(((bf16[32,32,128]{2,1,0:T(8,128)(2,1)}), bf16[32,32,128]{2,1,0:T(8,128)(2,1)S(1)}, u32[]{:S(2)}, u32[]{:S(2)}) %all-to-all-start) | async-done | bytes 262176 | tf_op jit(solution)/shard_map/all_to_all | solution.py:313
  28.2 0.0 copy-done.3
  28.2 0.0 copy-done.6
  28.2 5.0 %step.1 = (f32[180,1536]{1,0:T(8,128)}, bf16[32,32,128]{2,1,0:T(8,128)(2,1)}, bf16[32,128]{1,0:T(8,128)(2,1)S(1)}, bf16[32,128]{1,0:T(8,128)(2,1)S(1)}, bf16[768,256]{1,0:T(8,128)(2,1)S(1)}) custom-call(bf16[128,120]{1,0:T(8,128)(2,1)S(1)} %order.1, f32[180,1536]{1,0:T(8,128)} %get-tuple-element.22.base_in, f32[128,1536]{1,0:T(8,128)S(1)} %get-tuple-element.27.plain, ...), custom_call_target="tpu_custom_call" | custom-call | flops 4000000000 | bytes 4194304 | tf_op jit(solution)/shard_map/step/pallas_call | solution.py:253
  33.2 6.8 %all-to-all-start.1 = ((bf16[32,32,128]{2,1,0:T(8,128)(2,1)}), bf16[32,32,128]{2,1,0:T(8,128)(2,1)S(1)}, u32[]{:S(2)}, u32[]{:S(2)}) async-start(bf16[32,32,128]{2,1,0:T(8,128)(2,1)} %get-tuple-element.37), calls=%async_computation.1 | async-start | bytes 524288 | tf_op jit(solution)/shard_map/all_to_all | solution.py:313
  40.1 1.0 %collective-permute-start.3 = (bf16[32,128]{1,0:T(8,128)(2,1)S(1)}, bf16[32,128]{1,0:T(8,128)(2,1)S(1)}, u32[]{:S(2)}, u32[]{:S(2)}) collective-permute-start(bf16[32,128]{1,0:T(8,128)(2,1)S(1)} %get-tuple-element.34.own_minus), channel_id=1, source_target_pairs={{0,32},{32,64},{64,96},{96,128},{128,160},{160,192},{192,224},{224... | collective-permute-start | bytes 24584 | tf_op jit(solution)/shard_map/ppermute | solution.py:314
  41.1 0.0 collective-permute-start.4
  41.1 3.5 %early.3 = (f32[180,1536]{1,0:T(8,128)}, f32[128,1536]{1,0:T(8,128)S(1)}) custom-call(f32[180,1536]{1,0:T(8,128)} %get-tuple-element.30.element_state, bf16[768,256]{1,0:T(8,128)(2,1)S(1)} %get-tuple-element.31.table, s32[4,1536]{1,0:T(4,128)S(1)} %copy-done.5, f32[3,1536]{1,0:T(4,128)S(1)} %copy-done.4, bf16[180,540]{1,0:T(8,128)(2,1)S(1)} %bitcast.5), custom_call_target="tpu_custom_call" | custom-call | flops 2000000000 | bytes 4194304 | tf_op jit(solution)/shard_map/early/pallas_call | solution.py:253
  44.5 0.0 collective-permute-done.3.partner
  44.5 0.0 collective-permute-done.4.next_plus
  44.5 0.8 %fault.3 = (f32[128,1536]{1,0:T(8,128)S(1)}, s32[4,1536]{1,0:T(4,128)S(1)}, f32[16,128]{1,0:T(8,128)}) custom-call(f32[128,1536]{1,0:T(8,128)S(1)} %get-tuple-element.33.difference, bf16[32,128]{1,0:T(8,128)(2,1)S(1)} %collective-permute-done.3.partner, bf16[32,128]{1,0:T(8,128)(2,1)S(1)} %collective-permute-done.4.next_plus, ...), custom_call_target="tpu_custom_call" | custom-call | flops 1000000000 | bytes 4194304 | tf_op jit(solution)/shard_map/fault/pallas_call | solution.py:253
  45.4 6.5 %all-to-all-done.1.received = bf16[32,32,128]{2,1,0:T(8,128)(2,1)S(1)} async-done(((bf16[32,32,128]{2,1,0:T(8,128)(2,1)}), bf16[32,32,128]{2,1,0:T(8,128)(2,1)S(1)}, u32[]{:S(2)}, u32[]{:S(2)}) %all-to-all-start.1) | async-done | bytes 262176 | tf_op jit(solution)/shard_map/all_to_all | solution.py:313
  51.9 4.2 %last.1 = f32[180,1536]{1,0:T(8,128)} custom-call(bf16[128,120]{1,0:T(8,128)(2,1)S(1)} %order.1, f32[180,1536]{1,0:T(8,128)} %get-tuple-element.32.base_in, f32[128,1536]{1,0:T(8,128)S(1)} %get-tuple-element.36.plain, bf16[32,32,128]{2,1,0:T(8,128)(2,1)S(1)} %all-to-all-done.1.received, s32[4,1536]{1,0:T(4,128)S(1)} %get-tuple-element.38.index, ...), custom_call_target="tpu_custom_call" | custom-call | flops 4000000000 | bytes 4194304 | tf_op jit(solution)/shard_map/last/pallas_call | solution.py:253
  (2 shorter events, 0.0 us)
Async XLA Ops:
  0.6 0.8 %copy-start.9 = (f32[16,128]{1,0:T(8,128)S(1)}, f32[16,128]{1,0:T(8,128)}, u32[]{:S(2)}) copy-start(f32[16,128]{1,0:T(8,128)} %state_variable.5) | copy-start | bytes 24580
  0.6 0.8 %copy-start.8 = (f32[16,128]{1,0:T(8,128)S(1)}, f32[16,128]{1,0:T(8,128)}, u32[]{:S(2)}) copy-start(f32[16,128]{1,0:T(8,128)} %stress.5) | copy-start | bytes 24580
  0.7 0.8 %copy-start.7 = (s32[32,128]{1,0:T(8,128)S(1)}, s32[32,128]{1,0:T(8,128)}, u32[]{:S(2)}) copy-start(s32[32,128]{1,0:T(8,128)} %send_faces.5) | copy-start | bytes 49156
  0.7 1.3 %copy-start = (f32[180,1536]{1,0:T(8,128)S(1)}, f32[180,1536]{1,0:T(8,128)}, u32[]{:S(2)}) copy-start(f32[180,1536]{1,0:T(8,128)} %element_state.3) | copy-start | bytes 3317764
  0.7 1.3 %copy-start.2 = (bf16[120,180]{0,1:T(8,128)(2,1)S(1)}, bf16[120,180]{0,1:T(8,128)(2,1)}, u32[]{:S(2)}) copy-start(bf16[120,180]{0,1:T(8,128)(2,1)} %param.25) | copy-start | bytes 129604
  0.7 1.3 %copy-start.13 = (s32[128]{0:T(128)S(1)}, s32[128]{0:T(128)}, u32[]{:S(2)}) copy-start(s32[128]{0:T(128)} %param.19) | copy-start | bytes 1540
  0.7 1.3 %copy-start.12 = (s32[128]{0:T(128)S(1)}, s32[128]{0:T(128)}, u32[]{:S(2)}) copy-start(s32[128]{0:T(128)} %param.18) | copy-start | bytes 1540
  2.0 19.0 %copy-start.1 = (bf16[540,180]{0,1:T(8,128)(2,1)S(1)}, bf16[540,180]{0,1:T(8,128)(2,1)}, u32[]{:S(2)}) copy-start(bf16[540,180]{0,1:T(8,128)(2,1)} %param.26) | copy-start | bytes 583204
  2.0 19.0 %copy-start.4 = (f32[3,1536]{1,0:T(4,128)S(1)}, f32[3,1536]{1,0:T(4,128)}, u32[]{:S(2)}) copy-start(f32[3,1536]{1,0:T(4,128)} %geometry.3) | copy-start | bytes 55300
  2.0 19.0 %copy-start.5 = (s32[4,1536]{1,0:T(4,128)S(1)}, s32[4,1536]{1,0:T(4,128)}, u32[]{:S(2)}) copy-start(s32[4,1536]{1,0:T(4,128)} %face_source.7) | copy-start | bytes 73732
  5.0 23.2 %all-to-all-start = ((bf16[32,32,128]{2,1,0:T(8,128)(2,1)}), bf16[32,32,128]{2,1,0:T(8,128)(2,1)S(1)}, u32[]{:S(2)}, u32[]{:S(2)}) async-start(bf16[32,32,128]{2,1,0:T(8,128)(2,1)} %get-tuple-element.28), calls=%async_computation | async-start | bytes 524288 | tf_op jit(solution)/shard_map/all_to_all | solution.py:313
  17.0 7.4 %collective-permute-start = (bf16[32,128]{1,0:T(8,128)(2,1)S(1)}, bf16[32,128]{1,0:T(8,128)(2,1)S(1)}, u32[]{:S(2)}, u32[]{:S(2)}) collective-permute-start(bf16[32,128]{1,0:T(8,128)(2,1)S(1)} %get-tuple-element.24.own_minus), channel_id=1, source_target_pairs={{0,32},{32,64},{64,96},{96,128},{128,160},{160,192},{192,224},{224... | collective-permute-start | bytes 24584 | tf_op jit(solution)/shard_map/ppermute | solution.py:314
  19.1 5.4 %collective-permute-start.1 = (bf16[32,128]{1,0:T(8,128)(2,1)S(1)}, bf16[32,128]{1,0:T(8,128)(2,1)S(1)}, u32[]{:S(2)}, u32[]{:S(2)}) collective-permute-start(bf16[32,128]{1,0:T(8,128)(2,1)S(1)} %get-tuple-element.25.own_plus), channel_id=1, source_target_pairs={{0,224},{32,0},{64,32},{96,64},{128,96},{160,128},{192,160},{224,1... | collective-permute-start | bytes 24584 | tf_op jit(solution)/shard_map/ppermute | solution.py:315
  19.1 5.4 %collective-permute-start.2 = (f32[40,128]{1,0:T(8,128)S(1)}, f32[40,128]{1,0:T(8,128)S(1)}, u32[]{:S(2)}, u32[]{:S(2)}) collective-permute-start(f32[40,128]{1,0:T(8,128)S(1)} %get-tuple-element.26), channel_id=1, source_target_pairs={{0,224},{32,0},{64,32},{96,64},{128,96},{160,128},{192,160},{224,1... | collective-permute-start | bytes 61448 | tf_op jit(solution)/shard_map/ppermute | solution.py:310
  20.9 3.5 %copy-start.10 = (f32[16,10]{1,0:T(8,128)S(1)}, f32[16,10]{1,0:T(8,128)}, u32[]{:S(2)}) copy-start(f32[16,10]{1,0:T(8,128)} %to_points.3) | copy-start | bytes 1924
  20.9 3.5 %copy-start.11 = (f32[10,16]{1,0:T(8,128)S(1)}, f32[10,16]{1,0:T(8,128)}, u32[]{:S(2)}) copy-start(f32[10,16]{1,0:T(8,128)} %to_nodes.3) | copy-start | bytes 1924
  24.5 3.7 %copy-start.3 = (bf16[180,120]{1,0:T(8,128)(2,1)S(1)}, bf16[180,120]{1,0:T(8,128)(2,1)}, u32[]{:S(2)}) copy-start(bf16[180,120]{1,0:T(8,128)(2,1)} %lift_operator.3) | copy-start | bytes 129604
  24.5 3.7 %copy-start.6 = (f32[4,1536]{1,0:T(4,128)S(1)}, f32[4,1536]{1,0:T(4,128)}, u32[]{:S(2)}) copy-start(f32[4,1536]{1,0:T(4,128)} %face_area.3) | copy-start | bytes 73732
  33.2 18.6 %all-to-all-start.1 = ((bf16[32,32,128]{2,1,0:T(8,128)(2,1)}), bf16[32,32,128]{2,1,0:T(8,128)(2,1)S(1)}, u32[]{:S(2)}, u32[]{:S(2)}) async-start(bf16[32,32,128]{2,1,0:T(8,128)(2,1)} %get-tuple-element.37), calls=%async_computation.1 | async-start | bytes 524288 | tf_op jit(solution)/shard_map/all_to_all | solution.py:313
  40.1 4.5 %collective-permute-start.3 = (bf16[32,128]{1,0:T(8,128)(2,1)S(1)}, bf16[32,128]{1,0:T(8,128)(2,1)S(1)}, u32[]{:S(2)}, u32[]{:S(2)}) collective-permute-start(bf16[32,128]{1,0:T(8,128)(2,1)S(1)} %get-tuple-element.34.own_minus), channel_id=1, source_target_pairs={{0,32},{32,64},{64,96},{96,128},{128,160},{160,192},{192,224},{224... | collective-permute-start | bytes 24584 | tf_op jit(solution)/shard_map/ppermute | solution.py:314
  41.1 3.5 %collective-permute-start.4 = (bf16[32,128]{1,0:T(8,128)(2,1)S(1)}, bf16[32,128]{1,0:T(8,128)(2,1)S(1)}, u32[]{:S(2)}, u32[]{:S(2)}) collective-permute-start(bf16[32,128]{1,0:T(8,128)(2,1)S(1)} %get-tuple-element.35.own_plus), channel_id=1, source_target_pairs={{0,224},{32,0},{64,32},{96,64},{128,96},{160,128},{192,160},{224,1... | collective-permute-start | bytes 24584 | tf_op jit(solution)/shard_map/ppermute | solution.py:315

commit v6 on v5

--- a/solution.py
+++ b/solution.py
@@ -31,6 +31,8 @@
 REMOTE = PEERS * SLOTS // BLOCK
 FAULTS = 2 * SLOTS
 PARTS = 6
+WIDTH = ELEMS // PARTS
+CONSTANTS = ROWS + 2 * POINTS + 8
 SEND_CHUNK = 24
 REMOTE_CHUNK = 8
 LOCAL_CHUNK = 24
@@ -124,13 +126,14 @@
 
 def first_kernel(
     order, element_state, send_faces, plus_faces, minus_faces, stress, state_variable, fault_count, restriction,
-    sent, constants, plus_out, minus_out, table,
+    sent, own_plus, plus_out, minus_out, table,
 ):
     make_traces(element_state[...].astype(BF16), order_rows(order[...], restriction[...]), table, 0, TILES)
-    constants[0:POINTS, :] = stress[...]
-    constants[POINTS : 2 * POINTS, :] = state_variable[...]
-    constants[2 * POINTS :, :] = jnp.full((8, SLOTS), fault_count[0], jnp.int32).astype(F32)
-    pick_sent(table, send_faces, plus_faces, minus_faces, sent, plus_out, minus_out)
+    plus_out[ROWS : ROWS + POINTS, :] = stress[...]
+    plus_out[ROWS + POINTS : ROWS + 2 * POINTS, :] = state_variable[...]
+    plus_out[ROWS + 2 * POINTS :, :] = jnp.full((8, SLOTS), fault_count[0], jnp.int32).astype(F32)
+    pick_sent(table, send_faces, plus_faces, minus_faces, sent, own_plus, minus_out)
+    plus_out[0:ROWS, :] = own_plus[...].astype(F32)
 
 
 def early_kernel(
@@ -169,14 +172,14 @@
     difference, partner, next_plus, next_constants, face_source, plus_faces, minus_faces, own_plus, own_minus,
     fault_count, stress, state_variable, to_points, to_nodes, plain, index_out, slip_out, jump, masked,
 ):
-    plus_side = jnp.concatenate([own_plus[...].astype(F32), next_plus[...].astype(F32)], axis=1)
+    plus_side = jnp.concatenate([own_plus[...].astype(F32), next_plus[0:ROWS, :].astype(F32)], axis=1)
     minus_side = jnp.concatenate([partner[...].astype(F32), own_minus[...].astype(F32)], axis=1)
-    both_stress = jnp.concatenate([stress[...], next_constants[0:POINTS, :]], axis=1)
-    both_state = jnp.concatenate([state_variable[...], next_constants[POINTS : 2 * POINTS, :]], axis=1)
+    both_stress = jnp.concatenate([stress[...], next_constants[ROWS : ROWS + POINTS, :]], axis=1)
+    both_state = jnp.concatenate([state_variable[...], next_constants[ROWS + POINTS : ROWS + 2 * POINTS, :]], axis=1)
     slip_rate = friction(plus_side - minus_side, both_stress, both_state, to_points[...], to_nodes[...], jump)
     slot = lax.broadcasted_iota(jnp.int32, (1, SLOTS), 1)
     own_live = slot < fault_count[0]
-    next_live = slot.astype(F32) < next_constants[2 * POINTS : 2 * POINTS + 1, :]
+    next_live = slot.astype(F32) < next_constants[ROWS + 2 * POINTS : ROWS + 2 * POINTS + 1, :]
     sign = jnp.concatenate([jnp.where(own_live, 1.0, 0.0), jnp.where(next_live, -1.0, 0.0)], axis=1)
     slip_out[...] = jnp.where(own_live, slip_rate[:, :SLOTS], 0.0)
 
@@ -219,28 +222,32 @@
         arrived[block * ROWS : (block + 1) * ROWS, :] = jnp.concatenate(
             [received[2 * block], received[2 * block + 1]], axis=1
         )
+    lift = lax.dot_general(
+        lift_operator[...], order[...], (((1,), (1,)), ((), ())), preferred_element_type=F32
+    ).astype(BF16)
     for face in range(4):
+        if last and face == 3:
+            base_copy.wait()
         rows = slice(face * ROWS, (face + 1) * ROWS)
         for tile in range(TILES):
             columns = slice(tile * BLOCK, (tile + 1) * BLOCK)
-            face_jump = plain[rows, columns] - pick(arrived, index[face : face + 1, columns], 0, REMOTE, REMOTE_CHUNK)
+            face_jump = plain[rows, columns] - pick(
+                arrived, index[face : face + 1, columns], 0, REMOTE, REMOTE_CHUNK
+            )
             scaled[rows, columns] = (face_jump * face_area[face : face + 1, columns]).astype(BF16)
-    lift = lax.dot_general(
-        lift_operator[...], order[...], (((1,), (1,)), ((), ())), preferred_element_type=F32
-    ).astype(BF16)
-    base_copy.wait()
-    width = ELEMS // PARTS
-    copies = []
+    if not last:
+        base_copy.wait()
+    leaving = []
     for part in range(PARTS):
-        columns = slice(part * width, (part + 1) * width)
+        columns = slice(part * WIDTH, (part + 1) * WIDTH)
         lifted = jnp.dot(lift, scaled[:, columns], preferred_element_type=F32)
         state[:, columns] = base[:, columns] - TIME_STEP * lifted
-        copies.append(pltpu.make_async_copy(state.at[:, columns], state_out.at[:, columns], sems.at[part]))
-        copies[-1].start()
+        leaving.append(pltpu.make_async_copy(state.at[:, columns], state_out.at[:, columns], sems.at[part]))
+        leaving[-1].start()
     if not last:
         make_traces(state[...].astype(BF16), order_rows(order[...], restriction[...]), table, 0, TILES)
         pick_sent(table, send_faces, plus_faces, minus_faces, sent, plus_out, minus_out)
-    for copy in copies:
+    for copy in leaving:
         copy.wait()
 
 
@@ -294,7 +301,7 @@
     table_shape = ((LOCAL * ROWS, BLOCK), BF16)
     state_shape = (element_state.shape, F32)
     (order,) = call(order_kernel, "order", (), [], [((4 * ROWS, 4 * TRACE), BF16)], [VMEM], [], 4 * 10**9)
-    sent, constants, plus, minus, table = call(
+    sent, own_plus, plus, minus, table = call(
         first_kernel,
         "first",
         (
@@ -302,17 +309,18 @@
             restriction,
         ),
         [VMEM] * 7 + [SMEM, VMEM],
-        [sent_shape, ((2 * POINTS + 8, SLOTS), F32), side, side, table_shape],
+        [sent_shape, side, ((CONSTANTS, SLOTS), F32), side, table_shape],
         [VMEM] * 5,
         [],
         2 * 10**9,
     )
-    next_constants = lax.ppermute(constants, "seg", down)
+    next_constants = None
     for step in range(STEPS):
         last = step == STEPS - 1
         received = lax.all_to_all(sent, "dom", 0, 0, tiled=True)
         partner = lax.ppermute(minus, "seg", up)
         next_plus = lax.ppermute(plus, "seg", down)
+        next_constants = next_plus if next_constants is None else next_constants
         base, difference = call(
             early_kernel,
             "early",
@@ -327,7 +335,7 @@
             fault_kernel,
             "fault",
             (
-                difference, partner, next_plus, next_constants, face_source, plus_faces, minus_faces, plus, minus,
+                difference, partner, next_plus, next_constants, face_source, plus_faces, minus_faces, own_plus, minus,
                 fault_count, normal_stress, state_variable, to_points, to_nodes,
             ),
             [VMEM] * 9 + [SMEM] + [VMEM] * 4,
@@ -353,9 +361,10 @@
             (element_state,) = call(kernel, "last", args, specs, [state_shape], [HBM], scratch, 4 * 10**9)
             return element_state, slip
         outs = [state_shape, sent_shape, side, side, table_shape]
-        element_state, sent, plus, minus, table = call(
+        element_state, sent, own_plus, minus, table = call(
             kernel, "step", args, specs, outs, [HBM, VMEM, VMEM, VMEM, VMEM], scratch, 4 * 10**9
         )
+        plus = own_plus
 
 
 def solution(mesh):

time: 56.5 us -> 54.4 us (0.963)
  the two profiles are of different devices: /device:TPU:1 before, /device:TPU:6 now
where the time goes in v6:
time: 54.4 us; the launch traced here: 54.1 us
  Pallas kernels  19.9 us (37%)
  starting transfers between devices  19.3 us (35%)
  waiting for transfers between devices  12.7 us (23%)
  between operations  1.77 us (3%)
    pallas_call x8, Pallas kernels, call(): pl.pallas_call(kernel, out_shape=[pltpu.HBM(shape, dtype) if spec is HBM...  19.9 us
    all_to_all x2, starting transfers between devices, shards(): received = lax.all_to_all(sent, 'dom', 0, 0, tiled=True)  15.8 us
    all_to_all x2, waiting for transfers between devices, shards(): received = lax.all_to_all(sent, 'dom', 0, 0, tiled=True)  12.7 us
    ppermute x2, starting transfers between devices, shards(): next_plus = lax.ppermute(plus, 'seg', down)  3.47 us
  transfers between devices with their start and end apart: 6, of which 2 were waited for; matrix products, arithmetic and copies ran while one was open for 0% of the time, Pallas kernels for 16%

profile of v6, /device:TPU:6, one launch (start us, length us, event | category | flops | bytes accessed | tf_op | source)
XLA Modules:
  0.0 54.1 jit_solution(5161486705459562631)
XLA Ops:
  0.6 0.0 copy-start.9
  0.6 0.0 copy-start.8
  0.7 0.0 copy-start.7
  0.7 0.0 copy-start
  0.7 0.0 copy-start.2
  0.7 0.0 copy-start.13
  0.7 0.0 copy-start.12
  1.5 0.0 copy-done.9
  1.5 0.0 copy-done.8
  1.5 0.0 copy-done.7
  1.5 0.5 copy-done
  2.0 0.0 copy-done.2
  2.0 0.0 copy-done.13
  2.0 0.0 copy-done.12
  2.0 0.0 copy-start.1
  2.0 0.0 copy-start.4
  2.0 0.0 copy-start.5
  2.0 3.0 %first.1 = (bf16[32,32,128]{2,1,0:T(8,128)(2,1)}, bf16[32,128]{1,0:T(8,128)(2,1)S(1)}, f32[72,128]{1,0:T(8,128)S(1)}, bf16[32,128]{1,0:T(8,128)(2,1)S(1)}, bf16[768,256]{1,0:T(8,128)(2,1)S(1)}) custom-call(bf16[128,120]{1,0:T(8,128)(2,1)S(1)} %order.1, f32[180,1536]{1,0:T(8,128)S(1)} %copy-done, s32[32,128]{1,0:T(8,128)S(1)} %copy-done.7, ...), custom_call_target="tpu_custom_call" | custom-call | flops 2000000000 | bytes 4194304 | tf_op jit(solution)/shard_map/first/pallas_call | solution.py:260
  4.9 11.5 %all-to-all-start = ((bf16[32,32,128]{2,1,0:T(8,128)(2,1)}), bf16[32,32,128]{2,1,0:T(8,128)(2,1)S(1)}, u32[]{:S(2)}, u32[]{:S(2)}) async-start(bf16[32,32,128]{2,1,0:T(8,128)(2,1)} %get-tuple-element.28), calls=%async_computation | async-start | bytes 524288 | tf_op jit(solution)/shard_map/all_to_all | solution.py:320
  16.4 0.0 collective-permute-start
  16.5 1.7 %collective-permute-start.1 = (f32[72,128]{1,0:T(8,128)S(1)}, f32[72,128]{1,0:T(8,128)S(1)}, u32[]{:S(2)}, u32[]{:S(2)}) collective-permute-start(f32[72,128]{1,0:T(8,128)S(1)} %get-tuple-element.25), channel_id=1, source_target_pairs={{0,224},{32,0},{64,32},{96,64},{128,96},{160,128},{192,160},{224,1... | collective-permute-start | bytes 110600 | tf_op jit(solution)/shard_map/ppermute | solution.py:322
  18.2 0.0 copy-done.1
  18.2 0.0 copy-done.4
  18.2 0.0 copy-done.5
  18.2 0.0 copy-start.10
  18.2 0.0 copy-start.11
  18.2 3.5 %early.2 = (f32[180,1536]{1,0:T(8,128)}, f32[128,1536]{1,0:T(8,128)S(1)}) custom-call(f32[180,1536]{1,0:T(8,128)} %element_state.3, bf16[768,256]{1,0:T(8,128)(2,1)S(1)} %get-tuple-element.21.table, s32[4,1536]{1,0:T(4,128)S(1)} %copy-done.5, f32[3,1536]{1,0:T(4,128)S(1)} %copy-done.4, bf16[180,540]{1,0:T(8,128)(2,1)S(1)} %bitcast.4), custom_call_target="tpu_custom_call" | custom-call | flops 2000000000 | bytes 4194304 | tf_op jit(solution)/shard_map/early/pallas_call | solution.py:260
  21.7 0.0 collective-permute-done.partner
  21.7 0.0 collective-permute-done.1.next_plus.next_constants
  21.7 0.0 copy-done.10
  21.7 0.0 copy-done.11
  21.7 0.0 copy-start.3
  21.7 0.0 copy-start.6
  21.8 0.8 %fault.2 = (f32[128,1536]{1,0:T(8,128)S(1)}, s32[4,1536]{1,0:T(4,128)S(1)}, f32[16,128]{1,0:T(8,128)}) custom-call(f32[128,1536]{1,0:T(8,128)S(1)} %get-tuple-element.23.difference, bf16[32,128]{1,0:T(8,128)(2,1)S(1)} %collective-permute-done.partner, f32[72,128]{1,0:T(8,128)S(1)} %collective-permute-done.1.next_plus.next_constants, ...), custom_call_target="tpu_custom_call" | custom-call | flops 1000000000 | bytes 4194304 | tf_op jit(solution)/shard_map/fault/pallas_call | solution.py:260
  22.6 6.5 %all-to-all-done.received = bf16[32,32,128]{2,1,0:T(8,128)(2,1)S(1)} async-done(((bf16[32,32,128]{2,1,0:T(8,128)(2,1)}), bf16[32,32,128]{2,1,0:T(8,128)(2,1)S(1)}, u32[]{:S(2)}, u32[]{:S(2)}) %all-to-all-start) | async-done | bytes 262176 | tf_op jit(solution)/shard_map/all_to_all | solution.py:320
  29.1 0.0 copy-done.3
  29.1 0.0 copy-done.6
  29.1 5.1 %step.1 = (f32[180,1536]{1,0:T(8,128)}, bf16[32,32,128]{2,1,0:T(8,128)(2,1)}, bf16[32,128]{1,0:T(8,128)(2,1)S(1)}, bf16[32,128]{1,0:T(8,128)(2,1)S(1)}, bf16[768,256]{1,0:T(8,128)(2,1)S(1)}) custom-call(bf16[128,120]{1,0:T(8,128)(2,1)S(1)} %order.1, f32[180,1536]{1,0:T(8,128)} %get-tuple-element.22.base_in, f32[128,1536]{1,0:T(8,128)S(1)} %get-tuple-element.27.plain, ...), custom_call_target="tpu_custom_call" | custom-call | flops 4000000000 | bytes 4194304 | tf_op jit(solution)/shard_map/step/pallas_call | solution.py:260
  34.2 4.3 %all-to-all-start.1 = ((bf16[32,32,128]{2,1,0:T(8,128)(2,1)}), bf16[32,32,128]{2,1,0:T(8,128)(2,1)S(1)}, u32[]{:S(2)}, u32[]{:S(2)}) async-start(bf16[32,32,128]{2,1,0:T(8,128)(2,1)} %get-tuple-element.37), calls=%async_computation.1 | async-start | bytes 524288 | tf_op jit(solution)/shard_map/all_to_all | solution.py:320
  38.5 0.0 collective-permute-start.2
  38.5 1.7 %collective-permute-start.3 = (bf16[32,128]{1,0:T(8,128)(2,1)S(1)}, bf16[32,128]{1,0:T(8,128)(2,1)S(1)}, u32[]{:S(2)}, u32[]{:S(2)}) collective-permute-start(bf16[32,128]{1,0:T(8,128)(2,1)S(1)} %get-tuple-element.35.own_plus), channel_id=1, source_target_pairs={{0,224},{32,0},{64,32},{96,64},{128,96},{160,128},{192,160},{224,1... | collective-permute-start | bytes 24584 | tf_op jit(solution)/shard_map/ppermute | solution.py:322
  40.3 3.5 %early.3 = (f32[180,1536]{1,0:T(8,128)}, f32[128,1536]{1,0:T(8,128)S(1)}) custom-call(f32[180,1536]{1,0:T(8,128)} %get-tuple-element.30.element_state, bf16[768,256]{1,0:T(8,128)(2,1)S(1)} %get-tuple-element.31.table, s32[4,1536]{1,0:T(4,128)S(1)} %copy-done.5, f32[3,1536]{1,0:T(4,128)S(1)} %copy-done.4, bf16[180,540]{1,0:T(8,128)(2,1)S(1)} %bitcast.5), custom_call_target="tpu_custom_call" | custom-call | flops 2000000000 | bytes 4194304 | tf_op jit(solution)/shard_map/early/pallas_call | solution.py:260
  43.7 0.0 collective-permute-done.2.partner
  43.7 0.0 collective-permute-done.3.next_plus
  43.8 0.8 %fault.3 = (f32[128,1536]{1,0:T(8,128)S(1)}, s32[4,1536]{1,0:T(4,128)S(1)}, f32[16,128]{1,0:T(8,128)}) custom-call(f32[128,1536]{1,0:T(8,128)S(1)} %get-tuple-element.33.difference, bf16[32,128]{1,0:T(8,128)(2,1)S(1)} %collective-permute-done.2.partner, bf16[32,128]{1,0:T(8,128)(2,1)S(1)} %collective-permute-done.3.next_plus, ...), custom_call_target="tpu_custom_call" | custom-call | flops 1000000000 | bytes 4194304 | tf_op jit(solution)/shard_map/fault/pallas_call | solution.py:260
  44.6 6.2 %all-to-all-done.1.received = bf16[32,32,128]{2,1,0:T(8,128)(2,1)S(1)} async-done(((bf16[32,32,128]{2,1,0:T(8,128)(2,1)}), bf16[32,32,128]{2,1,0:T(8,128)(2,1)S(1)}, u32[]{:S(2)}, u32[]{:S(2)}) %all-to-all-start.1) | async-done | bytes 262176 | tf_op jit(solution)/shard_map/all_to_all | solution.py:320
  50.8 3.2 %last.1 = f32[180,1536]{1,0:T(8,128)} custom-call(bf16[128,120]{1,0:T(8,128)(2,1)S(1)} %order.1, f32[180,1536]{1,0:T(8,128)} %get-tuple-element.32.base_in, f32[128,1536]{1,0:T(8,128)S(1)} %get-tuple-element.36.plain, bf16[32,32,128]{2,1,0:T(8,128)(2,1)S(1)} %all-to-all-done.1.received, s32[4,1536]{1,0:T(4,128)S(1)} %get-tuple-element.38.index, ...), custom_call_target="tpu_custom_call" | custom-call | flops 4000000000 | bytes 4194304 | tf_op jit(solution)/shard_map/last/pallas_call | solution.py:260
  (1 shorter events, 0.0 us)
Async XLA Ops:
  0.6 0.8 %copy-start.9 = (f32[16,128]{1,0:T(8,128)S(1)}, f32[16,128]{1,0:T(8,128)}, u32[]{:S(2)}) copy-start(f32[16,128]{1,0:T(8,128)} %state_variable.5) | copy-start | bytes 24580
  0.6 0.8 %copy-start.8 = (f32[16,128]{1,0:T(8,128)S(1)}, f32[16,128]{1,0:T(8,128)}, u32[]{:S(2)}) copy-start(f32[16,128]{1,0:T(8,128)} %stress.5) | copy-start | bytes 24580
  0.7 0.8 %copy-start.7 = (s32[32,128]{1,0:T(8,128)S(1)}, s32[32,128]{1,0:T(8,128)}, u32[]{:S(2)}) copy-start(s32[32,128]{1,0:T(8,128)} %send_faces.5) | copy-start | bytes 49156
  0.7 1.3 %copy-start = (f32[180,1536]{1,0:T(8,128)S(1)}, f32[180,1536]{1,0:T(8,128)}, u32[]{:S(2)}) copy-start(f32[180,1536]{1,0:T(8,128)} %element_state.3) | copy-start | bytes 3317764
  0.7 1.3 %copy-start.2 = (bf16[120,180]{0,1:T(8,128)(2,1)S(1)}, bf16[120,180]{0,1:T(8,128)(2,1)}, u32[]{:S(2)}) copy-start(bf16[120,180]{0,1:T(8,128)(2,1)} %param.25) | copy-start | bytes 129604
  0.7 1.3 %copy-start.13 = (s32[128]{0:T(128)S(1)}, s32[128]{0:T(128)}, u32[]{:S(2)}) copy-start(s32[128]{0:T(128)} %param.19) | copy-start | bytes 1540
  0.7 1.3 %copy-start.12 = (s32[128]{0:T(128)S(1)}, s32[128]{0:T(128)}, u32[]{:S(2)}) copy-start(s32[128]{0:T(128)} %param.18) | copy-start | bytes 1540
  2.0 16.2 %copy-start.1 = (bf16[540,180]{0,1:T(8,128)(2,1)S(1)}, bf16[540,180]{0,1:T(8,128)(2,1)}, u32[]{:S(2)}) copy-start(bf16[540,180]{0,1:T(8,128)(2,1)} %param.26) | copy-start | bytes 583204
  2.0 16.2 %copy-start.4 = (f32[3,1536]{1,0:T(4,128)S(1)}, f32[3,1536]{1,0:T(4,128)}, u32[]{:S(2)}) copy-start(f32[3,1536]{1,0:T(4,128)} %geometry.3) | copy-start | bytes 55300
  2.0 16.2 %copy-start.5 = (s32[4,1536]{1,0:T(4,128)S(1)}, s32[4,1536]{1,0:T(4,128)}, u32[]{:S(2)}) copy-start(s32[4,1536]{1,0:T(4,128)} %face_source.7) | copy-start | bytes 73732
  4.9 24.2 %all-to-all-start = ((bf16[32,32,128]{2,1,0:T(8,128)(2,1)}), bf16[32,32,128]{2,1,0:T(8,128)(2,1)S(1)}, u32[]{:S(2)}, u32[]{:S(2)}) async-start(bf16[32,32,128]{2,1,0:T(8,128)(2,1)} %get-tuple-element.28), calls=%async_computation | async-start | bytes 524288 | tf_op jit(solution)/shard_map/all_to_all | solution.py:320
  16.4 5.3 %collective-permute-start = (bf16[32,128]{1,0:T(8,128)(2,1)S(1)}, bf16[32,128]{1,0:T(8,128)(2,1)S(1)}, u32[]{:S(2)}, u32[]{:S(2)}) collective-permute-start(bf16[32,128]{1,0:T(8,128)(2,1)S(1)} %get-tuple-element.24.own_minus), channel_id=1, source_target_pairs={{0,32},{32,64},{64,96},{96,128},{128,160},{160,192},{192,224},{224... | collective-permute-start | bytes 24584 | tf_op jit(solution)/shard_map/ppermute | solution.py:321
  16.5 5.2 %collective-permute-start.1 = (f32[72,128]{1,0:T(8,128)S(1)}, f32[72,128]{1,0:T(8,128)S(1)}, u32[]{:S(2)}, u32[]{:S(2)}) collective-permute-start(f32[72,128]{1,0:T(8,128)S(1)} %get-tuple-element.25), channel_id=1, source_target_pairs={{0,224},{32,0},{64,32},{96,64},{128,96},{160,128},{192,160},{224,1... | collective-permute-start | bytes 110600 | tf_op jit(solution)/shard_map/ppermute | solution.py:322
  18.2 3.5 %copy-start.10 = (f32[16,10]{1,0:T(8,128)S(1)}, f32[16,10]{1,0:T(8,128)}, u32[]{:S(2)}) copy-start(f32[16,10]{1,0:T(8,128)} %to_points.3) | copy-start | bytes 1924
  18.2 3.5 %copy-start.11 = (f32[10,16]{1,0:T(8,128)S(1)}, f32[10,16]{1,0:T(8,128)}, u32[]{:S(2)}) copy-start(f32[10,16]{1,0:T(8,128)} %to_nodes.3) | copy-start | bytes 1924
  21.7 7.4 %copy-start.3 = (bf16[180,120]{1,0:T(8,128)(2,1)S(1)}, bf16[180,120]{1,0:T(8,128)(2,1)}, u32[]{:S(2)}) copy-start(bf16[180,120]{1,0:T(8,128)(2,1)} %lift_operator.3) | copy-start | bytes 129604
  21.7 7.4 %copy-start.6 = (f32[4,1536]{1,0:T(4,128)S(1)}, f32[4,1536]{1,0:T(4,128)}, u32[]{:S(2)}) copy-start(f32[4,1536]{1,0:T(4,128)} %face_area.3) | copy-start | bytes 73732
  34.2 16.6 %all-to-all-start.1 = ((bf16[32,32,128]{2,1,0:T(8,128)(2,1)}), bf16[32,32,128]{2,1,0:T(8,128)(2,1)S(1)}, u32[]{:S(2)}, u32[]{:S(2)}) async-start(bf16[32,32,128]{2,1,0:T(8,128)(2,1)} %get-tuple-element.37), calls=%async_computation.1 | async-start | bytes 524288 | tf_op jit(solution)/shard_map/all_to_all | solution.py:320
  38.5 5.2 %collective-permute-start.2 = (bf16[32,128]{1,0:T(8,128)(2,1)S(1)}, bf16[32,128]{1,0:T(8,128)(2,1)S(1)}, u32[]{:S(2)}, u32[]{:S(2)}) collective-permute-start(bf16[32,128]{1,0:T(8,128)(2,1)S(1)} %get-tuple-element.34.own_minus), channel_id=1, source_target_pairs={{0,32},{32,64},{64,96},{96,128},{128,160},{160,192},{192,224},{224... | collective-permute-start | bytes 24584 | tf_op jit(solution)/shard_map/ppermute | solution.py:321
  38.5 5.2 %collective-permute-start.3 = (bf16[32,128]{1,0:T(8,128)(2,1)S(1)}, bf16[32,128]{1,0:T(8,128)(2,1)S(1)}, u32[]{:S(2)}, u32[]{:S(2)}) collective-permute-start(bf16[32,128]{1,0:T(8,128)(2,1)S(1)} %get-tuple-element.35.own_plus), channel_id=1, source_target_pairs={{0,224},{32,0},{64,32},{96,64},{128,96},{160,128},{192,160},{224,1... | collective-permute-start | bytes 24584 | tf_op jit(solution)/shard_map/ppermute | solution.py:322

commit v7 on v6

--- a/solution.py
+++ b/solution.py
@@ -29,8 +29,10 @@
 TILES = ELEMS // BLOCK
 LOCAL = 4 * TILES
 REMOTE = PEERS * SLOTS // BLOCK
+ROTATE = 22
 FAULTS = 2 * SLOTS
 PARTS = 6
+ORDER = [(i + ROTATE) % PEERS for i in range(PEERS)]
 WIDTH = ELEMS // PARTS
 CONSTANTS = ROWS + 2 * POINTS + 8
 SEND_CHUNK = 24
@@ -86,7 +88,7 @@
     plus_out[...] = picked[:, :SLOTS]
     minus_out[...] = picked[:, SLOTS:]
     for pair in range(0, PEERS, 2):
-        index = jnp.concatenate([send_faces[pair : pair + 1, :], send_faces[pair + 1 : pair + 2, :]], axis=1)
+        index = jnp.concatenate([send_faces[peer : peer + 1, :] for peer in ORDER[pair : pair + 2]], axis=1)
         picked = pick(table, index, 0, LOCAL, SEND_CHUNK).astype(BF16)
         sent[pair] = picked[:, :SLOTS]
         sent[pair + 1] = picked[:, SLOTS:]
@@ -220,7 +222,7 @@
     base_copy.start()
     for block in range(REMOTE):
         arrived[block * ROWS : (block + 1) * ROWS, :] = jnp.concatenate(
-            [received[2 * block], received[2 * block + 1]], axis=1
+            [received[ORDER.index(peer)] for peer in (2 * block, 2 * block + 1)], axis=1
         )
     lift = lax.dot_general(
         lift_operator[...], order[...], (((1,), (1,)), ((), ())), preferred_element_type=F32
@@ -317,7 +319,7 @@
     next_constants = None
     for step in range(STEPS):
         last = step == STEPS - 1
-        received = lax.all_to_all(sent, "dom", 0, 0, tiled=True)
+        received = lax.all_to_all(sent, "dom", 0, 0, axis_index_groups=[ORDER], tiled=True)
         partner = lax.ppermute(minus, "seg", up)
         next_plus = lax.ppermute(plus, "seg", down)
         next_constants = next_plus if next_constants is None else next_constants

time: 54.4 us -> 51 us (0.938)
  the two profiles are of different devices: /device:TPU:6 before, /device:TPU:1 now
where the time goes in v7:
time: 51 us; the launch traced here: 50.7 us
  starting transfers between devices  28.4 us (56%)
  Pallas kernels  19.9 us (39%)
  between operations  1.74 us (3%)
  local copies, waits for them, and re-layouts  0.52 us (1%)
    all_to_all x2, starting transfers between devices, shards(): lax.all_to_all(sent, 'dom', 0, 0, axis_index_groups=[ORDER], tiled=True)  22.7 us
    pallas_call x8, Pallas kernels, call(): pl.pallas_call(kernel, out_shape=[pltpu.HBM(shape, dtype) if spec is HBM...  19.9 us
    ppermute x2, starting transfers between devices, shards(): partner = lax.ppermute(minus, 'seg', up)  5.67 us
  transfers between devices with their start and end apart: 6, of which 1 were waited for; matrix products, arithmetic and copies ran while one was open for 0% of the time, Pallas kernels for 17%

profile of v7, /device:TPU:1, one launch (start us, length us, event | category | flops | bytes accessed | tf_op | source)
XLA Modules:
  0.0 50.7 jit_solution(2224437427660201492)
XLA Ops:
  0.6 0.0 copy-start.9
  0.6 0.0 copy-start.8
  0.7 0.0 copy-start.7
  0.7 0.0 copy-start
  0.7 0.0 copy-start.2
  0.7 0.0 copy-start.13
  0.7 0.0 copy-start.12
  1.5 0.0 copy-done.9
  1.5 0.0 copy-done.8
  1.5 0.0 copy-done.7
  1.5 0.5 copy-done
  2.0 0.0 copy-done.2
  2.0 0.0 copy-done.13
  2.0 0.0 copy-done.12
  2.0 0.0 copy-start.1
  2.0 0.0 copy-start.4
  2.0 0.0 copy-start.5
  2.0 3.0 %first.1 = (bf16[32,32,128]{2,1,0:T(8,128)(2,1)}, bf16[32,128]{1,0:T(8,128)(2,1)S(1)}, f32[72,128]{1,0:T(8,128)S(1)}, bf16[32,128]{1,0:T(8,128)(2,1)S(1)}, bf16[768,256]{1,0:T(8,128)(2,1)S(1)}) custom-call(bf16[128,120]{1,0:T(8,128)(2,1)S(1)} %order.1, f32[180,1536]{1,0:T(8,128)S(1)} %copy-done, s32[32,128]{1,0:T(8,128)S(1)} %copy-done.7, ...), custom_call_target="tpu_custom_call" | custom-call | flops 2000000000 | bytes 4194304 | tf_op jit(solution)/shard_map/first/pallas_call | solution.py:262
  4.9 13.5 %all-to-all-start = ((bf16[32,32,128]{2,1,0:T(8,128)(2,1)}), bf16[32,32,128]{2,1,0:T(8,128)(2,1)S(1)}, u32[]{:S(2)}, u32[]{:S(2)}) async-start(bf16[32,32,128]{2,1,0:T(8,128)(2,1)} %get-tuple-element.28), calls=%async_computation | async-start | bytes 524288 | tf_op jit(solution)/shard_map/all_to_all | solution.py:322
  18.5 2.1 %collective-permute-start = (bf16[32,128]{1,0:T(8,128)(2,1)S(1)}, bf16[32,128]{1,0:T(8,128)(2,1)S(1)}, u32[]{:S(2)}, u32[]{:S(2)}) collective-permute-start(bf16[32,128]{1,0:T(8,128)(2,1)S(1)} %get-tuple-element.24.own_minus), channel_id=1, source_target_pairs={{0,32},{32,64},{64,96},{96,128},{128,160},{160,192},{192,224},{224... | collective-permute-start | bytes 24584 | tf_op jit(solution)/shard_map/ppermute | solution.py:323
  20.6 0.0 collective-permute-start.1
  20.6 0.0 copy-done.1
  20.6 0.0 copy-done.4
  20.6 0.0 copy-done.5
  20.6 0.0 copy-start.10
  20.6 0.0 copy-start.11
  20.6 3.5 %early.2 = (f32[180,1536]{1,0:T(8,128)}, f32[128,1536]{1,0:T(8,128)S(1)}) custom-call(f32[180,1536]{1,0:T(8,128)} %element_state.3, bf16[768,256]{1,0:T(8,128)(2,1)S(1)} %get-tuple-element.21.table, s32[4,1536]{1,0:T(4,128)S(1)} %copy-done.5, f32[3,1536]{1,0:T(4,128)S(1)} %copy-done.4, bf16[180,540]{1,0:T(8,128)(2,1)S(1)} %bitcast.4), custom_call_target="tpu_custom_call" | custom-call | flops 2000000000 | bytes 4194304 | tf_op jit(solution)/shard_map/early/pallas_call | solution.py:262
  24.1 0.0 collective-permute-done.partner
  24.1 0.2 collective-permute-done.1.next_plus.next_constants
  24.2 0.0 copy-done.10
  24.2 0.0 copy-done.11
  24.2 0.0 copy-start.3
  24.3 0.0 copy-start.6
  24.3 0.8 %fault.2 = (f32[128,1536]{1,0:T(8,128)S(1)}, s32[4,1536]{1,0:T(4,128)S(1)}, f32[16,128]{1,0:T(8,128)}) custom-call(f32[128,1536]{1,0:T(8,128)S(1)} %get-tuple-element.23.difference, bf16[32,128]{1,0:T(8,128)(2,1)S(1)} %collective-permute-done.partner, f32[72,128]{1,0:T(8,128)S(1)} %collective-permute-done.1.next_plus.next_constants, ...), custom_call_target="tpu_custom_call" | custom-call | flops 1000000000 | bytes 4194304 | tf_op jit(solution)/shard_map/fault/pallas_call | solution.py:262
  25.1 0.0 all-to-all-done.received
  25.2 0.0 copy-done.3
  25.2 0.0 copy-done.6
  25.2 5.1 %step.1 = (f32[180,1536]{1,0:T(8,128)}, bf16[32,32,128]{2,1,0:T(8,128)(2,1)}, bf16[32,128]{1,0:T(8,128)(2,1)S(1)}, bf16[32,128]{1,0:T(8,128)(2,1)S(1)}, bf16[768,256]{1,0:T(8,128)(2,1)S(1)}) custom-call(bf16[128,120]{1,0:T(8,128)(2,1)S(1)} %order.1, f32[180,1536]{1,0:T(8,128)} %get-tuple-element.22.base_in, f32[128,1536]{1,0:T(8,128)S(1)} %get-tuple-element.27.plain, ...), custom_call_target="tpu_custom_call" | custom-call | flops 4000000000 | bytes 4194304 | tf_op jit(solution)/shard_map/step/pallas_call | solution.py:262
  30.2 9.2 %all-to-all-start.1 = ((bf16[32,32,128]{2,1,0:T(8,128)(2,1)}), bf16[32,32,128]{2,1,0:T(8,128)(2,1)S(1)}, u32[]{:S(2)}, u32[]{:S(2)}) async-start(bf16[32,32,128]{2,1,0:T(8,128)(2,1)} %get-tuple-element.37), calls=%async_computation.1 | async-start | bytes 524288 | tf_op jit(solution)/shard_map/all_to_all | solution.py:322
  39.4 3.6 %collective-permute-start.2 = (bf16[32,128]{1,0:T(8,128)(2,1)S(1)}, bf16[32,128]{1,0:T(8,128)(2,1)S(1)}, u32[]{:S(2)}, u32[]{:S(2)}) collective-permute-start(bf16[32,128]{1,0:T(8,128)(2,1)S(1)} %get-tuple-element.34.own_minus), channel_id=1, source_target_pairs={{0,32},{32,64},{64,96},{96,128},{128,160},{160,192},{192,224},{224... | collective-permute-start | bytes 24584 | tf_op jit(solution)/shard_map/ppermute | solution.py:323
  43.0 0.0 collective-permute-start.3
  43.0 3.5 %early.3 = (f32[180,1536]{1,0:T(8,128)}, f32[128,1536]{1,0:T(8,128)S(1)}) custom-call(f32[180,1536]{1,0:T(8,128)} %get-tuple-element.30.element_state, bf16[768,256]{1,0:T(8,128)(2,1)S(1)} %get-tuple-element.31.table, s32[4,1536]{1,0:T(4,128)S(1)} %copy-done.5, f32[3,1536]{1,0:T(4,128)S(1)} %copy-done.4, bf16[180,540]{1,0:T(8,128)(2,1)S(1)} %bitcast.5), custom_call_target="tpu_custom_call" | custom-call | flops 2000000000 | bytes 4194304 | tf_op jit(solution)/shard_map/early/pallas_call | solution.py:262
  46.5 0.0 collective-permute-done.2.partner
  46.5 0.0 collective-permute-done.3.next_plus
  46.5 0.8 %fault.3 = (f32[128,1536]{1,0:T(8,128)S(1)}, s32[4,1536]{1,0:T(4,128)S(1)}, f32[16,128]{1,0:T(8,128)}) custom-call(f32[128,1536]{1,0:T(8,128)S(1)} %get-tuple-element.33.difference, bf16[32,128]{1,0:T(8,128)(2,1)S(1)} %collective-permute-done.2.partner, bf16[32,128]{1,0:T(8,128)(2,1)S(1)} %collective-permute-done.3.next_plus, ...), custom_call_target="tpu_custom_call" | custom-call | flops 1000000000 | bytes 4194304 | tf_op jit(solution)/shard_map/fault/pallas_call | solution.py:262
  47.3 0.0 all-to-all-done.1.received
  47.3 3.2 %last.1 = f32[180,1536]{1,0:T(8,128)} custom-call(bf16[128,120]{1,0:T(8,128)(2,1)S(1)} %order.1, f32[180,1536]{1,0:T(8,128)} %get-tuple-element.32.base_in, f32[128,1536]{1,0:T(8,128)S(1)} %get-tuple-element.36.plain, bf16[32,32,128]{2,1,0:T(8,128)(2,1)S(1)} %all-to-all-done.1.received, s32[4,1536]{1,0:T(4,128)S(1)} %get-tuple-element.38.index, ...), custom_call_target="tpu_custom_call" | custom-call | flops 4000000000 | bytes 4194304 | tf_op jit(solution)/shard_map/last/pallas_call | solution.py:262
  (1 shorter events, 0.0 us)
Async XLA Ops:
  0.6 0.8 %copy-start.9 = (f32[16,128]{1,0:T(8,128)S(1)}, f32[16,128]{1,0:T(8,128)}, u32[]{:S(2)}) copy-start(f32[16,128]{1,0:T(8,128)} %state_variable.5) | copy-start | bytes 24580
  0.6 0.8 %copy-start.8 = (f32[16,128]{1,0:T(8,128)S(1)}, f32[16,128]{1,0:T(8,128)}, u32[]{:S(2)}) copy-start(f32[16,128]{1,0:T(8,128)} %stress.5) | copy-start | bytes 24580
  0.7 0.8 %copy-start.7 = (s32[32,128]{1,0:T(8,128)S(1)}, s32[32,128]{1,0:T(8,128)}, u32[]{:S(2)}) copy-start(s32[32,128]{1,0:T(8,128)} %send_faces.5) | copy-start | bytes 49156
  0.7 1.3 %copy-start = (f32[180,1536]{1,0:T(8,128)S(1)}, f32[180,1536]{1,0:T(8,128)}, u32[]{:S(2)}) copy-start(f32[180,1536]{1,0:T(8,128)} %element_state.3) | copy-start | bytes 3317764
  0.7 1.3 %copy-start.2 = (bf16[120,180]{0,1:T(8,128)(2,1)S(1)}, bf16[120,180]{0,1:T(8,128)(2,1)}, u32[]{:S(2)}) copy-start(bf16[120,180]{0,1:T(8,128)(2,1)} %param.25) | copy-start | bytes 129604
  0.7 1.3 %copy-start.13 = (s32[128]{0:T(128)S(1)}, s32[128]{0:T(128)}, u32[]{:S(2)}) copy-start(s32[128]{0:T(128)} %param.19) | copy-start | bytes 1540
  0.7 1.3 %copy-start.12 = (s32[128]{0:T(128)S(1)}, s32[128]{0:T(128)}, u32[]{:S(2)}) copy-start(s32[128]{0:T(128)} %param.18) | copy-start | bytes 1540
  2.0 18.6 %copy-start.1 = (bf16[540,180]{0,1:T(8,128)(2,1)S(1)}, bf16[540,180]{0,1:T(8,128)(2,1)}, u32[]{:S(2)}) copy-start(bf16[540,180]{0,1:T(8,128)(2,1)} %param.26) | copy-start | bytes 583204
  2.0 18.6 %copy-start.4 = (f32[3,1536]{1,0:T(4,128)S(1)}, f32[3,1536]{1,0:T(4,128)}, u32[]{:S(2)}) copy-start(f32[3,1536]{1,0:T(4,128)} %geometry.3) | copy-start | bytes 55300
  2.0 18.6 %copy-start.5 = (s32[4,1536]{1,0:T(4,128)S(1)}, s32[4,1536]{1,0:T(4,128)}, u32[]{:S(2)}) copy-start(s32[4,1536]{1,0:T(4,128)} %face_source.7) | copy-start | bytes 73732
  4.9 20.2 %all-to-all-start = ((bf16[32,32,128]{2,1,0:T(8,128)(2,1)}), bf16[32,32,128]{2,1,0:T(8,128)(2,1)S(1)}, u32[]{:S(2)}, u32[]{:S(2)}) async-start(bf16[32,32,128]{2,1,0:T(8,128)(2,1)} %get-tuple-element.28), calls=%async_computation | async-start | bytes 524288 | tf_op jit(solution)/shard_map/all_to_all | solution.py:322
  18.5 5.6 %collective-permute-start = (bf16[32,128]{1,0:T(8,128)(2,1)S(1)}, bf16[32,128]{1,0:T(8,128)(2,1)S(1)}, u32[]{:S(2)}, u32[]{:S(2)}) collective-permute-start(bf16[32,128]{1,0:T(8,128)(2,1)S(1)} %get-tuple-element.24.own_minus), channel_id=1, source_target_pairs={{0,32},{32,64},{64,96},{96,128},{128,160},{160,192},{192,224},{224... | collective-permute-start | bytes 24584 | tf_op jit(solution)/shard_map/ppermute | solution.py:323
  20.6 3.7 %collective-permute-start.1 = (f32[72,128]{1,0:T(8,128)S(1)}, f32[72,128]{1,0:T(8,128)S(1)}, u32[]{:S(2)}, u32[]{:S(2)}) collective-permute-start(f32[72,128]{1,0:T(8,128)S(1)} %get-tuple-element.25), channel_id=1, source_target_pairs={{0,224},{32,0},{64,32},{96,64},{128,96},{160,128},{192,160},{224,1... | collective-permute-start | bytes 110600 | tf_op jit(solution)/shard_map/ppermute | solution.py:324
  20.6 3.7 %copy-start.10 = (f32[16,10]{1,0:T(8,128)S(1)}, f32[16,10]{1,0:T(8,128)}, u32[]{:S(2)}) copy-start(f32[16,10]{1,0:T(8,128)} %to_points.3) | copy-start | bytes 1924
  20.6 3.7 %copy-start.11 = (f32[10,16]{1,0:T(8,128)S(1)}, f32[10,16]{1,0:T(8,128)}, u32[]{:S(2)}) copy-start(f32[10,16]{1,0:T(8,128)} %to_nodes.3) | copy-start | bytes 1924
  24.2 0.9 %copy-start.3 = (bf16[180,120]{1,0:T(8,128)(2,1)S(1)}, bf16[180,120]{1,0:T(8,128)(2,1)}, u32[]{:S(2)}) copy-start(bf16[180,120]{1,0:T(8,128)(2,1)} %lift_operator.3) | copy-start | bytes 129604
  24.3 0.9 %copy-start.6 = (f32[4,1536]{1,0:T(4,128)S(1)}, f32[4,1536]{1,0:T(4,128)}, u32[]{:S(2)}) copy-start(f32[4,1536]{1,0:T(4,128)} %face_area.3) | copy-start | bytes 73732
  30.2 17.1 %all-to-all-start.1 = ((bf16[32,32,128]{2,1,0:T(8,128)(2,1)}), bf16[32,32,128]{2,1,0:T(8,128)(2,1)S(1)}, u32[]{:S(2)}, u32[]{:S(2)}) async-start(bf16[32,32,128]{2,1,0:T(8,128)(2,1)} %get-tuple-element.37), calls=%async_computation.1 | async-start | bytes 524288 | tf_op jit(solution)/shard_map/all_to_all | solution.py:322
  39.4 7.0 %collective-permute-start.2 = (bf16[32,128]{1,0:T(8,128)(2,1)S(1)}, bf16[32,128]{1,0:T(8,128)(2,1)S(1)}, u32[]{:S(2)}, u32[]{:S(2)}) collective-permute-start(bf16[32,128]{1,0:T(8,128)(2,1)S(1)} %get-tuple-element.34.own_minus), channel_id=1, source_target_pairs={{0,32},{32,64},{64,96},{96,128},{128,160},{160,192},{192,224},{224... | collective-permute-start | bytes 24584 | tf_op jit(solution)/shard_map/ppermute | solution.py:323
  43.0 3.5 %collective-permute-start.3 = (bf16[32,128]{1,0:T(8,128)(2,1)S(1)}, bf16[32,128]{1,0:T(8,128)(2,1)S(1)}, u32[]{:S(2)}, u32[]{:S(2)}) collective-permute-start(bf16[32,128]{1,0:T(8,128)(2,1)S(1)} %get-tuple-element.35.own_plus), channel_id=1, source_target_pairs={{0,224},{32,0},{64,32},{96,64},{128,96},{160,128},{192,160},{224,1... | collective-permute-start | bytes 24584 | tf_op jit(solution)/shard_map/ppermute | solution.py:324
